TPU v7x, 128 devices: a whole 4x4x4 slice. The times are simulated.
128 devices in a mesh: src: 16 (over x, y), tgt: 8 (over z, core).
Axes of the slice: x: 4, y: 4, z: 4, core: 2. Of those that a mesh axis runs over, the one named last changes fastest.
Arguments:
- source_emb: bfloat16 [64, 1024, 768], P('src', 'tgt')
- target_emb: bfloat16 [32, 1024, 768], P('tgt', 'src')
- slot_source: int32 [16, 8, 6], P('src', 'tgt'), may hold values from 0 to 63, as said below
- slot_target: int32 [16, 8, 6], P('src', 'tgt'), may hold values from 0 to 31, as said below
Outputs:
- log_posterior: float32 [16, 8, 6, 1024, 1024], P('src', 'tgt')
- row_potential: float32 [64, 1024], P('src')
- column_potential: float32 [32, 1024], P('tgt')
Inputs may be any that keep to these rules, and one draw needn't show every extreme that they name: `slot_source`: the slots of the worker at index t of tgt name target blocks of that index, t * 4 to (t + 1) * 4 - 1. The 6 slots of one worker name source blocks of distinct indices of src (block // 4). No pair of blocks is named twice, and every source block is named by some slot. `slot_target`: every target block is named by some slot of its index of tgt.
All inputs are finite; a program needn't handle non-finite values.
Results may differ from a plain program's by a relative error of at most 0.0003.
Values may be sent and summed in bfloat16 or wider, within the bound.
No kernel may reach another device: no remote copies, remote signals or barrier semaphores. Data moves between devices by JAX's collectives and lax.ppermute only.
A program may use at most 192 MiB of HBM per device.

v0:
```python
import math

import jax
import jax.numpy as jnp
from jax import lax
from jax.sharding import PartitionSpec as P

ITERS = 3


NEG = -1e30


def combine_blocks(maxima, totals, labels, groups):
    matches = labels[:, None] == jnp.arange(groups)[None, :]
    largest = jnp.max(jnp.where(matches[:, :, None], maxima[:, None, :], NEG), axis=0)
    diffs = jnp.where(matches[:, :, None], maxima[:, None, :] - largest[None, :, :], NEG)
    scaled = jnp.where(matches[:, :, None], totals[:, None, :] * jnp.exp(diffs), 0.0)
    return (largest, jnp.sum(scaled, axis=0))


def home_plan(slot_ids, own_row, per_row):
    matched = slot_ids // per_row == own_row
    chosen = jnp.sum(jnp.where(matched, slot_ids % per_row, 0), axis=1)
    return jnp.where(jnp.any(matched, axis=1), chosen, -1)


def select_rows(table, plan):
    picked = jnp.take(table, jnp.maximum(plan, 0), axis=0)
    present = (plan >= 0).reshape((-1,) + (1,) * (table.ndim - 1))
    return jnp.where(present, picked, jnp.zeros((), table.dtype))


def on_device(source_emb, target_emb, slot_source, slot_target):
    src_blocks = source_emb.shape[0]
    tgt_blocks = target_emb.shape[0]
    features = source_emb.shape[2]
    src_count = lax.axis_size("src")
    own_row = lax.axis_index("src")
    own_col = lax.axis_index("tgt")
    tile_src = slot_source[0, 0]
    tile_tgt = slot_target[0, 0] - own_col * tgt_blocks
    tile_home = tile_src // src_blocks
    targets = lax.all_gather(target_emb, "src", axis=1, tiled=True)
    block_rows = targets.shape[1]
    tile_targets = jnp.take(targets, tile_tgt, axis=0)
    column_slots = lax.all_gather(slot_source, "src", axis=0, tiled=True).reshape(src_count, -1)
    plan_column = home_plan(column_slots, own_row, src_blocks)
    whole_blocks = lax.all_gather(source_emb, "tgt", axis=1, tiled=True)
    outgoing = select_rows(whole_blocks, plan_column)
    incoming = lax.all_to_all(outgoing, "src", split_axis=0, concat_axis=0, tiled=True)
    tile_sources = jnp.take(incoming, tile_home, axis=0)
    score_scale = 2.0 / math.sqrt(features)
    scores = (
        jnp.einsum("jid,jkd->jik", tile_sources, tile_targets, preferred_element_type=jnp.float32)
        * score_scale
    )
    column_pot = jnp.zeros((tgt_blocks, block_rows), jnp.float32)
    row_pot = jnp.zeros((src_blocks, block_rows), jnp.float32)
    tile_row = jnp.zeros((scores.shape[0], block_rows), jnp.float32)
    for iteration in range(ITERS):
        tile_col = jnp.take(column_pot, tile_tgt, axis=0)
        shifted = scores + tile_col[:, None, :]
        row_max = jnp.max(shifted, axis=2)
        row_sum = jnp.sum(jnp.exp(shifted - row_max[:, :, None]), axis=2)
        send_max, send_sum = combine_blocks(row_max, row_sum, tile_home, src_count)
        got_max, got_sum = (
            lax.all_to_all(send_max, "src", split_axis=0, concat_axis=0, tiled=True),
            lax.all_to_all(send_sum, "src", split_axis=0, concat_axis=0, tiled=True),
        )
        local_max, local_sum = combine_blocks(got_max, got_sum, plan_column, src_blocks)
        largest = lax.pmax(local_max, "tgt")
        summed = lax.psum(local_sum * jnp.exp(local_max - largest), "tgt")
        row_pot = -(largest + jnp.log(summed))
        returned = lax.all_to_all(
            select_rows(row_pot, plan_column), "src", split_axis=0, concat_axis=0, tiled=True
        )
        tile_row = jnp.take(returned, tile_home, axis=0)
        shifted = scores + tile_row[:, :, None]
        col_max = jnp.max(shifted, axis=1)
        col_sum = jnp.sum(jnp.exp(shifted - col_max[:, None, :]), axis=1)
        local_max, local_sum = combine_blocks(col_max, col_sum, tile_tgt, tgt_blocks)
        largest = lax.pmax(local_max, "src")
        summed = lax.psum(local_sum * jnp.exp(local_max - largest), "src")
        column_pot = -(largest + jnp.log(summed))
    tile_col = jnp.take(column_pot, tile_tgt, axis=0)
    log_post = scores + tile_row[:, :, None] + tile_col[:, None, :]
    return (log_post[None, None], row_pot, column_pot)


def solution(mesh):
    placed = (
        P("src", "tgt", None),
        P("tgt", "src", None),
        P("src", "tgt", None),
        P("src", "tgt", None),
    )
    return jax.shard_map(
        on_device,
        mesh=mesh,
        in_specs=placed,
        out_specs=(P("src", "tgt", None, None, None), P("src", None), P("tgt", None)),
        check_vma=False,
    )
```

profile of v0, /device:TPU:0, one launch (start us, length us, event | category | flops | bytes accessed | tf_op | source)
XLA Modules:
  0.0 1403.1 jit_solution(14254075494999021200)
XLA Ops:
  8.7 21.0 %all_gather.9 = s32[16,1,6]{2,1,0:T(1,128)S(1)} all-gather(s32[1,1,6]{2,1,0:T(1,128)} %param.12), channel_id=1, replica_groups=mesh['src'=16,'tgt'=8] {'src'}, dimensions={0}, use_global_device_ids=true | all-gather | bytes 408 | tf_op jit(solution)/shard_map/all_gather | solution.py:47
  29.9 24.2 %all-gather.3.cloned.1.call-done = bf16[4,1024,768]{2,1,0:T(8,128)(2,1)} async-done(((bf16[4,128,768]{2,1,0:T(8,128)(2,1)}), bf16[4,1024,768]{2,1,0:T(8,128)(2,1)}) %all-gather.3.cloned.1.call-update) | async-done | bytes 6291472 | tf_op jit(solution)/shard_map/all_gather | solution.py:49
  54.2 13.1 gather_fusion
  67.3 21.3 %select_select_fusion = bf16[16,1024,768]{2,1,0:T(8,128)(2,1)} fusion(bf16[16,1024,768]{2,1,0:T(8,128)(2,1)} %gather_fusion, pred[16]{0:T(512)(128)(4,1)S(1)} %broadcast_compare_fusion, pred[16]{0:T(512)(128)(4,1)S(1)} %get-tuple-element.10), kind=kLoop, calls=%fused_computation.20 | loop fusion | flops 25165824 | bytes 50331680 | tf_op jit(solution)/shard_map/jit(_where)/select_n | solution.py:31
  96.8 414.0 %all-gather.5.cloned.1.call-done = bf16[4,1024,768]{2,1,0:T(8,128)(2,1)} async-done(((bf16[4,64,768]{2,1,0:T(8,128)(2,1)}), bf16[4,1024,768]{2,1,0:T(8,128)(2,1)}) %all-gather.5.cloned.1.call-update) | async-done | bytes 6291472 | tf_op jit(solution)/shard_map/all_gather | solution.py:44
  518.8 34.8 %all-to-all-done = bf16[16,1024,768]{2,1,0:T(8,128)(2,1)} async-done(((bf16[16,1024,768]{2,1,0:T(8,128)(2,1)}), bf16[16,1024,768]{2,1,0:T(8,128)(2,1)}, u32[]{:S(2)}, u32[]{:S(2)}) %all-to-all-start) | async-done | bytes 25165856 | tf_op jit(solution)/shard_map/all_to_all | solution.py:51
  553.7 13.7 gather_fusion.1
  567.3 19.2 %add_reduce_fusion.4 = (f32[6,1024]{1,0:T(8,128)S(1)}, f32[6,1024,1024]{2,1,0:T(8,128)}) fusion(f32[6,1024]{1,0:T(8,128)S(1)} %broadcast_select_fusion.6, bf16[6,1024,768]{2,1,0:T(8,128)(2,1)} %gather_fusion.2, pred[6]{0:T(512)(128)(4,1)S(1)} %get-tuple-element.16, bf16[6,1024,768]{2,1,0:T(8,128)(2,1)} %gather_fusion.1, pred[6]{0:T(512)(128)(4,1)S(1)} %get-tuple-element.17), kind=kOutput, calls=%fused_computation.25 | convolution fusion | flops 9691981824 | bytes 44089356 | tf_op jit(solution)/shard_map/jid,jkd->jik/dot_general | solution.py:55
  586.5 10.9 exponential_reduce_fusion.5
  598.2 21.0 %all-to-all-start.1 = ((f32[16,1,1024]{2,1,0:T(1,128)}), f32[16,1,1024]{2,1,0:T(1,128)S(1)}, u32[]{:S(2)}, u32[]{:S(2)}) async-start(f32[16,1,1024]{2,1,0:T(1,128)} %copy.13), calls=%async_computation.1 | async-start | bytes 131072 | tf_op jit(solution)/shard_map/all_to_all | solution.py:68
  630.5 23.9 %pmax.42 = f32[4,1024]{1,0:T(4,128)S(1)} all-reduce(f32[4,1024]{1,0:T(4,128)S(1)} %select_reduce_fusion.11), channel_id=1, replica_groups=mesh['src'=16,'tgt'=8] {'tgt'}, use_global_device_ids=true, to_apply=%region_5.7 | all-reduce | flops 4096 | bytes 32768 | tf_op jit(solution)/shard_map/pmax | solution.py:72
  654.6 23.6 %psum.42 = f32[4,1024]{1,0:T(4,128)S(1)} all-reduce(f32[4,1024]{1,0:T(4,128)S(1)} %exponential_multiply_fusion.5), channel_id=1, replica_groups=mesh['src'=16,'tgt'=8] {'tgt'}, use_global_device_ids=true, to_apply=%region_9.11 | all-reduce | flops 4096 | bytes 32768 | tf_op jit(solution)/shard_map/psum | solution.py:73
  704.1 10.6 exponential_reduce_fusion.4
  714.8 71.2 %pmax.43 = f32[4,1024]{1,0:T(4,128)S(1)} all-reduce(f32[4,1024]{1,0:T(4,128)S(1)} %select_reduce_fusion.17), channel_id=1, replica_groups=mesh['src'=16,'tgt'=8] {'src'}, use_global_device_ids=true, to_apply=%region_12.16 | all-reduce | flops 4096 | bytes 32768 | tf_op jit(solution)/shard_map/pmax | solution.py:83
  786.2 69.6 %psum.43 = f32[4,1024]{1,0:T(4,128)S(1)} all-reduce(f32[4,1024]{1,0:T(4,128)S(1)} %exponential_multiply_fusion.4), channel_id=1, replica_groups=mesh['src'=16,'tgt'=8] {'src'}, use_global_device_ids=true, to_apply=%region_15.19 | all-reduce | flops 4096 | bytes 32768 | tf_op jit(solution)/shard_map/psum | solution.py:84
  856.4 9.4 add_reduce_fusion.2
  865.8 11.0 exponential_reduce_fusion.3
  892.3 23.9 %pmax.44 = f32[4,1024]{1,0:T(4,128)S(1)} all-reduce(f32[4,1024]{1,0:T(4,128)S(1)} %select_reduce_fusion.9), channel_id=1, replica_groups=mesh['src'=16,'tgt'=8] {'tgt'}, use_global_device_ids=true, to_apply=%region_19.23 | all-reduce | flops 4096 | bytes 32768 | tf_op jit(solution)/shard_map/pmax | solution.py:72
  916.4 23.6 %psum.44 = f32[4,1024]{1,0:T(4,128)S(1)} all-reduce(f32[4,1024]{1,0:T(4,128)S(1)} %exponential_multiply_fusion.3), channel_id=1, replica_groups=mesh['src'=16,'tgt'=8] {'tgt'}, use_global_device_ids=true, to_apply=%region_23.27 | all-reduce | flops 4096 | bytes 32768 | tf_op jit(solution)/shard_map/psum | solution.py:73
  940.7 14.4 %all_to_all.95 = f32[16,1,1024]{2,1,0:T(1,128)S(1)} all-to-all(f32[16,1,1024]{2,1,0:T(1,128)S(1)} %copy.18), channel_id=1, replica_groups=mesh['src'=16,'tgt'=8] {'src'}, dimensions={0} | all-to-all | bytes 131072 | tf_op jit(solution)/shard_map/all_to_all | solution.py:75
  965.1 10.6 exponential_reduce_fusion.2
  975.8 71.2 %pmax.45 = f32[4,1024]{1,0:T(4,128)S(1)} all-reduce(f32[4,1024]{1,0:T(4,128)S(1)} %select_reduce_fusion.15), channel_id=1, replica_groups=mesh['src'=16,'tgt'=8] {'src'}, use_global_device_ids=true, to_apply=%region_26.30 | all-reduce | flops 4096 | bytes 32768 | tf_op jit(solution)/shard_map/pmax | solution.py:83
  1047.2 69.6 %psum.45 = f32[4,1024]{1,0:T(4,128)S(1)} all-reduce(f32[4,1024]{1,0:T(4,128)S(1)} %exponential_multiply_fusion.2), channel_id=1, replica_groups=mesh['src'=16,'tgt'=8] {'src'}, use_global_device_ids=true, to_apply=%region_29.33 | all-reduce | flops 4096 | bytes 32768 | tf_op jit(solution)/shard_map/psum | solution.py:84
  1117.4 9.4 add_reduce_fusion
  1126.8 11.0 exponential_reduce_fusion.1
  1153.3 23.9 %pmax.46 = f32[4,1024]{1,0:T(4,128)S(1)} all-reduce(f32[4,1024]{1,0:T(4,128)S(1)} %select_reduce_fusion.7), channel_id=1, replica_groups=mesh['src'=16,'tgt'=8] {'tgt'}, use_global_device_ids=true, to_apply=%region_33.37 | all-reduce | flops 4096 | bytes 32768 | tf_op jit(solution)/shard_map/pmax | solution.py:72
  1177.4 23.6 %psum.46 = f32[4,1024]{1,0:T(4,128)S(1)} all-reduce(f32[4,1024]{1,0:T(4,128)S(1)} %exponential_multiply_fusion.1), channel_id=1, replica_groups=mesh['src'=16,'tgt'=8] {'tgt'}, use_global_device_ids=true, to_apply=%region_37.41 | all-reduce | flops 4096 | bytes 32768 | tf_op jit(solution)/shard_map/psum | solution.py:73
  1201.7 14.4 %all_to_all.96 = f32[16,1,1024]{2,1,0:T(1,128)S(1)} all-to-all(f32[16,1,1024]{2,1,0:T(1,128)S(1)} %copy.21), channel_id=1, replica_groups=mesh['src'=16,'tgt'=8] {'src'}, dimensions={0} | all-to-all | bytes 131072 | tf_op jit(solution)/shard_map/all_to_all | solution.py:75
  1226.1 10.6 exponential_reduce_fusion
  1236.9 71.2 %pmax.47 = f32[4,1024]{1,0:T(4,128)S(1)} all-reduce(f32[4,1024]{1,0:T(4,128)S(1)} %select_reduce_fusion.13), channel_id=1, replica_groups=mesh['src'=16,'tgt'=8] {'src'}, use_global_device_ids=true, to_apply=%region_40.44 | all-reduce | flops 4096 | bytes 32768 | tf_op jit(solution)/shard_map/pmax | solution.py:83
  1308.2 69.6 %psum.47 = f32[4,1024]{1,0:T(4,128)S(1)} all-reduce(f32[4,1024]{1,0:T(4,128)S(1)} %exponential_multiply_fusion), channel_id=1, replica_groups=mesh['src'=16,'tgt'=8] {'src'}, use_global_device_ids=true, to_apply=%region_43.47 | all-reduce | flops 4096 | bytes 32768 | tf_op jit(solution)/shard_map/psum | solution.py:84
  1378.4 17.3 %add_bitcast_fusion = f32[1,1,6,1024,1024]{4,3,2,1,0:T(8,128)} fusion(f32[6,1024,1024]{2,1,0:T(8,128)} %get-tuple-element.15, f32[6,1024]{1,0:T(8,128)S(1)} %broadcast_select_fusion, f32[6,1024]{1,0:T(8,128)S(1)} %broadcast_select_fusion.1), kind=kLoop, calls=%fused_computation.13 | loop fusion | flops 12582912 | bytes 50380800 | tf_op jit(solution)/shard_map/broadcast_in_dim | solution.py:88
  (118 shorter events, 111.0 us)
Async XLA Ops:
  8.0 46.2 %all-gather.3.cloned.1.call-start = ((), (), s32[]{:S(2)}) async-start(), calls=%async_computation.10 | async-start | bytes 7077888 | tf_op jit(solution)/shard_map/all_gather | solution.py:49
  88.6 7.3 copy-start.3
  88.6 7.9 copy-start.2
  88.6 465.1 %all-to-all-start = ((bf16[16,1024,768]{2,1,0:T(8,128)(2,1)}), bf16[16,1024,768]{2,1,0:T(8,128)(2,1)}, u32[]{:S(2)}, u32[]{:S(2)}) async-start(bf16[16,1024,768]{2,1,0:T(8,128)(2,1)} %select_select_fusion), calls=%async_computation | async-start | bytes 50331648 | tf_op jit(solution)/shard_map/all_to_all | solution.py:51
  95.2 415.5 %all-gather.5.cloned.1.call-start = ((), (), s32[]{:S(2)}) async-start(), calls=%async_computation.11 | async-start | bytes 6684672 | tf_op jit(solution)/shard_map/all_gather | solution.py:44
  598.2 28.6 %all-to-all-start.1 = ((f32[16,1,1024]{2,1,0:T(1,128)}), f32[16,1,1024]{2,1,0:T(1,128)S(1)}, u32[]{:S(2)}, u32[]{:S(2)}) async-start(f32[16,1,1024]{2,1,0:T(1,128)} %copy.13), calls=%async_computation.1 | async-start | bytes 131072 | tf_op jit(solution)/shard_map/all_to_all | solution.py:68
  626.9 27.5 %all-to-all-start.2 = ((f32[16,1,1024]{2,1,0:T(1,128)}), f32[16,1,1024]{2,1,0:T(1,128)S(1)}, u32[]{:S(2)}, u32[]{:S(2)}) async-start(f32[16,1,1024]{2,1,0:T(1,128)} %copy.14), calls=%async_computation.2 | async-start | bytes 131072 | tf_op jit(solution)/shard_map/all_to_all | solution.py:69
  679.5 14.5 %all-to-all-start.3 = ((f32[16,1,1024]{2,1,0:T(1,128)}), f32[16,1,1024]{2,1,0:T(1,128)S(1)}, u32[]{:S(2)}, u32[]{:S(2)}) async-start(f32[16,1,1024]{2,1,0:T(1,128)} %copy.15), calls=%async_computation.3 | async-start | bytes 131072 | tf_op jit(solution)/shard_map/all_to_all | solution.py:75
  877.6 11.1 all-to-all-start.4
  888.7 27.5 %all-to-all-start.5 = ((f32[16,1,1024]{2,1,0:T(1,128)}), f32[16,1,1024]{2,1,0:T(1,128)S(1)}, u32[]{:S(2)}, u32[]{:S(2)}) async-start(f32[16,1,1024]{2,1,0:T(1,128)} %copy.17), calls=%async_computation.5 | async-start | bytes 131072 | tf_op jit(solution)/shard_map/all_to_all | solution.py:69
  1138.6 11.1 all-to-all-start.7
  1149.7 27.5 %all-to-all-start.8 = ((f32[16,1,1024]{2,1,0:T(1,128)}), f32[16,1,1024]{2,1,0:T(1,128)S(1)}, u32[]{:S(2)}, u32[]{:S(2)}) async-start(f32[16,1,1024]{2,1,0:T(1,128)} %copy.20), calls=%async_computation.8 | async-start | bytes 131072 | tf_op jit(solution)/shard_map/all_to_all | solution.py:69
  1201.0 35.8 %copy-start = (f32[4,1024]{1,0:T(4,128)}, f32[4,1024]{1,0:T(4,128)S(1)}, u32[]{:S(2)}) copy-start(f32[4,1024]{1,0:T(4,128)S(1)} %add_negate_fusion.1) | copy-start | bytes 49156
  1377.8 17.9 %copy-start.1 = (f32[4,1024]{1,0:T(4,128)}, f32[4,1024]{1,0:T(4,128)S(1)}, u32[]{:S(2)}) copy-start(f32[4,1024]{1,0:T(4,128)S(1)} %add_negate_fusion) | copy-start | bytes 49156
Sparse Core Ops, SparseCore 0:
  10.5 43.5 all-gather.2
Sparse Core Ops, SparseCore 1:
  97.9 412.8 all-gather.4
where the time goes:
time: 1410 us; the launch traced here: 1400 us
  blocking collectives  614 us (44%)
  waiting for transfers between devices  502 us (36%)
  other arithmetic  154 us (11%)
  starting transfers between devices  52 us (4%)
  local copies, waits for them, and re-layouts  45.7 us (3%)
  matrix products  19.2 us (1%)
  between operations  16 us (1%)
    all_gather x1, waiting for transfers between devices, on_device(): targets = lax.all_gather(target_emb, 'src', axis=1, tiled=True)  414 us
    pmax x3, blocking collectives, on_device(): largest = lax.pmax(local_max, 'src')  214 us
    psum x3, blocking collectives, on_device(): summed = lax.psum(local_sum * jnp.exp(local_max - largest), 'src')  209 us
    pmax x3, blocking collectives, on_device(): largest = lax.pmax(local_max, 'tgt')  71.5 us
    psum x3, blocking collectives, on_device(): summed = lax.psum(local_sum * jnp.exp(local_max - largest), 'tgt')  70.7 us
    all_to_all x1, waiting for transfers between devices, on_device(): lax.all_to_all(outgoing, 'src', split_axis=0, concat_axis=0, tiled=True)  34.8 us
    reduce_sum x3, other arithmetic, on_device(): row_sum = jnp.sum(jnp.exp(shifted - row_max[:, :, None]), axis=2)  32.9 us
    reduce_sum x3, other arithmetic, on_device(): col_sum = jnp.sum(jnp.exp(shifted - col_max[:, None, :]), axis=1)  31.9 us
  transfers between devices with their start and end apart: 10, of which 7 were waited for; matrix products, arithmetic and copies ran while one was open for 1% of the time, Pallas kernels for 0%

commit v1 on v0

--- a/solution.py
+++ b/solution.py
@@ -1,14 +1,19 @@
+import functools
 import math
 
 import jax
 import jax.numpy as jnp
 from jax import lax
+from jax.experimental import pallas as pl
+from jax.experimental.pallas import tpu as pltpu
 from jax.sharding import PartitionSpec as P
 
 ITERS = 3
-
-
 NEG = -1e30
+F32, BF16 = jnp.float32, jnp.bfloat16
+LIMIT = 20.0
+ROWS = 512
+NT = (((1,), (1,)), ((), ()))
 
 
 def combine_blocks(maxima, totals, labels, groups):
@@ -31,34 +36,18 @@
     return jnp.where(present, picked, jnp.zeros((), table.dtype))
 
 
-def on_device(source_emb, target_emb, slot_source, slot_target):
-    src_blocks = source_emb.shape[0]
-    tgt_blocks = target_emb.shape[0]
-    features = source_emb.shape[2]
+def log_domain(pieces, targets, tile_home, tile_tgt, plan_column, src_blocks):
+    tgt_blocks, block_rows, features = targets.shape
     src_count = lax.axis_size("src")
-    own_row = lax.axis_index("src")
-    own_col = lax.axis_index("tgt")
-    tile_src = slot_source[0, 0]
-    tile_tgt = slot_target[0, 0] - own_col * tgt_blocks
-    tile_home = tile_src // src_blocks
-    targets = lax.all_gather(target_emb, "src", axis=1, tiled=True)
-    block_rows = targets.shape[1]
+    tile_sources = pieces.transpose(1, 0, 2, 3).reshape(pieces.shape[1], block_rows, features)
     tile_targets = jnp.take(targets, tile_tgt, axis=0)
-    column_slots = lax.all_gather(slot_source, "src", axis=0, tiled=True).reshape(src_count, -1)
-    plan_column = home_plan(column_slots, own_row, src_blocks)
-    whole_blocks = lax.all_gather(source_emb, "tgt", axis=1, tiled=True)
-    outgoing = select_rows(whole_blocks, plan_column)
-    incoming = lax.all_to_all(outgoing, "src", split_axis=0, concat_axis=0, tiled=True)
-    tile_sources = jnp.take(incoming, tile_home, axis=0)
-    score_scale = 2.0 / math.sqrt(features)
-    scores = (
-        jnp.einsum("jid,jkd->jik", tile_sources, tile_targets, preferred_element_type=jnp.float32)
-        * score_scale
+    scores = jnp.einsum("jid,jkd->jik", tile_sources, tile_targets, preferred_element_type=F32) * (
+        2.0 / math.sqrt(features)
     )
-    column_pot = jnp.zeros((tgt_blocks, block_rows), jnp.float32)
-    row_pot = jnp.zeros((src_blocks, block_rows), jnp.float32)
-    tile_row = jnp.zeros((scores.shape[0], block_rows), jnp.float32)
-    for iteration in range(ITERS):
+    column_pot = jnp.zeros((tgt_blocks, block_rows), F32)
+
+    def iterate(_, carry):
+        column_pot, _, _ = carry
         tile_col = jnp.take(column_pot, tile_tgt, axis=0)
         shifted = scores + tile_col[:, None, :]
         row_max = jnp.max(shifted, axis=2)
@@ -82,10 +71,243 @@
         local_max, local_sum = combine_blocks(col_max, col_sum, tile_tgt, tgt_blocks)
         largest = lax.pmax(local_max, "src")
         summed = lax.psum(local_sum * jnp.exp(local_max - largest), "src")
-        column_pot = -(largest + jnp.log(summed))
+        return (-(largest + jnp.log(summed)), row_pot, tile_row)
+
+    init = (column_pot, jnp.zeros((src_blocks, block_rows), F32), jnp.zeros((scores.shape[0], block_rows), F32))
+    column_pot, row_pot, tile_row = lax.fori_loop(0, ITERS, iterate, init)
     tile_col = jnp.take(column_pot, tile_tgt, axis=0)
     log_post = scores + tile_row[:, :, None] + tile_col[:, None, :]
     return (log_post[None, None], row_pot, column_pot)
+
+
+def stack3(x):
+    hi = x.astype(BF16).astype(F32)
+    mid = (x - hi).astype(BF16).astype(F32)
+    low = x - hi - mid
+    row = lax.broadcasted_iota(jnp.int32, (16, x.shape[1]), 0)
+    parts = [jnp.broadcast_to(p, row.shape) for p in (hi, mid, low)]
+    return jnp.where(row == 0, parts[0], jnp.where(row == 1, parts[1], jnp.where(row == 2, parts[2], 0.0))).astype(BF16)
+
+
+def lane_totals(lanes):
+    ones = jnp.ones((8, 128), F32)
+    return lax.dot_general(ones, lanes, NT, preferred_element_type=F32, precision=lax.Precision.HIGHEST)[0:1]
+
+
+def scores_kernel(scale, named, x_ref, y_ref, k_ref, sum_ref, work, lane_sum, lowest):
+    blocks, width, _ = y_ref.shape
+    per = width // ROWS
+    count = blocks * per * blocks
+
+    def product(n, slot):
+        work[slot] = lax.dot_general(
+            x_ref[n // blocks], y_ref[lax.rem(n, blocks)], NT, preferred_element_type=F32
+        )
+
+    def weigh(n, slot):
+        i, c = n // blocks, lax.rem(n, blocks)
+        e = jnp.exp2(work[slot] * scale)
+        k = e.astype(BF16)
+        rows = pl.ds(pl.multiple_of(i * ROWS, ROWS), ROWS)
+        k_ref[rows, pl.ds(pl.multiple_of(c * width, width), width)] = k
+        acc, low = e[:, :128], k[:, :128]
+        for g in range(1, width // 128):
+            acc = acc + e[:, g * 128 : (g + 1) * 128]
+            low = jnp.minimum(low, k[:, g * 128 : (g + 1) * 128])
+        here = jnp.where(named[i // per, c] > 0, acc, 0.0)
+        lane_sum[i] = jnp.where(c == 0, here, lane_sum[i] + here)
+        lowest[...] = jnp.minimum(lowest[...], jnp.min(low.reshape(ROWS // 16, 16, 128), axis=0))
+
+    lowest[...] = jnp.ones_like(lowest)
+    lane_sum[...] = jnp.zeros_like(lane_sum)
+    product(0, 0)
+
+    def step(m, carry):
+        product(m * 2 + 1, 1)
+        weigh(m * 2, 0)
+        product(jnp.minimum(m * 2 + 2, count - 1), 0)
+        weigh(m * 2 + 1, 1)
+        return carry
+
+    lax.fori_loop(0, count // 2, step, 0)
+    low = jnp.min(lowest[...].astype(F32))
+    totals = [lane_totals(lane_sum[i]) for i in range(blocks * per)]
+    high = functools.reduce(jnp.maximum, [jnp.max(t) for t in totals])
+    fine = (low > math.exp(-LIMIT)) & (high < math.exp(LIMIT))
+    for i, total in enumerate(totals):
+        total = jnp.where(fine, total, jnp.nan)
+        cols = slice((i % per) * ROWS, (i % per + 1) * ROWS)
+        sum_ref[:, i // per, :, cols] = jnp.broadcast_to(total[None], (sum_ref.shape[0], 1, ROWS))
+
+
+def score_weights(x, y, named, copies):
+    blocks, width, depth = y.shape
+    n = blocks * width
+    whole = pl.BlockSpec(memory_space=pltpu.VMEM)
+    return pl.pallas_call(
+        functools.partial(scores_kernel, 2.0 / math.sqrt(depth) * math.log2(math.e)),
+        in_specs=[pl.BlockSpec(memory_space=pltpu.SMEM), whole, whole],
+        out_specs=[whole, whole],
+        scratch_shapes=[
+            pltpu.VMEM((2, ROWS, width), F32),
+            pltpu.VMEM((n // ROWS, ROWS, 128), F32),
+            pltpu.VMEM((16, 128), BF16),
+        ],
+        out_shape=[pltpu.VMEM((n, n), BF16), jax.ShapeDtypeStruct((copies, blocks, 1, width), F32)],
+        compiler_params=pltpu.CompilerParams(vmem_limit_bytes=26 << 20),
+        name="score_weights",
+    )(named, x.reshape(n // ROWS, ROWS, depth), y)
+
+
+def put(o_ref, block, start, out):
+    o_ref[:, block, :, start : start + out.shape[1]] = jnp.broadcast_to(out[None], (o_ref.shape[0],) + out.shape)
+
+
+def column_kernel(named, g_ref, k_in, o_ref, k_ref):
+    total = jnp.sum(g_ref[...], axis=0)
+    blocks, _, width = total.shape
+    fine = (jnp.min(total) > 0.0) & (jnp.max(total) < 1e38)
+    spoil = jnp.where(fine, 0.0, jnp.nan)
+    lhs = [stack3(1.0 / total[b]) for b in range(blocks)]
+    for c in range(blocks):
+        live = [jnp.where(named[b, c] > 0, lhs[b], jnp.zeros_like(lhs[b])) for b in range(blocks)]
+        for start in range(0, width, ROWS):
+            cols = slice(c * width + start, c * width + start + ROWS)
+            acc = jnp.zeros((16, ROWS), F32)
+            for b in range(blocks):
+                acc = acc + jnp.dot(live[b], k_ref[b * width : (b + 1) * width, cols], preferred_element_type=F32)
+            put(o_ref, c, start, acc[0:1] + acc[1:2] + acc[2:3] + spoil)
+
+
+def row_kernel(named, g_ref, k_in, o_ref, k_ref):
+    total = jnp.sum(g_ref[...], axis=0)
+    blocks, _, width = total.shape
+    fine = (jnp.min(total) >= math.exp(-LIMIT)) & (jnp.max(total) <= math.exp(LIMIT))
+    spoil = jnp.where(fine, 0.0, jnp.nan)
+    inv = 1.0 / total
+    half = blocks // 2
+    lhs = [stack3(inv[c]) for c in range(half)]
+    for b in range(blocks):
+        live = [jnp.where(named[b, c] > 0, lhs[c], jnp.zeros_like(lhs[c])) for c in range(half)]
+        flat = [jnp.where(named[b, c] > 0, inv[c], jnp.zeros_like(inv[c])) for c in range(half, blocks)]
+        for start in range(0, width, ROWS):
+            rows = slice(b * width + start, b * width + start + ROWS)
+            acc = jnp.zeros((16, ROWS), F32)
+            for c in range(half):
+                acc = acc + lax.dot_general(
+                    live[c], k_ref[rows, c * width : (c + 1) * width], NT, preferred_element_type=F32
+                )
+            lanes = jnp.zeros((ROWS, 128), F32)
+            for c in range(half, blocks):
+                for g in range(0, width, 128):
+                    part = k_ref[rows, c * width + g : c * width + g + 128].astype(F32)
+                    lanes = lanes + part * flat[c - half][:, g : g + 128]
+            put(o_ref, b, start, acc[0:1] + acc[1:2] + acc[2:3] + lane_totals(lanes) + spoil)
+
+
+def weighted_sums(kernel, name, named, gathered, k, copies):
+    whole = pl.BlockSpec(memory_space=pltpu.VMEM)
+    return pl.pallas_call(
+        kernel,
+        in_specs=[pl.BlockSpec(memory_space=pltpu.SMEM), whole, whole],
+        out_specs=[whole, whole],
+        out_shape=[jax.ShapeDtypeStruct((copies,) + gathered.shape[1:], F32), pltpu.VMEM(k.shape, k.dtype)],
+        input_output_aliases={2: 1},
+        compiler_params=pltpu.CompilerParams(vmem_limit_bytes=12 << 20),
+        name=name,
+    )(named, gathered, pltpu.with_memory_space_constraint(k, pltpu.VMEM))
+
+
+def posterior_kernel(scale, tile_tgt, x_ref, y_ref, r_ref, c_ref, o_ref):
+    width, depth = y_ref.shape[1:]
+    row = jnp.broadcast_to(r_ref[0], (128, width)).T
+    x = x_ref[...].reshape(width, depth)
+    for start in range(0, width, 256):
+        cols = slice(start, start + 256)
+        s = lax.dot_general(x, y_ref[0, cols], NT, preferred_element_type=F32) * scale
+        for g in range(0, 256, 128):
+            out = s[:, g : g + 128] + row + c_ref[0, :, start + g : start + g + 128]
+            o_ref[0, 0, 0, :, start + g : start + g + 128] = out
+
+
+def posterior(pieces, targets, tile_row, column_pot, tile_tgt):
+    parts, tiles, piece, depth = pieces.shape
+    width = targets.shape[1]
+    return pl.pallas_call(
+        functools.partial(posterior_kernel, 2.0 / math.sqrt(depth)),
+        grid_spec=pltpu.PrefetchScalarGridSpec(
+            num_scalar_prefetch=1,
+            grid=(tiles,),
+            in_specs=[
+                pl.BlockSpec((parts, 1, piece, depth), lambda j, t: (0, j, 0, 0)),
+                pl.BlockSpec((1, width, depth), lambda j, t: (t[j], 0, 0)),
+                pl.BlockSpec((1, 1, width), lambda j, t: (j, 0, 0)),
+                pl.BlockSpec((1, 1, width), lambda j, t: (t[j], 0, 0)),
+            ],
+            out_specs=pl.BlockSpec((1, 1, 1, width, width), lambda j, t: (0, 0, j, 0, 0)),
+        ),
+        out_shape=jax.ShapeDtypeStruct((1, 1, tiles, width, width), F32),
+        compiler_params=pltpu.CompilerParams(vmem_limit_bytes=40 << 20),
+        name="posterior",
+    )(tile_tgt, pieces, targets, tile_row, column_pot)
+
+
+def swap(x, axis):
+    return lax.all_to_all(x, axis, split_axis=0, concat_axis=0, tiled=True)
+
+
+def on_device(source_emb, target_emb, slot_source, slot_target):
+    src_blocks, tgt_blocks = source_emb.shape[0], target_emb.shape[0]
+    src_count, tgt_count = lax.axis_size("src"), lax.axis_size("tgt")
+    own_row, own_col = lax.axis_index("src"), lax.axis_index("tgt")
+    tiles = slot_source.shape[2]
+    tile_src = slot_source[0, 0]
+    tile_tgt = slot_target[0, 0] - own_col * tgt_blocks
+    tile_home = tile_src // src_blocks
+
+    slots = jnp.concatenate([slot_source[0, 0], slot_target[0, 0]])
+    slots = jnp.pad(slots, (0, 128 - 2 * tiles))[None, None]
+    column_slots = swap(jnp.broadcast_to(slots, (src_count, 1, 128)), "src")[:, 0]
+    row_slots = swap(jnp.broadcast_to(slots, (tgt_count, 1, 128)), "tgt")[:, 0, :tiles]
+    named_src = column_slots[:, :tiles].reshape(-1) - own_row * src_blocks
+    named_tgt = column_slots[:, tiles : 2 * tiles].reshape(-1) - own_col * tgt_blocks
+    named = jnp.any(
+        (named_src[:, None, None] == jnp.arange(src_blocks)[None, :, None])
+        & (named_tgt[:, None, None] == jnp.arange(tgt_blocks)[None, None, :]),
+        axis=0,
+    ).astype(jnp.int32)
+    plan_column = home_plan(column_slots[:, :tiles], own_row, src_blocks)
+
+    targets = lax.all_gather(target_emb, "src", axis=1, tiled=True)
+    whole_blocks = lax.all_gather(source_emb, "tgt", axis=1, tiled=True)
+    all_pieces = lax.all_gather(source_emb, "src", axis=0, tiled=True)
+    pieces = swap(jnp.take(all_pieces, row_slots, axis=0), "tgt")
+
+    weights, sums = score_weights(whole_blocks, targets, named, tgt_count)
+    for iteration in range(ITERS):
+        if iteration:
+            sums, weights = weighted_sums(row_kernel, "row_sums", named, gathered, weights, tgt_count)
+        row_gathered = swap(sums, "tgt")
+        sums, weights = weighted_sums(column_kernel, "column_sums", named, row_gathered, weights, src_count)
+        gathered = swap(sums, "src")
+
+    row_total = jnp.sum(row_gathered, axis=0)[:, 0]
+    row_pot = -jnp.log(row_total)
+    column_pot = -jnp.log(jnp.sum(gathered, axis=0))
+    tile_row = jnp.take(swap(select_rows(row_pot, plan_column)[:, None], "src"), tile_home, axis=0)
+    log_post = posterior(pieces, targets, tile_row, column_pot, tile_tgt)
+
+    def unfinished(carry):
+        return carry[0]
+
+    def redo(carry):
+        return (jnp.zeros((), jnp.bool_),) + log_domain(
+            pieces, targets, tile_home, tile_tgt, plan_column, src_blocks
+        )
+
+    out_of_range = jnp.logical_not(row_total[0, 0] > 0.0)
+    carry = (out_of_range, log_post, row_pot, column_pot[:, 0])
+    return lax.while_loop(unfinished, redo, carry)[1:]
 
 
 def solution(mesh):

time: 1410 us -> 1450 us (1.028)
  waiting for transfers between devices: 502 us -> 255 us
  local copies, waits for them, and re-layouts: 45.7 us -> 228 us
  Pallas kernels: 0 us -> 96.7 us
  starting transfers between devices: 52 us -> 102 us
  blocking collectives: 614 us -> 575 us
    all_gather x1, waiting for transfers between devices: 414 us -> 63.3 us  [on_device(): targets = lax.all_gather(target_emb, 'src', axis=1, tiled=True)]
    unnamed x17 -> x38, local copies, waits for them, and re-layouts: 0.15 us -> 135 us
    all_to_all x8 -> x18, waiting for transfers between devices: 62.8 us -> 163 us  [the longest x9 140 us: swap(): return lax.all_to_all(x, axis, split_axis=0, concat_axis=0, tiled=True)]
    pallas_call x0 -> x7, Pallas kernels: none -> 96.7 us  [the longest x1 40.7 us: score_weights(): pl.pallas_call(functools.partial(scores_kernel, 2.0 / math.sqrt(depth) *...]
    while x0 -> x30, local copies, waits for them, and re-layouts: none -> 57.9 us  [the longest x2 33 us: on_device(): return lax.while_loop(unfinished, redo, carry)[1:]]
    all_to_all x8 -> x18, starting transfers between devices: 52 us -> 102 us  [the longest x9 44 us: swap(): return lax.all_to_all(x, axis, split_axis=0, concat_axis=0, tiled=True)]
    all_gather x1 -> x0, blocking collectives: 21 us -> none  [on_device(): lax.all_gather(slot_source, 'src', axis=0, tiled=True)]
    select_n x1 -> x4, other arithmetic: 21.3 us -> 0.31 us  [select_rows(): return jnp.where(present, picked, jnp.zeros((), table.dtype))]
  transfers between devices with their start and end apart: 10 -> 21, of which waited for: 7 -> 12; matrix products, arithmetic and copies ran while one was open for 1% -> 4% of each run, Pallas kernels for 0% -> 5%
where the time goes in v1:
time: 1450 us
  blocking collectives  575 us (40%)
  waiting for transfers between devices  255 us (18%)
  local copies, waits for them, and re-layouts  228 us (16%)
  other arithmetic  153 us (11%)
  starting transfers between devices  102 us (7%)
  Pallas kernels  96.7 us (7%)
  matrix products  19.3 us (1%)
  between operations  14.9 us (1%)
    pmax x3, blocking collectives, iterate(): largest = lax.pmax(local_max, 'src')  214 us
    psum x3, blocking collectives, iterate(): summed = lax.psum(local_sum * jnp.exp(local_max - largest), 'src')  209 us
    all_to_all x9, waiting for transfers between devices, swap(): return lax.all_to_all(x, axis, split_axis=0, concat_axis=0, tiled=True)  140 us
    unnamed x38, local copies, waits for them, and re-layouts  135 us
    pmax x3, blocking collectives, iterate(): largest = lax.pmax(local_max, 'tgt')  71.5 us
    psum x3, blocking collectives, iterate(): summed = lax.psum(local_sum * jnp.exp(local_max - largest), 'tgt')  70.7 us
    all_gather x1, waiting for transfers between devices, on_device(): targets = lax.all_gather(target_emb, 'src', axis=1, tiled=True)  63.3 us
    all_to_all x9, starting transfers between devices, swap(): return lax.all_to_all(x, axis, split_axis=0, concat_axis=0, tiled=True)  44 us
  transfers between devices with their start and end apart: 21, of which 12 were waited for; matrix products, arithmetic and copies ran while one was open for 4% of the time, Pallas kernels for 5%

profile of v1, /device:TPU:0, one launch (start us, length us, event | category | flops | bytes accessed | tf_op | source)
XLA Modules:
  0.0 1445.1 jit_solution(1058144068068203888)
XLA Ops:
  26.4 26.9 %all-gather.4.cloned.1.call-done = bf16[4,1024,768]{2,1,0:T(8,128)(2,1)} async-done(((bf16[4,128,768]{2,1,0:T(8,128)(2,1)}), bf16[4,1024,768]{2,1,0:T(8,128)(2,1)}) %all-gather.4.cloned.1.call-update) | async-done | bytes 6291472 | tf_op jit(solution)/shard_map/all_gather | solution.py:282
  53.3 63.3 %all-gather.6.cloned.1.call-done.y_ref = bf16[4,1024,768]{2,1,0:T(8,128)(2,1)} async-done(((bf16[4,64,768]{2,1,0:T(8,128)(2,1)}), bf16[4,1024,768]{2,1,0:T(8,128)(2,1)}) %all-gather.6.cloned.1.call-update) | async-done | bytes 6291472 | tf_op jit(solution)/shard_map/all_gather | solution.py:281
  116.6 40.7 %score_weights.1 = (bf16[4096,4096]{1,0:T(8,128)(2,1)S(1)}, f32[8,4,1,1024]{3,2,1,0:T(1,128)}) custom-call(s32[4,4]{1,0:T(4,128)} %convert_element_type.3.named, bf16[8,512,768]{2,1,0:T(8,128)(2,1)} %bitcast.93, bf16[4,1024,768]{2,1,0:T(8,128)(2,1)} %all-gather.6.cloned.1.call-done.y_ref), custom_call_target="tpu_custom_call" | custom-call | tf_op jit(solution)/shard_map/score_weights/pallas_call | solution.py:147
  157.3 11.6 copy-done
  183.4 11.3 copy-done.1
  201.1 11.1 copy-done.2
  247.4 11.1 copy-done.4
  285.4 11.1 copy-done.6
  329.2 11.1 copy-done.8
  371.4 11.1 gather_fusion.5
  406.2 103.1 %all-to-all-done.10.x_ref = bf16[8,6,128,768]{3,2,1,0:T(8,128)(2,1)} async-done(((bf16[8,6,128,768]{3,2,1,0:T(8,128)(2,1)}), bf16[8,6,128,768]{3,2,1,0:T(8,128)(2,1)}, u32[]{:S(2)}, u32[]{:S(2)}) %all-to-all-start.10) | async-done | bytes 9437216 | tf_op jit(solution)/shard_map/all_to_all | solution.py:256
  509.3 18.8 %posterior.1 = f32[1,1,6,1024,1024]{4,3,2,1,0:T(8,128)} custom-call(s32[6]{0:T(128)S(1)} %broadcast_subtract_fusion.tile_tgt, bf16[8,6,128,768]{3,2,1,0:T(8,128)(2,1)} %all-to-all-done.10.x_ref, bf16[4,1024,768]{2,1,0:T(8,128)(2,1)} %all-gather.6.cloned.1.call-done.y_ref, f32[6,1,1024]{2,1,0:T(1,128)S(1)} %broadcast_select_fusion.5.r_ref, ...), custom_call_target="tpu_custom_call" | custom-call | tf_op jit(solution)/shard_map/posterior/pallas_call | solution.py:236
  528.1 24.7 %copy.41 = f32[1,1,6,1024,1024]{3,4,2,1,0:T(8,128)} copy(f32[1,1,6,1024,1024]{4,3,2,1,0:T(8,128)} %posterior.1) | data formatting | bytes 50331648 | tf_op jit(solution)/shard_map/while | solution.py:310
  561.1 852.5 %while.28 = (pred[]{:T(512)}, f32[1,1,6,1024,1024]{3,4,2,1,0:T(8,128)}, f32[4,1024]{1,0:T(4,128)}, f32[4,1024]{1,0:T(4,128)}, s32[6]{0:T(128)S(1)}, /*index=5*/b...) while((pred[]{:T(512)}, ...), condition=%region_22.24_spmd, body=%region_5.23_spmd | while | flops 9751538688 | bytes 267753552 | solution.py:310
  569.7 19.3 %multiply_bitcast_fusion = f32[6,1024,1024]{1,2,0:T(8,128)} fusion(bf16[6,1024,768]{2,1,0:T(8,128)(2,1)} %bitcast.92, bf16[6,1024,768]{2,1,0:T(8,128)(2,1)} %gather_fusion.3, pred[6]{0:T(512)(128)(4,1)S(1)} %compare_and_fusion.2), kind=kOutput, calls=%fused_computation.46 | convolution fusion | flops 9674686464 | bytes 44040200 | tf_op jit(solution)/shard_map/while/body/jid,jkd->jik/dot_general | solution.py:44
  589.0 24.7 %copy.36 = f32[6,1024,1024]{2,1,0:T(8,128)} copy(f32[6,1024,1024]{1,2,0:T(8,128)} %multiply_bitcast_fusion) | data formatting | bytes 50331648 | tf_op jit(solution)/shard_map/while
  613.8 782.1 %while.30 = (s32[]{:T(128)}, f32[4,1024]{1,0:T(4,128)S(1)}, f32[4,1024]{1,0:T(4,128)}, f32[6,1024]{1,0:T(8,128)}, s32[6]{0:T(128)S(1)}, /*index=5*/s32[6]{0:T(12...) while((s32[]{:T(128)}, f32[4,1024]{1,0:T(4,128)S(1)}, ...), condition=%wide.region_21.22_spmd.clone, body=%wide.region_6.21_spmd.clone.sunk | while | flops 64261480 | bytes 103953968 | solution.py:77
  652.4 23.9 %pmax.20 = f32[4,1024]{1,0:T(4,128)S(1)} all-reduce(f32[4,1024]{1,0:T(4,128)S(1)} %select_reduce_fusion.13), channel_id=1, replica_groups=mesh['src'=16,'tgt'=8] {'tgt'}, use_global_device_ids=true, to_apply=%region_10.10 | all-reduce | flops 4096 | bytes 32768 | tf_op jit(solution)/shard_map/while/body/while/body/eval_jaxpr/pmax | solution.py:61
  676.5 23.6 %psum.20 = f32[4,1024]{1,0:T(4,128)S(1)} all-reduce(f32[4,1024]{1,0:T(4,128)S(1)} %exponential_multiply_fusion.4), channel_id=1, replica_groups=mesh['src'=16,'tgt'=8] {'tgt'}, use_global_device_ids=true, to_apply=%region_14.14 | all-reduce | flops 4096 | bytes 32768 | tf_op jit(solution)/shard_map/while/body/while/body/eval_jaxpr/psum | solution.py:62
  736.9 71.2 %pmax.21 = f32[4,1024]{1,0:T(4,128)S(1)} all-reduce(f32[4,1024]{1,0:T(4,128)S(1)} %select_reduce_fusion.16), channel_id=1, replica_groups=mesh['src'=16,'tgt'=8] {'src'}, use_global_device_ids=true, to_apply=%region_17.17 | all-reduce | flops 4096 | bytes 32768 | tf_op jit(solution)/shard_map/while/body/while/body/eval_jaxpr/pmax | solution.py:72
  808.2 69.6 %psum.21 = f32[4,1024]{1,0:T(4,128)S(1)} all-reduce(f32[4,1024]{1,0:T(4,128)S(1)} %exponential_multiply_fusion.5), channel_id=1, replica_groups=mesh['src'=16,'tgt'=8] {'src'}, use_global_device_ids=true, to_apply=%region_20.20 | all-reduce | flops 4096 | bytes 32768 | tf_op jit(solution)/shard_map/while/body/while/body/eval_jaxpr/psum | solution.py:73
  892.2 10.9 exponential_reduce_fusion.4
  911.5 23.9 %pmax.20 = f32[4,1024]{1,0:T(4,128)S(1)} all-reduce(f32[4,1024]{1,0:T(4,128)S(1)} %select_reduce_fusion.13), channel_id=1, replica_groups=mesh['src'=16,'tgt'=8] {'tgt'}, use_global_device_ids=true, to_apply=%region_10.10 | all-reduce | flops 4096 | bytes 32768 | tf_op jit(solution)/shard_map/while/body/while/body/eval_jaxpr/pmax | solution.py:61
  935.5 23.6 %psum.20 = f32[4,1024]{1,0:T(4,128)S(1)} all-reduce(f32[4,1024]{1,0:T(4,128)S(1)} %exponential_multiply_fusion.4), channel_id=1, replica_groups=mesh['src'=16,'tgt'=8] {'tgt'}, use_global_device_ids=true, to_apply=%region_14.14 | all-reduce | flops 4096 | bytes 32768 | tf_op jit(solution)/shard_map/while/body/while/body/eval_jaxpr/psum | solution.py:62
  995.9 71.2 %pmax.21 = f32[4,1024]{1,0:T(4,128)S(1)} all-reduce(f32[4,1024]{1,0:T(4,128)S(1)} %select_reduce_fusion.16), channel_id=1, replica_groups=mesh['src'=16,'tgt'=8] {'src'}, use_global_device_ids=true, to_apply=%region_17.17 | all-reduce | flops 4096 | bytes 32768 | tf_op jit(solution)/shard_map/while/body/while/body/eval_jaxpr/pmax | solution.py:72
  1067.2 69.6 %psum.21 = f32[4,1024]{1,0:T(4,128)S(1)} all-reduce(f32[4,1024]{1,0:T(4,128)S(1)} %exponential_multiply_fusion.5), channel_id=1, replica_groups=mesh['src'=16,'tgt'=8] {'src'}, use_global_device_ids=true, to_apply=%region_20.20 | all-reduce | flops 4096 | bytes 32768 | tf_op jit(solution)/shard_map/while/body/while/body/eval_jaxpr/psum | solution.py:73
  1170.5 23.9 %pmax.20 = f32[4,1024]{1,0:T(4,128)S(1)} all-reduce(f32[4,1024]{1,0:T(4,128)S(1)} %select_reduce_fusion.13), channel_id=1, replica_groups=mesh['src'=16,'tgt'=8] {'tgt'}, use_global_device_ids=true, to_apply=%region_10.10 | all-reduce | flops 4096 | bytes 32768 | tf_op jit(solution)/shard_map/while/body/while/body/eval_jaxpr/pmax | solution.py:61
  1194.6 23.6 %psum.20 = f32[4,1024]{1,0:T(4,128)S(1)} all-reduce(f32[4,1024]{1,0:T(4,128)S(1)} %exponential_multiply_fusion.4), channel_id=1, replica_groups=mesh['src'=16,'tgt'=8] {'tgt'}, use_global_device_ids=true, to_apply=%region_14.14 | all-reduce | flops 4096 | bytes 32768 | tf_op jit(solution)/shard_map/while/body/while/body/eval_jaxpr/psum | solution.py:62
  1254.9 71.2 %pmax.21 = f32[4,1024]{1,0:T(4,128)S(1)} all-reduce(f32[4,1024]{1,0:T(4,128)S(1)} %select_reduce_fusion.16), channel_id=1, replica_groups=mesh['src'=16,'tgt'=8] {'src'}, use_global_device_ids=true, to_apply=%region_17.17 | all-reduce | flops 4096 | bytes 32768 | tf_op jit(solution)/shard_map/while/body/while/body/eval_jaxpr/pmax | solution.py:72
  1326.3 69.6 %psum.21 = f32[4,1024]{1,0:T(4,128)S(1)} all-reduce(f32[4,1024]{1,0:T(4,128)S(1)} %exponential_multiply_fusion.5), channel_id=1, replica_groups=mesh['src'=16,'tgt'=8] {'src'}, use_global_device_ids=true, to_apply=%region_20.20 | all-reduce | flops 4096 | bytes 32768 | tf_op jit(solution)/shard_map/while/body/while/body/eval_jaxpr/psum | solution.py:73
  1396.5 17.1 %add_bitcast_fusion = f32[1,1,6,1024,1024]{3,4,2,1,0:T(8,128)} fusion(f32[6,1024,1024]{1,2,0:T(8,128)} %multiply_bitcast_fusion, f32[6,1024]{1,0:T(8,128)S(1)} %broadcast_select_fusion.3, f32[6,1024]{1,0:T(8,128)} %get-tuple-element.100), kind=kLoop, calls=%fused_computation.45 | loop fusion | flops 12582912 | bytes 50380800 | tf_op jit(solution)/shard_map/while/body/broadcast_in_dim | solution.py:80
  1413.6 24.7 %copy.43 = f32[1,1,6,1024,1024]{4,3,2,1,0:T(8,128)} copy(f32[1,1,6,1024,1024]{3,4,2,1,0:T(8,128)} %get-tuple-element.427) | data formatting | bytes 50331648
  (262 shorter events, 412.3 us)
Async XLA Ops:
  7.2 46.2 %all-gather.4.cloned.1.call-start = ((), (), s32[]{:S(2)}) async-start(), calls=%async_computation.13 | async-start | bytes 7077888 | tf_op jit(solution)/shard_map/all_gather | solution.py:282
  7.9 108.7 %all-gather.6.cloned.1.call-start = ((), (), s32[]{:S(2)}) async-start(), calls=%async_computation.14 | async-start | bytes 6684672 | tf_op jit(solution)/shard_map/all_gather | solution.py:281
  8.6 362.8 %all-gather.8.cloned.1.call-start = ((), (), s32[]{:S(2)}) async-start(), calls=%async_computation.15 | async-start | bytes 13369344 | tf_op jit(solution)/shard_map/all_gather | solution.py:283
  10.7 14.6 %all-to-all-start.3 = ((s32[16,1,128]{2,1,0:T(1,128)}), s32[16,1,128]{2,1,0:T(1,128)S(1)}, u32[]{:S(2)}, u32[]{:S(2)}) async-start(s32[16,1,128]{2,1,0:T(1,128)} %broadcast_in_dim.309), calls=%async_computation.3 | async-start | bytes 16384 | tf_op jit(solution)/shard_map/all_to_all | solution.py:256
  26.4 200.5 %copy-start.11 = (s32[4,4]{1,0:T(4,128)S(1)}, s32[4,4]{1,0:T(4,128)}, u32[]{:S(2)}) copy-start(s32[4,4]{1,0:T(4,128)} %convert_element_type.3.named) | copy-start | bytes 196
  180.0 32.1 %all-to-all-start.9 = ((s32[8,1,128]{2,1,0:T(1,128)}), s32[8,1,128]{2,1,0:T(1,128)S(1)}, u32[]{:S(2)}, u32[]{:S(2)}) async-start(s32[8,1,128]{2,1,0:T(1,128)} %broadcast_in_dim.310), calls=%async_computation.9 | async-start | bytes 8192 | tf_op jit(solution)/shard_map/all_to_all | solution.py:256
  212.2 14.7 %all-to-all-start.5 = ((f32[16,4,1,1024]{3,2,1,0:T(1,128)}), f32[16,4,1,1024]{3,2,1,0:T(1,128)S(1)}, u32[]{:S(2)}, u32[]{:S(2)}) async-start(f32[16,4,1,1024]{3,2,1,0:T(1,128)} %get-tuple-element.123), calls=%async_computation.5 | async-start | bytes 524288 | tf_op jit(solution)/shard_map/all_to_all | solution.py:256
  258.5 10.6 all-to-all-start.6
  296.4 12.3 all-to-all-start.7
  300.3 71.1 %copy-start.19 = (s32[16]{0:T(128)}, s32[16]{0:T(128)S(1)}, u32[]{:S(2)}) copy-start(s32[16]{0:T(128)S(1)} %get-tuple-element.382) | copy-start | bytes 196
  340.3 9.4 all-to-all-start.8
  349.9 32.7 %copy-start.12 = (f32[4,1024]{1,0:T(4,128)}, f32[4,1024]{1,0:T(4,128)S(1)}, u32[]{:S(2)}) copy-start(f32[4,1024]{1,0:T(4,128)S(1)} %log_negate_fusion.1) | copy-start | bytes 49156
  351.2 31.3 %all-to-all-start.11 = ((f32[16,1,1024]{2,1,0:T(1,128)}), f32[16,1,1024]{2,1,0:T(1,128)S(1)}, u32[]{:S(2)}, u32[]{:S(2)}) async-start(f32[16,1,1024]{2,1,0:T(1,128)} %copy.40), calls=%async_computation.11 | async-start | bytes 131072 | tf_op jit(solution)/shard_map/all_to_all | solution.py:256
  371.4 32.0 %copy-start.22 = (s32[1,1,6]{2,1,0:T(1,128)S(1)}, s32[1,1,6]{2,1,0:T(1,128)}, u32[]{:S(2)}) copy-start(s32[1,1,6]{2,1,0:T(1,128)} %param.12) | copy-start | bytes 76
  371.4 32.0 %copy-start.21 = (s32[1,1,6]{2,1,0:T(1,128)S(1)}, s32[1,1,6]{2,1,0:T(1,128)}, u32[]{:S(2)}) copy-start(s32[1,1,6]{2,1,0:T(1,128)} %param.13) | copy-start | bytes 76
  382.5 15.8 %all-to-all-start.12 = ((f32[16,4,1,1024]{3,2,1,0:T(1,128)}), f32[16,4,1,1024]{3,2,1,0:T(1,128)S(1)}, u32[]{:S(2)}, u32[]{:S(2)}) async-start(f32[16,4,1,1024]{3,2,1,0:T(1,128)} %get-tuple-element.131), calls=%async_computation.12 | async-start | bytes 524288 | tf_op jit(solution)/shard_map/all_to_all | solution.py:256
  398.4 110.9 %all-to-all-start.10 = ((bf16[8,6,128,768]{3,2,1,0:T(8,128)(2,1)}), bf16[8,6,128,768]{3,2,1,0:T(8,128)(2,1)}, u32[]{:S(2)}, u32[]{:S(2)}) async-start(bf16[8,6,128,768]{3,2,1,0:T(8,128)(2,1)} %broadcast_select_fusion.4), calls=%async_computation.10 | async-start | bytes 18874368 | tf_op jit(solution)/shard_map/all_to_all | solution.py:256
  528.1 33.0 %copy-start.20 = (s32[16]{0:T(128)S(1)}, s32[16]{0:T(128)}, u32[]{:S(2)}) copy-start(s32[16]{0:T(128)} %copy-done.19) | copy-start | bytes 196
  613.8 782.7 %copy-start.18 = (pred[6]{0:T(512)(128)(4,1)S(1)}, pred[6]{0:T(512)(128)(4,1)}, u32[]{:S(2)}) copy-start(pred[6]{0:T(512)(128)(4,1)} %copy-done.17) | copy-start | bytes 22 | tf_op jit(solution)/shard_map/while
  624.7 20.4 %all-to-all-start = ((f32[16,1,1024]{2,1,0:T(1,128)}), f32[16,1,1024]{2,1,0:T(1,128)S(1)}, u32[]{:S(2)}, u32[]{:S(2)}) async-start(f32[16,1,1024]{2,1,0:T(1,128)} %copy.62), calls=%async_computation | async-start | bytes 131072 | tf_op jit(solution)/shard_map/while/body/while/body/eval_jaxpr/all_to_all | solution.py:57
  645.1 31.2 %all-to-all-start.1 = ((f32[16,1,1024]{2,1,0:T(1,128)}), f32[16,1,1024]{2,1,0:T(1,128)S(1)}, u32[]{:S(2)}, u32[]{:S(2)}) async-start(f32[16,1,1024]{2,1,0:T(1,128)} %copy.64), calls=%async_computation.1 | async-start | bytes 131072 | tf_op jit(solution)/shard_map/while/body/while/body/eval_jaxpr/all_to_all | solution.py:58
  700.1 36.7 %copy-start.13 = (f32[4,1024]{1,0:T(4,128)}, f32[4,1024]{1,0:T(4,128)S(1)}, u32[]{:S(2)}) copy-start(f32[4,1024]{1,0:T(4,128)S(1)} %add_negate_fusion.4) | copy-start | bytes 49156 | tf_op jit(solution)/shard_map/while/body/while
  701.4 14.6 %all-to-all-start.2 = ((f32[16,1,1024]{2,1,0:T(1,128)}), f32[16,1,1024]{2,1,0:T(1,128)S(1)}, u32[]{:S(2)}, u32[]{:S(2)}) async-start(f32[16,1,1024]{2,1,0:T(1,128)} %copy.66), calls=%async_computation.2 | async-start | bytes 131072 | tf_op jit(solution)/shard_map/while/body/while/body/eval_jaxpr/all_to_all | solution.py:64
  888.7 15.5 %all-to-all-start = ((f32[16,1,1024]{2,1,0:T(1,128)}), f32[16,1,1024]{2,1,0:T(1,128)S(1)}, u32[]{:S(2)}, u32[]{:S(2)}) async-start(f32[16,1,1024]{2,1,0:T(1,128)} %copy.62), calls=%async_computation | async-start | bytes 131072 | tf_op jit(solution)/shard_map/while/body/while/body/eval_jaxpr/all_to_all | solution.py:57
  904.2 31.2 %all-to-all-start.1 = ((f32[16,1,1024]{2,1,0:T(1,128)}), f32[16,1,1024]{2,1,0:T(1,128)S(1)}, u32[]{:S(2)}, u32[]{:S(2)}) async-start(f32[16,1,1024]{2,1,0:T(1,128)} %copy.64), calls=%async_computation.1 | async-start | bytes 131072 | tf_op jit(solution)/shard_map/while/body/while/body/eval_jaxpr/all_to_all | solution.py:58
  959.1 36.7 %copy-start.13 = (f32[4,1024]{1,0:T(4,128)}, f32[4,1024]{1,0:T(4,128)S(1)}, u32[]{:S(2)}) copy-start(f32[4,1024]{1,0:T(4,128)S(1)} %add_negate_fusion.4) | copy-start | bytes 49156 | tf_op jit(solution)/shard_map/while/body/while
  960.5 14.6 %all-to-all-start.2 = ((f32[16,1,1024]{2,1,0:T(1,128)}), f32[16,1,1024]{2,1,0:T(1,128)S(1)}, u32[]{:S(2)}, u32[]{:S(2)}) async-start(f32[16,1,1024]{2,1,0:T(1,128)} %copy.66), calls=%async_computation.2 | async-start | bytes 131072 | tf_op jit(solution)/shard_map/while/body/while/body/eval_jaxpr/all_to_all | solution.py:64
  1147.7 15.5 %all-to-all-start = ((f32[16,1,1024]{2,1,0:T(1,128)}), f32[16,1,1024]{2,1,0:T(1,128)S(1)}, u32[]{:S(2)}, u32[]{:S(2)}) async-start(f32[16,1,1024]{2,1,0:T(1,128)} %copy.62), calls=%async_computation | async-start | bytes 131072 | tf_op jit(solution)/shard_map/while/body/while/body/eval_jaxpr/all_to_all | solution.py:57
  1163.2 31.2 %all-to-all-start.1 = ((f32[16,1,1024]{2,1,0:T(1,128)}), f32[16,1,1024]{2,1,0:T(1,128)S(1)}, u32[]{:S(2)}, u32[]{:S(2)}) async-start(f32[16,1,1024]{2,1,0:T(1,128)} %copy.64), calls=%async_computation.1 | async-start | bytes 131072 | tf_op jit(solution)/shard_map/while/body/while/body/eval_jaxpr/all_to_all | solution.py:58
  1218.2 36.7 %copy-start.13 = (f32[4,1024]{1,0:T(4,128)}, f32[4,1024]{1,0:T(4,128)S(1)}, u32[]{:S(2)}) copy-start(f32[4,1024]{1,0:T(4,128)S(1)} %add_negate_fusion.4) | copy-start | bytes 49156 | tf_op jit(solution)/shard_map/while/body/while
  1219.5 14.6 %all-to-all-start.2 = ((f32[16,1,1024]{2,1,0:T(1,128)}), f32[16,1,1024]{2,1,0:T(1,128)S(1)}, u32[]{:S(2)}, u32[]{:S(2)}) async-start(f32[16,1,1024]{2,1,0:T(1,128)} %copy.66), calls=%async_computation.2 | async-start | bytes 131072 | tf_op jit(solution)/shard_map/while/body/while/body/eval_jaxpr/all_to_all | solution.py:64
  1234.8 20.1 %copy-start.16 = (f32[6,1024]{1,0:T(8,128)}, f32[6,1024]{1,0:T(8,128)S(1)}, u32[]{:S(2)}) copy-start(f32[6,1024]{1,0:T(8,128)S(1)} %broadcast_select_fusion.13) | copy-start | bytes 73732 | tf_op jit(solution)/shard_map/while/body/while
  (16 other events, 187.9 us)
Sparse Core Ops, SparseCore 0:
  9.7 43.5 all-gather.3
  55.5 61.1 all-gather.5
  118.8 89.5 all-gather.7

commit v2 on v0

v2 whole, which is shorter than its diff:
```python
import functools
import math

import jax
import jax.numpy as jnp
from jax import lax
from jax.experimental import pallas as pl
from jax.experimental.pallas import tpu as pltpu
from jax.sharding import PartitionSpec as P

ITERS = 3
NEG = -1e30
F32, BF16 = jnp.float32, jnp.bfloat16
LIMIT = 20.0
ROWS = 512
PARTS = 2
LIGHT = pl.CostEstimate(flops=0, bytes_accessed=1024, transcendentals=0)
NT = (((1,), (1,)), ((), ()))


def combine_blocks(maxima, totals, labels, groups):
    matches = labels[:, None] == jnp.arange(groups)[None, :]
    largest = jnp.max(jnp.where(matches[:, :, None], maxima[:, None, :], NEG), axis=0)
    diffs = jnp.where(matches[:, :, None], maxima[:, None, :] - largest[None, :, :], NEG)
    scaled = jnp.where(matches[:, :, None], totals[:, None, :] * jnp.exp(diffs), 0.0)
    return (largest, jnp.sum(scaled, axis=0))


def home_plan(slot_ids, own_row, per_row):
    matched = slot_ids // per_row == own_row
    chosen = jnp.sum(jnp.where(matched, slot_ids % per_row, 0), axis=1)
    return jnp.where(jnp.any(matched, axis=1), chosen, -1)


def select_rows(table, plan):
    picked = jnp.take(table, jnp.maximum(plan, 0), axis=0, mode="clip")
    present = (plan >= 0).reshape((-1,) + (1,) * (table.ndim - 1))
    return jnp.where(present, picked, jnp.zeros((), table.dtype))


def log_domain(scores, tile_home, tile_tgt, plan_column, src_blocks, tgt_blocks):
    block_rows = scores.shape[1]
    src_count = lax.axis_size("src")

    def iterate(_, carry):
        column_pot, _, _ = carry
        tile_col = jnp.take(column_pot, tile_tgt, axis=0)
        shifted = scores + tile_col[:, None, :]
        row_max = jnp.max(shifted, axis=2)
        row_sum = jnp.sum(jnp.exp(shifted - row_max[:, :, None]), axis=2)
        send_max, send_sum = combine_blocks(row_max, row_sum, tile_home, src_count)
        local_max, local_sum = combine_blocks(swap(send_max, "src"), swap(send_sum, "src"), plan_column, src_blocks)
        largest = lax.pmax(local_max, "tgt")
        summed = lax.psum(local_sum * jnp.exp(local_max - largest), "tgt")
        row_pot = -(largest + jnp.log(summed))
        tile_row = jnp.take(swap(select_rows(row_pot, plan_column), "src"), tile_home, axis=0)
        shifted = scores + tile_row[:, :, None]
        col_max = jnp.max(shifted, axis=1)
        col_sum = jnp.sum(jnp.exp(shifted - col_max[:, None, :]), axis=1)
        local_max, local_sum = combine_blocks(col_max, col_sum, tile_tgt, tgt_blocks)
        largest = lax.pmax(local_max, "src")
        summed = lax.psum(local_sum * jnp.exp(local_max - largest), "src")
        return (-(largest + jnp.log(summed)), row_pot, tile_row)

    init = (
        jnp.zeros((tgt_blocks, block_rows), F32),
        jnp.zeros((src_blocks, block_rows), F32),
        jnp.zeros((scores.shape[0], block_rows), F32),
    )
    return lax.fori_loop(0, ITERS, iterate, init)


def stack3(x):
    hi = x.astype(BF16).astype(F32)
    mid = (x - hi).astype(BF16).astype(F32)
    low = x - hi - mid
    row = lax.broadcasted_iota(jnp.int32, (16, x.shape[1]), 0)
    parts = [jnp.broadcast_to(p, row.shape) for p in (hi, mid, low)]
    return jnp.where(row == 0, parts[0], jnp.where(row == 1, parts[1], jnp.where(row == 2, parts[2], 0.0))).astype(BF16)


def lane_totals(lanes):
    ones = jnp.ones((8, 128), F32)
    return lax.dot_general(ones, lanes, NT, preferred_element_type=F32, precision=lax.Precision.HIGHEST)[0:1]


def put(o_ref, block, cols, out):
    o_ref[:, block, :, cols] = jnp.broadcast_to(out[None], (o_ref.shape[0],) + out.shape)


def start_all(copies):
    for copy in copies:
        copy.start()


def wait_all(copies):
    for copy in copies:
        copy.wait()


def scores_kernel(scale, side, named, where, x_hbm, *refs):
    pieces, refs = refs[:8], refs[-11:]
    k_hbm, sum_ref, targets_hbm, x, y, k_out, lowest, x_sem, y_sem, k_sem, leave = refs
    blocks, width, _ = y.shape
    rows = k_out.shape[1]
    half = blocks // 2
    small = width // (side * side)

    def target_copy(route, far, near):
        first = lax.rem(where[route] - near + side, side)
        second = lax.rem(where[1 - route] - far + side, side)
        at = (first * side + second if route == 0 else second * side + first) * small
        return pltpu.make_async_copy(
            pieces[route * side + far].at[near],
            y.at[pl.ds(route * half, half), pl.ds(pl.multiple_of(at, small), small), :],
            y_sem.at[route, far, near],
        )

    def target_copies(route):
        return [target_copy(route, far, near) for far in range(side) for near in range(side)]

    def source_copy(b):
        return pltpu.make_async_copy(x_hbm.at[b], x.at[b], x_sem.at[b])

    def out_copy(i, slot):
        at = pl.ds(pl.multiple_of(i * rows, rows), rows)
        return pltpu.make_async_copy(k_out.at[slot], k_hbm.at[at], k_sem.at[slot])

    start_all(target_copies(0))
    source_copy(0).start()
    start_all(target_copies(1))
    start_all([source_copy(b) for b in range(1, blocks)])
    lowest[...] = jnp.ones_like(lowest)
    wait_all(target_copies(0) + target_copies(1))
    whole_targets = pltpu.make_async_copy(y, targets_hbm, leave)
    whole_targets.start()
    per = width // rows

    def step(i, carry):
        b, part, slot = i // per, lax.rem(i, per), lax.rem(i, 2)

        @pl.when(part == 0)
        def _():
            source_copy(b).wait()

        @pl.when(i >= 2)
        def _():
            out_copy(i - 2, slot).wait()

        low = lowest[...]
        lanes = jnp.zeros((rows, 128), F32)
        here = x[b, pl.ds(pl.multiple_of(part * rows, rows), rows), :]
        for c in range(blocks):
            s = lax.dot_general(here, y[c], NT, preferred_element_type=F32)
            e = jnp.exp2(s * scale)
            k = e.astype(BF16)
            is_named = named[b, c] > 0
            k_out[slot, :, c * width : (c + 1) * width] = jnp.where(is_named, k, jnp.zeros_like(k))
            acc, least = e[:, :128], k[:, :128]
            for g in range(128, width, 128):
                acc = acc + e[:, g : g + 128]
                least = jnp.minimum(least, k[:, g : g + 128])
            lanes = lanes + jnp.where(is_named, acc, 0.0)
            low = jnp.minimum(low, jnp.min(least.reshape(rows // 16, 16, 128), axis=0))
        lowest[...] = low
        out_copy(i, slot).start()
        total = lane_totals(lanes)
        fine = (jnp.min(low.astype(F32)) > math.exp(-LIMIT)) & (jnp.max(total) < math.exp(LIMIT))
        put(sum_ref, b, pl.ds(pl.multiple_of(part * rows, rows), rows), jnp.where(fine, total, jnp.nan))
        return carry

    lax.fori_loop(0, blocks * per, step, 0)
    for i in (blocks * per - 2, blocks * per - 1):
        out_copy(i, i % 2).wait()
    whole_targets.wait()


ANYWHERE = pl.BlockSpec(memory_space=pl.ANY)
SCALARS = pl.BlockSpec(memory_space=pltpu.SMEM)
WHOLE = pl.BlockSpec(memory_space=pltpu.VMEM)


def far(arrays):
    return [pltpu.with_memory_space_constraint(x, pltpu.HBM) for x in arrays]


def score_weights(x, pieces, where, named, copies, side, after):
    blocks, width, depth = x.shape
    n = blocks * width
    return pl.pallas_call(
        functools.partial(scores_kernel, 2.0 / math.sqrt(depth) * math.log2(math.e), side),
        in_specs=[SCALARS, SCALARS] + [ANYWHERE] * (9 + len(after)),
        out_specs=[ANYWHERE, WHOLE, ANYWHERE],
        scratch_shapes=[
            pltpu.VMEM((blocks, width, depth), BF16),
            pltpu.VMEM((blocks, width, depth), BF16),
            pltpu.VMEM((2, ROWS, n), BF16),
            pltpu.VMEM((16, 128), BF16),
            pltpu.SemaphoreType.DMA((blocks,)),
            pltpu.SemaphoreType.DMA((2, side, side)),
            pltpu.SemaphoreType.DMA((2,)),
            pltpu.SemaphoreType.DMA,
        ],
        out_shape=[
            jax.ShapeDtypeStruct((n, n), BF16),
            jax.ShapeDtypeStruct((copies, blocks, 1, width), F32),
            jax.ShapeDtypeStruct((blocks, width, depth), BF16),
        ],
        compiler_params=pltpu.CompilerParams(vmem_limit_bytes=44 << 20),
        cost_estimate=LIGHT,
        name="score_weights",
    )(named, where, *far([x, *pieces, *after]))


def inverse_parts(g_ref, low, high):
    total = jnp.sum(g_ref[...], axis=0)
    fine = (jnp.min(total) >= low) & (jnp.max(total) <= high)
    return [1.0 / total[b] for b in range(total.shape[0])], jnp.where(fine, 0.0, jnp.nan)


def column_kernel(g_ref, k_hbm, *refs):
    o_ref, k, sem = refs[-3:]
    parts, n, cols = k.shape
    copies = [pltpu.make_async_copy(k_hbm.at[:, pl.ds(j * cols, cols)], k.at[j], sem.at[j]) for j in range(parts)]
    start_all(copies)
    inv, spoil = inverse_parts(g_ref, 1e-38, 1e38)
    blocks, width = len(inv), inv[0].shape[1]
    lhs = [stack3(v) for v in inv]
    per = width // cols
    for j in range(parts):
        copies[j].wait()
        acc = jnp.zeros((16, cols), F32)
        for b in range(blocks):
            acc = acc + jnp.dot(lhs[b], k[j, b * width : (b + 1) * width, :], preferred_element_type=F32)
        start = (j % per) * cols
        put(o_ref, j // per, slice(start, start + cols), acc[0:1] + acc[1:2] + acc[2:3] + spoil)


def row_kernel(g_ref, k_hbm, *refs):
    o_ref, k, sem = refs[-3:]
    parts, rows, n = k.shape
    copies = [pltpu.make_async_copy(k_hbm.at[pl.ds(j * rows, rows)], k.at[j], sem.at[j]) for j in range(parts)]
    start_all(copies)
    inv, spoil = inverse_parts(g_ref, math.exp(-LIMIT), math.exp(LIMIT))
    blocks, width = len(inv), inv[0].shape[1]
    half = blocks // 2
    lhs = [stack3(v) for v in inv[:half]]
    per = width // rows
    for j in range(parts):
        copies[j].wait()
        acc = jnp.zeros((16, rows), F32)
        for c in range(half):
            acc = acc + lax.dot_general(
                lhs[c], k[j, :, c * width : (c + 1) * width], NT, preferred_element_type=F32
            )
        lanes = jnp.zeros((rows, 128), F32)
        for c in range(half, blocks):
            for g in range(0, width, 128):
                at = c * width + g
                lanes = lanes + k[j, :, at : at + 128].astype(F32) * inv[c][:, g : g + 128]
        start = (j % per) * rows
        put(o_ref, j // per, slice(start, start + rows), acc[0:1] + acc[1:2] + acc[2:3] + lane_totals(lanes) + spoil)


def weighted_sums(kernel, gathered, k, copies, after=()):
    n = k.shape[0]
    parts = n // ROWS
    shape = (parts, n, ROWS) if kernel is column_kernel else (parts, ROWS, n)
    return pl.pallas_call(
        kernel,
        in_specs=[WHOLE, ANYWHERE] + [ANYWHERE] * len(after),
        out_specs=WHOLE,
        out_shape=jax.ShapeDtypeStruct((copies,) + gathered.shape[1:], F32),
        scratch_shapes=[pltpu.VMEM(shape, BF16), pltpu.SemaphoreType.DMA((parts,))],
        compiler_params=pltpu.CompilerParams(vmem_limit_bytes=44 << 20),
        cost_estimate=LIGHT,
        name="column_sums" if kernel is column_kernel else "row_sums",
    )(gathered, *far([k, *after]))


def cut_kernel(x_ref, *refs):
    outs = refs[-PARTS:]
    rows = outs[0].shape[1]
    for part, out in enumerate(outs):
        out[...] = x_ref[:, part * rows : (part + 1) * rows, :]


def cut(x, after):
    shape = (x.shape[0], x.shape[1] // PARTS, x.shape[2])
    return pl.pallas_call(
        cut_kernel,
        in_specs=[WHOLE] + [ANYWHERE] * len(after),
        out_specs=[WHOLE] * PARTS,
        out_shape=[jax.ShapeDtypeStruct(shape, x.dtype)] * PARTS,
        compiler_params=pltpu.CompilerParams(vmem_limit_bytes=16 << 20),
        cost_estimate=LIGHT,
        name="cut_rows",
    )(x, *far(after))


def gate_kernel(x_ref, *refs):
    refs[-1][...] = x_ref[...]


def gate(x, after):
    return pl.pallas_call(
        gate_kernel,
        in_specs=[WHOLE] + [ANYWHERE] * len(after),
        out_specs=WHOLE,
        out_shape=jax.ShapeDtypeStruct(x.shape, x.dtype),
        cost_estimate=LIGHT,
        name="gate",
    )(x, *far(after))


def pick_kernel(ids, table, first, *refs):
    del first
    outs, buf, come, go = refs[:-3], refs[-3], refs[-2], refs[-1]
    groups, tiles = buf.shape[:2]

    def fetch(i, j):
        return pltpu.make_async_copy(table.at[ids[i, j]], buf.at[i, j], come.at[i, j])

    for i in range(groups):
        start_all([fetch(i, j) for j in range(tiles)])
    stores = [pltpu.make_async_copy(buf.at[i], outs[i], go.at[i]) for i in range(groups)]
    for i in range(groups):
        wait_all([fetch(i, j) for j in range(tiles)])
        stores[i].start()
    wait_all(stores)


def pick(table, ids, after):
    groups, tiles = ids.shape
    shape = (tiles,) + table.shape[1:]
    return pl.pallas_call(
        pick_kernel,
        in_specs=[SCALARS, ANYWHERE, ANYWHERE],
        out_specs=[ANYWHERE] * groups,
        out_shape=[jax.ShapeDtypeStruct(shape, table.dtype)] * groups,
        scratch_shapes=[
            pltpu.VMEM((groups,) + shape, table.dtype),
            pltpu.SemaphoreType.DMA((groups, tiles)),
            pltpu.SemaphoreType.DMA((groups,)),
        ],
        compiler_params=pltpu.CompilerParams(vmem_limit_bytes=16 << 20),
        cost_estimate=LIGHT,
        name="pick_pieces",
    )(ids, *far([table, after]))


def posterior_kernel(scale, count, tile_tgt, places, *refs):
    x_hbm, refs = refs[:count], refs[count:]
    y_hbm, r_ref, c_ref, o_hbm, x, y, o, x_sem, y_sem, o_sem = refs
    tiles, width, depth = x.shape
    piece = x_hbm[0].shape[1]
    groups = count // PARTS
    cuts = o_sem.shape[1]
    rows = width // cuts

    def x_copies(j):
        return [
            pltpu.make_async_copy(
                x_hbm[part * groups + p].at[j],
                x.at[j, pl.ds(pl.multiple_of((places[p] * PARTS + part) * piece, piece), piece)],
                x_sem.at[j, part, p],
            )
            for part in range(PARTS)
            for p in range(groups)
        ]

    def y_copy(j):
        return pltpu.make_async_copy(y_hbm.at[tile_tgt[j]], y.at[j], y_sem.at[j])

    def o_copy(j, q):
        at = pl.ds(q * rows, rows)
        return pltpu.make_async_copy(o.at[j, at], o_hbm.at[0, 0, j, at], o_sem.at[j, q])

    for j in range(tiles):
        y_copy(j).start()
        start_all(x_copies(j))

    def step(j, carry):
        y_copy(j).wait()
        wait_all(x_copies(j))
        col = c_ref[tile_tgt[j]]
        for q in range(cuts):
            at = slice(q * rows, (q + 1) * rows)
            row = jnp.broadcast_to(r_ref[j, :, at], (128, rows)).T
            for start in range(0, width, 256):
                s = lax.dot_general(x[j, at], y[j, start : start + 256], NT, preferred_element_type=F32) * scale
                for g in range(0, 256, 128):
                    cols = slice(start + g, start + g + 128)
                    o[j, at, cols] = s[:, g : g + 128] + row + col[:, cols]
            o_copy(j, q).start()
        return carry

    lax.fori_loop(0, tiles, step, 0)
    for j in range(tiles):
        wait_all([o_copy(j, q) for q in range(cuts)])


def posterior(pieces, places, targets, tile_row, column_pot, tile_tgt):
    tiles, _, depth = pieces[0].shape
    width = targets.shape[1]
    cuts = 2
    return pl.pallas_call(
        functools.partial(posterior_kernel, 2.0 / math.sqrt(depth), len(pieces)),
        in_specs=[SCALARS, SCALARS] + [ANYWHERE] * (len(pieces) + 1) + [WHOLE, WHOLE],
        out_specs=ANYWHERE,
        scratch_shapes=[
            pltpu.VMEM((tiles, width, depth), BF16),
            pltpu.VMEM((tiles, width, depth), BF16),
            pltpu.VMEM((tiles, width, width), F32),
            pltpu.SemaphoreType.DMA((tiles, PARTS, len(pieces) // PARTS)),
            pltpu.SemaphoreType.DMA((tiles,)),
            pltpu.SemaphoreType.DMA((tiles, cuts)),
        ],
        out_shape=jax.ShapeDtypeStruct((1, 1, tiles, width, width), F32),
        compiler_params=pltpu.CompilerParams(vmem_limit_bytes=54 << 20),
        cost_estimate=LIGHT,
        name="posterior",
    )(tile_tgt, places, *far([*pieces, targets]), tile_row[:, None], column_pot[:, None])


def swap(x, axis):
    return lax.all_to_all(x, axis, split_axis=0, concat_axis=0, tiled=True)


def torus_pieces(shard, side):
    half = shard.shape[0] // 2

    def shift(x, axis, by):
        def to(i):
            a, b = divmod(i, side)
            a, b = ((a + by) % side, b) if axis == 0 else (a, (b + by) % side)
            return a * side + b

        return lax.ppermute(x, "src", [(i, to(i)) for i in range(side * side)])

    pieces = []
    lines = []
    for route, part in enumerate((shard[:half], shard[half:])):
        lines.append(jnp.stack([part] + [shift(part, route, k) for k in range(1, side)]))
    back = [shift(line, 1 - route, 1) for route, line in enumerate(lines)]
    ahead = [shift(line, 1 - route, -1) for route, line in enumerate(lines)]
    mid = side // 2
    for route, line in enumerate(lines):
        far = [shift(back[route][:mid], 1 - route, 1), shift(ahead[route][mid:], 1 - route, -1)]
        pieces += [line, back[route], jnp.concatenate(far), ahead[route]]
    return pieces


def on_device(source_emb, target_emb, slot_source, slot_target):
    src_blocks, tgt_blocks = source_emb.shape[0], target_emb.shape[0]
    src_count, tgt_count = lax.axis_size("src"), lax.axis_size("tgt")
    own_row, own_col = lax.axis_index("src"), lax.axis_index("tgt")
    tiles = slot_source.shape[2]
    tile_src = slot_source[0, 0]
    tile_tgt = slot_target[0, 0] - own_col * tgt_blocks
    tile_home = tile_src // src_blocks

    cores = 2
    length = tgt_count // cores
    turns = [(far, other) for far in range(length) for other in range(cores)]

    def turned(t, far, other):
        return (t // cores + far) % length * cores + (t % cores + other) % cores

    def turn(x, far, other):
        return lax.ppermute(x, "tgt", [(t, turned(t, far, other)) for t in range(tgt_count)])

    places = jnp.stack([turned(own_col, length - far, other) for far, other in turns])

    whole_blocks = lax.all_gather(source_emb, "tgt", axis=1, tiled=True)
    side = math.isqrt(src_count)
    target_pieces = torus_pieces(target_emb, side)

    slots = jnp.concatenate([slot_source[0, 0], slot_target[0, 0]])
    slots = jnp.pad(slots, (0, 128 - 2 * tiles))[None, None]
    column_slots = swap(jnp.broadcast_to(slots, (src_count, 1, 128)), "src")[:, 0]
    row_slots = swap(jnp.broadcast_to(slots, (tgt_count, 1, 128)), "tgt")[:, 0, :tiles]
    named_src = column_slots[:, :tiles].reshape(-1) - own_row * src_blocks
    named_tgt = column_slots[:, tiles : 2 * tiles].reshape(-1) - own_col * tgt_blocks
    named = jnp.any(
        (named_src[:, None, None] == jnp.arange(src_blocks)[None, :, None])
        & (named_tgt[:, None, None] == jnp.arange(tgt_blocks)[None, None, :]),
        axis=0,
    ).astype(jnp.int32)
    plan_column = home_plan(column_slots[:, :tiles], own_row, src_blocks)

    aims = row_slots[jnp.stack([turned(own_col, far, other) for far, other in turns])]
    shards = cut(source_emb, [whole_blocks, named] + target_pieces)
    tables = [lax.all_gather(shard, "src", axis=0, tiled=True) for shard in shards]
    where = jnp.stack([own_row // side, own_row % side])
    weights, sums, targets = score_weights(whole_blocks, target_pieces, where, named, tgt_count, side, shards)
    pieces = [[None] * len(turns) for _ in range(PARTS)]
    beside = [0] + [i for i, (far, _) in enumerate(turns) if far % 2]
    across = [i for i in range(len(turns)) if i not in beside]
    stages = [(0, beside), (0, across), (1, list(range(len(turns))))]
    picked = []
    for (part, chosen), iteration in zip(stages, range(ITERS)):
        if iteration:
            sums = weighted_sums(row_kernel, gathered, weights, tgt_count, after=picked)
            sums = gate(sums, arrived)
        row_gathered = swap(sums, "tgt")
        sums = weighted_sums(column_kernel, row_gathered, weights, src_count)
        picked = list(pick(tables[part], aims[jnp.array(chosen)], row_gathered))
        arrived = [turn(x, *turns[i]) if i else x for x, i in zip(picked, chosen)]
        for x, i in zip(arrived, chosen):
            pieces[part][i] = x
        gathered = swap(sums, "src")
    pieces = pieces[0] + pieces[1]

    row_total = jnp.sum(row_gathered, axis=0)[:, 0]
    row_pot = -jnp.log(row_total)
    column_pot = -jnp.log(jnp.sum(gathered, axis=0)[:, 0])
    tile_row = jnp.take(swap(select_rows(row_pot, plan_column), "src"), tile_home, axis=0, mode="clip")

    def unfinished(carry):
        return carry[0]

    def redo(carry):
        zeros = [jnp.zeros_like(carry[1]), jnp.zeros_like(carry[3])]
        scores = posterior(pieces, places, targets, zeros[1], zeros[0], tile_tgt)[0, 0]
        potentials = log_domain(scores, tile_home, tile_tgt, plan_column, src_blocks, tgt_blocks)
        return (jnp.zeros((), jnp.bool_),) + potentials

    out_of_range = jnp.logical_not(row_total[0, 0] > 0.0)
    carry = (out_of_range, column_pot, row_pot, tile_row)
    _, column_pot, row_pot, tile_row = lax.while_loop(unfinished, redo, carry)
    log_post = posterior(pieces, places, targets, tile_row, column_pot, tile_tgt)
    return (log_post, row_pot, column_pot)


def solution(mesh):
    placed = (
        P("src", "tgt", None),
        P("tgt", "src", None),
        P("src", "tgt", None),
        P("src", "tgt", None),
    )
    return jax.shard_map(
        on_device,
        mesh=mesh,
        in_specs=placed,
        out_specs=(P("src", "tgt", None, None, None), P("src", None), P("tgt", None)),
        check_vma=False,
    )
```

time: 1410 us -> 1160 us (0.82)
  waiting for transfers between devices: 502 us -> 84.6 us
  Pallas kernels: 0 us -> 153 us
  starting transfers between devices: 52 us -> 142 us
  blocking collectives: 614 us -> 581 us
  other arithmetic: 154 us -> 131 us
  matrix products: 19.2 us -> 0 us
    all_gather x1 -> x2, waiting for transfers between devices: 414 us -> 1.5 us  [on_device(): lax.all_gather(shard, 'src', axis=0, tiled=True)]
    pallas_call x0 -> x14, Pallas kernels: none -> 153 us  [the longest x5 61 us: weighted_sums(): pl.pallas_call(kernel, in_specs=[WHOLE, ANYWHERE] + [ANYWHERE] * len(afte...]
    ppermute x0 -> x28, starting transfers between devices: none -> 50.9 us  [the longest x14 27.2 us: turn(): lax.ppermute(x, 'tgt', [(t, turned(t, far, other)) for t in range(tgt_cou...]
    all_to_all x8 -> x17, starting transfers between devices: 52 us -> 91.1 us  [swap(): return lax.all_to_all(x, axis, split_axis=0, concat_axis=0, tiled=True)]
    gather x13 -> x15, local copies, waits for them, and re-layouts: 40.6 us -> 9.08 us  [the longest x4 2.32 us: select_rows(): picked = jnp.take(table, jnp.maximum(plan, 0), axis=0, mode='clip')]
    ppermute x0 -> x28, waiting for transfers between devices: none -> 25.5 us  [the longest x14 13 us: turn(): lax.ppermute(x, 'tgt', [(t, turned(t, far, other)) for t in range(tgt_cou...]
    all_gather x1, waiting for transfers between devices: 24.2 us -> 0.01 us  [on_device(): whole_blocks = lax.all_gather(source_emb, 'tgt', axis=1, tiled=True)]
    select_n x1 -> x4, other arithmetic: 21.3 us -> 0.31 us  [select_rows(): return jnp.where(present, picked, jnp.zeros((), table.dtype))]
  transfers between devices with their start and end apart: 10 -> 48, of which waited for: 7 -> 18; matrix products, arithmetic and copies ran while one was open for 1% -> 5% of each run, Pallas kernels for 0% -> 10%
where the time goes in v2:
time: 1160 us; the launch traced here: 1150 us
  blocking collectives  581 us (50%)
  Pallas kernels  153 us (13%)
  starting transfers between devices  142 us (12%)
  other arithmetic  131 us (11%)
  waiting for transfers between devices  84.6 us (7%)
  local copies, waits for them, and re-layouts  41.8 us (4%)
  between operations  15.6 us (1%)
    pmax x3, blocking collectives, iterate(): largest = lax.pmax(local_max, 'src')  214 us
    psum x3, blocking collectives, iterate(): summed = lax.psum(local_sum * jnp.exp(local_max - largest), 'src')  209 us
    all_to_all x17, starting transfers between devices, swap(): return lax.all_to_all(x, axis, split_axis=0, concat_axis=0, tiled=True)  91.1 us
    pmax x3, blocking collectives, iterate(): largest = lax.pmax(local_max, 'tgt')  74.2 us
    psum x3, blocking collectives, iterate(): summed = lax.psum(local_sum * jnp.exp(local_max - largest), 'tgt')  70.7 us
    pallas_call x5, Pallas kernels, weighted_sums(): pl.pallas_call(kernel, in_specs=[WHOLE, ANYWHERE] + [ANYWHERE] * len(afte...  61 us
    all_to_all x17, waiting for transfers between devices, swap(): return lax.all_to_all(x, axis, split_axis=0, concat_axis=0, tiled=True)  56.2 us
    pallas_call x1, Pallas kernels, score_weights(): pl.pallas_call(functools.partial(scores_kernel, 2.0 / math.sqrt(depth) *...  40.1 us
  transfers between devices with their start and end apart: 48, of which 18 were waited for; matrix products, arithmetic and copies ran while one was open for 5% of the time, Pallas kernels for 10%

profile of v2, /device:TPU:0, one launch (start us, length us, event | category | flops | bytes accessed | tf_op | source)
XLA Modules:
  0.0 1150.1 jit_solution(11578911999903070206)
XLA Ops:
  76.2 40.1 %score_weights.1 = (bf16[4096,4096]{1,0:T(8,128)(2,1)}, f32[8,4,1,1024]{3,2,1,0:T(1,128)}, bf16[4,1024,768]{2,1,0:T(8,128)(2,1)}) custom-call(s32[4,4]{1,0:T(4,128)S(1)} %copy-done.16, s32[2]{0:T(128)S(1)} %pad_add_fusion.1.where, bf16[4,1024,768]{2,1,0:T(8,128)(2,1)} %all-gather.4.cloned.1.call-done.refs_0_.x_hbm, bf16[4,2,64,768]{3,2,1,0:T(8,128)(2,1)} %copy-done.28, ...), custom_call_target="tpu_custom_call" | custom-call | bytes 1024 | tf_op jit(solution)/shard_map/score_weights/pallas_call | solution.py:190
  137.8 12.1 %column_sums.3 = f32[16,4,1,1024]{3,2,1,0:T(1,128)S(1)} custom-call(f32[8,4,1,1024]{3,2,1,0:T(1,128)S(1)} %copy-done.4, bf16[4096,4096]{1,0:T(8,128)(2,1)} %get-tuple-element.214.k_hbm), custom_call_target="tpu_custom_call" | custom-call | bytes 1024 | tf_op jit(solution)/shard_map/column_sums/pallas_call | solution.py:269
  149.9 14.1 %all_to_all.85.g_ref = f32[16,4,1,1024]{3,2,1,0:T(1,128)S(1)} all-to-all(f32[16,4,1,1024]{3,2,1,0:T(1,128)S(1)} %column_sums.3), channel_id=1, replica_groups=mesh['src'=16,'tgt'=8] {'src'}, dimensions={0} | all-to-all | bytes 524288 | tf_op jit(solution)/shard_map/all_to_all | solution.py:427
  164.0 12.4 %row_sums.2.x_ref = f32[8,4,1,1024]{3,2,1,0:T(1,128)S(1)} custom-call(f32[16,4,1,1024]{3,2,1,0:T(1,128)S(1)} %all_to_all.85.g_ref, bf16[4096,4096]{1,0:T(8,128)(2,1)} %get-tuple-element.214.k_hbm, bf16[6,64,768]{2,1,0:T(8,128)(2,1)} %get-tuple-element.445.refs_0_, bf16[6,64,768]{2,1,0:T(8,128)(2,1)} %copy-done.13, bf16[6,64,768]{2,1,0:T(8,128)(2,1)} %copy-done.12, ...), custom_call_target="tpu_custom_call" | custom-call | bytes 1024 | tf_op jit(solution)/shard_map/row_sums/pallas_call | solution.py:269
  194.2 14.2 %collective-permute-start.20 = (bf16[6,64,768]{2,1,0:T(8,128)(2,1)S(1)}, bf16[6,64,768]{2,1,0:T(8,128)(2,1)}, u32[]{:S(2)}, u32[]{:S(2)}) collective-permute-start(bf16[6,64,768]{2,1,0:T(8,128)(2,1)S(1)} %get-tuple-element.221.refs_2_), channel_id=1, source_target_pairs={{0,5},{1,4},{2,7},{3,6},{4,1},{5,0},{6,3},{7,2},{8,13},{9,12},{10,... | collective-permute-start | bytes 1769480 | tf_op jit(solution)/shard_map/ppermute | solution.py:471
  209.3 12.3 %column_sums.4 = f32[16,4,1,1024]{3,2,1,0:T(1,128)} custom-call(f32[8,4,1,1024]{3,2,1,0:T(1,128)S(1)} %copy-done.6, bf16[4096,4096]{1,0:T(8,128)(2,1)} %get-tuple-element.214.k_hbm), custom_call_target="tpu_custom_call" | custom-call | bytes 1024 | tf_op jit(solution)/shard_map/column_sums/pallas_call | solution.py:269
  234.8 12.0 %row_sums.3.x_ref = f32[8,4,1,1024]{3,2,1,0:T(1,128)S(1)} custom-call(f32[16,4,1,1024]{3,2,1,0:T(1,128)S(1)} %all-to-all-done.8.g_ref, bf16[4096,4096]{1,0:T(8,128)(2,1)} %get-tuple-element.214.k_hbm, bf16[6,64,768]{2,1,0:T(8,128)(2,1)} %copy-done.9, bf16[6,64,768]{2,1,0:T(8,128)(2,1)} %copy-done.8, bf16[6,64,768]{2,1,0:T(8,128)(2,1)} %copy-done.7), custom_call_target="tpu_custom_call" | custom-call | bytes 1024 | tf_op jit(solution)/shard_map/row_sums/pallas_call | solution.py:269
  286.8 12.3 %column_sums.5 = f32[16,4,1,1024]{3,2,1,0:T(1,128)} custom-call(f32[8,4,1,1024]{3,2,1,0:T(1,128)S(1)} %copy-done.2, bf16[4096,4096]{1,0:T(8,128)(2,1)} %get-tuple-element.214.k_hbm), custom_call_target="tpu_custom_call" | custom-call | bytes 1024 | tf_op jit(solution)/shard_map/column_sums/pallas_call | solution.py:269
  320.3 801.2 %while.28 = (pred[]{:T(512)}, f32[4,1024]{1,0:T(4,128)}, f32[4,1024]{1,0:T(4,128)}, f32[6,1024]{1,0:T(8,128)}, s32[6]{0:T(128)S(1)}, /*index=5*/s32[8]{0:T(128)S...) while((pred[]{:T(512)}, f32[4,1024]{1,0:T(4,128)}, ...), condition=%region_22.23_spmd, body=%region_5.22_spmd | while | flops 64245064 | bytes 104062064 | solution.py:531
  321.7 19.0 %posterior.2 = f32[1,1,6,1024,1024]{4,3,2,1,0:T(8,128)} custom-call(s32[6]{0:T(128)S(1)} %get-tuple-element.493.tile_tgt, s32[8]{0:T(128)S(1)} %get-tuple-element.494.places, bf16[6,64,768]{2,1,0:T(8,128)(2,1)} %get-tuple-element.495.refs_0_, bf16[6,64,768]{2,1,0:T(8,128)(2,1)} %get-tuple-element.496.refs_1_, ...), custom_call_target="tpu_custom_call" | custom-call | bytes 1024 | tf_op jit(solution)/shard_map/while/body/posterior/pallas_call | solution.py:407
  340.8 780.1 %while.30 = (s32[]{:T(128)}, f32[4,1024]{1,0:T(4,128)S(1)}, f32[4,1024]{1,0:T(4,128)}, f32[6,1024]{1,0:T(8,128)}, s32[6]{0:T(128)S(1)}, /*index=5*/s32[6]{0:T(12...) while((s32[]{:T(128)}, f32[4,1024]{1,0:T(4,128)S(1)}, ...), condition=%wide.region_21.21_spmd.clone, body=%wide.region_6.20_spmd.clone.sunk | while | flops 64245064 | bytes 103953936 | solution.py:70
  355.7 10.9 exponential_reduce_fusion.4
  375.0 26.5 %pmax.20 = f32[4,1024]{1,0:T(4,128)S(1)} all-reduce(f32[4,1024]{1,0:T(4,128)S(1)} %select_reduce_fusion.13), channel_id=1, replica_groups=mesh['src'=16,'tgt'=8] {'tgt'}, use_global_device_ids=true, to_apply=%region_10.9 | all-reduce | flops 4096 | bytes 32768 | tf_op jit(solution)/shard_map/while/body/while/body/eval_jaxpr/pmax | solution.py:53
  401.7 23.6 %psum.20 = f32[4,1024]{1,0:T(4,128)S(1)} all-reduce(f32[4,1024]{1,0:T(4,128)S(1)} %exponential_multiply_fusion.4), channel_id=1, replica_groups=mesh['src'=16,'tgt'=8] {'tgt'}, use_global_device_ids=true, to_apply=%region_14.13 | all-reduce | flops 4096 | bytes 32768 | tf_op jit(solution)/shard_map/while/body/while/body/eval_jaxpr/psum | solution.py:54
  441.6 9.4 add_reduce_fusion.5
  451.1 10.6 exponential_reduce_fusion.5
  461.8 71.2 %pmax.21 = f32[4,1024]{1,0:T(4,128)S(1)} all-reduce(f32[4,1024]{1,0:T(4,128)S(1)} %select_reduce_fusion.16), channel_id=1, replica_groups=mesh['src'=16,'tgt'=8] {'src'}, use_global_device_ids=true, to_apply=%region_17.16 | all-reduce | flops 4096 | bytes 32768 | tf_op jit(solution)/shard_map/while/body/while/body/eval_jaxpr/pmax | solution.py:61
  533.1 69.6 %psum.21 = f32[4,1024]{1,0:T(4,128)S(1)} all-reduce(f32[4,1024]{1,0:T(4,128)S(1)} %exponential_multiply_fusion.5), channel_id=1, replica_groups=mesh['src'=16,'tgt'=8] {'src'}, use_global_device_ids=true, to_apply=%region_20.19 | all-reduce | flops 4096 | bytes 32768 | tf_op jit(solution)/shard_map/while/body/while/body/eval_jaxpr/psum | solution.py:62
  617.2 10.9 exponential_reduce_fusion.4
  636.4 23.9 %pmax.20 = f32[4,1024]{1,0:T(4,128)S(1)} all-reduce(f32[4,1024]{1,0:T(4,128)S(1)} %select_reduce_fusion.13), channel_id=1, replica_groups=mesh['src'=16,'tgt'=8] {'tgt'}, use_global_device_ids=true, to_apply=%region_10.9 | all-reduce | flops 4096 | bytes 32768 | tf_op jit(solution)/shard_map/while/body/while/body/eval_jaxpr/pmax | solution.py:53
  660.5 23.6 %psum.20 = f32[4,1024]{1,0:T(4,128)S(1)} all-reduce(f32[4,1024]{1,0:T(4,128)S(1)} %exponential_multiply_fusion.4), channel_id=1, replica_groups=mesh['src'=16,'tgt'=8] {'tgt'}, use_global_device_ids=true, to_apply=%region_14.13 | all-reduce | flops 4096 | bytes 32768 | tf_op jit(solution)/shard_map/while/body/while/body/eval_jaxpr/psum | solution.py:54
  700.7 9.4 add_reduce_fusion.5
  710.1 10.6 exponential_reduce_fusion.5
  720.9 71.2 %pmax.21 = f32[4,1024]{1,0:T(4,128)S(1)} all-reduce(f32[4,1024]{1,0:T(4,128)S(1)} %select_reduce_fusion.16), channel_id=1, replica_groups=mesh['src'=16,'tgt'=8] {'src'}, use_global_device_ids=true, to_apply=%region_17.16 | all-reduce | flops 4096 | bytes 32768 | tf_op jit(solution)/shard_map/while/body/while/body/eval_jaxpr/pmax | solution.py:61
  792.2 69.6 %psum.21 = f32[4,1024]{1,0:T(4,128)S(1)} all-reduce(f32[4,1024]{1,0:T(4,128)S(1)} %exponential_multiply_fusion.5), channel_id=1, replica_groups=mesh['src'=16,'tgt'=8] {'src'}, use_global_device_ids=true, to_apply=%region_20.19 | all-reduce | flops 4096 | bytes 32768 | tf_op jit(solution)/shard_map/while/body/while/body/eval_jaxpr/psum | solution.py:62
  876.2 10.9 exponential_reduce_fusion.4
  895.5 23.9 %pmax.20 = f32[4,1024]{1,0:T(4,128)S(1)} all-reduce(f32[4,1024]{1,0:T(4,128)S(1)} %select_reduce_fusion.13), channel_id=1, replica_groups=mesh['src'=16,'tgt'=8] {'tgt'}, use_global_device_ids=true, to_apply=%region_10.9 | all-reduce | flops 4096 | bytes 32768 | tf_op jit(solution)/shard_map/while/body/while/body/eval_jaxpr/pmax | solution.py:53
  919.6 23.6 %psum.20 = f32[4,1024]{1,0:T(4,128)S(1)} all-reduce(f32[4,1024]{1,0:T(4,128)S(1)} %exponential_multiply_fusion.4), channel_id=1, replica_groups=mesh['src'=16,'tgt'=8] {'tgt'}, use_global_device_ids=true, to_apply=%region_14.13 | all-reduce | flops 4096 | bytes 32768 | tf_op jit(solution)/shard_map/while/body/while/body/eval_jaxpr/psum | solution.py:54
  969.2 10.6 exponential_reduce_fusion.5
  979.9 71.2 %pmax.21 = f32[4,1024]{1,0:T(4,128)S(1)} all-reduce(f32[4,1024]{1,0:T(4,128)S(1)} %select_reduce_fusion.16), channel_id=1, replica_groups=mesh['src'=16,'tgt'=8] {'src'}, use_global_device_ids=true, to_apply=%region_17.16 | all-reduce | flops 4096 | bytes 32768 | tf_op jit(solution)/shard_map/while/body/while/body/eval_jaxpr/pmax | solution.py:61
  1051.3 69.6 %psum.21 = f32[4,1024]{1,0:T(4,128)S(1)} all-reduce(f32[4,1024]{1,0:T(4,128)S(1)} %exponential_multiply_fusion.5), channel_id=1, replica_groups=mesh['src'=16,'tgt'=8] {'src'}, use_global_device_ids=true, to_apply=%region_20.19 | all-reduce | flops 4096 | bytes 32768 | tf_op jit(solution)/shard_map/while/body/while/body/eval_jaxpr/psum | solution.py:62
  1124.1 19.0 %posterior.3 = f32[1,1,6,1024,1024]{4,3,2,1,0:T(8,128)} custom-call(s32[6]{0:T(128)S(1)} %get-tuple-element.604, s32[8]{0:T(128)S(1)} %get-tuple-element.602, bf16[6,64,768]{2,1,0:T(8,128)(2,1)} %get-tuple-element.539, bf16[6,64,768]{2,1,0:T(8,128)(2,1)} %get-tuple-element.549, bf16[6,64,768]{2,1,0:T(8,128)(2,1)} %get-tuple-element.541, ...), custom_call_target="tpu_custom_call" | custom-call | bytes 1024 | tf_op jit(solution)/shard_map/posterior/pallas_call | solution.py:407
  (358 shorter events, 315.4 us)
Async XLA Ops:
  7.2 58.0 %all-gather.4.cloned.1.call-start = ((), (), s32[]{:S(2)}) async-start(), calls=%async_computation.12 | async-start | bytes 7077888 | tf_op jit(solution)/shard_map/all_gather | solution.py:475
  22.6 21.5 %collective-permute-start.10 = (bf16[4,2,64,768]{3,2,1,0:T(8,128)(2,1)S(1)}, bf16[4,2,64,768]{3,2,1,0:T(8,128)(2,1)S(1)}, u32[]{:S(2)}, u32[]{:S(2)}) collective-permute-start(bf16[4,2,64,768]{3,2,1,0:T(8,128)(2,1)S(1)} %pad_maximum_fusion.1.refs_6_.refs_4_), channel_id=1, source_target_pairs={{0,32},{8,40},{16,48},{24,56},{32,64},{40,72},{48,80},{56,88},{64,... | collective-permute-start | bytes 2359304 | tf_op jit(solution)/shard_map/ppermute | solution.py:439
  24.1 25.3 %collective-permute-start.12 = (bf16[4,2,64,768]{3,2,1,0:T(8,128)(2,1)S(1)}, bf16[4,2,64,768]{3,2,1,0:T(8,128)(2,1)S(1)}, u32[]{:S(2)}, u32[]{:S(2)}) collective-permute-start(bf16[4,2,64,768]{3,2,1,0:T(8,128)(2,1)S(1)} %pad_maximum_fusion.1.refs_6_.refs_4_), channel_id=1, source_target_pairs={{0,96},{8,104},{16,112},{24,120},{32,0},{40,8},{48,16},{56,24},{64... | collective-permute-start | bytes 2359304 | tf_op jit(solution)/shard_map/ppermute | solution.py:439
  28.2 23.3 %collective-permute-start.3 = (bf16[4,2,64,768]{3,2,1,0:T(8,128)(2,1)S(1)}, bf16[4,2,64,768]{3,2,1,0:T(8,128)(2,1)}, u32[]{:S(2)}, u32[]{:S(2)}) collective-permute-start(bf16[4,2,64,768]{3,2,1,0:T(8,128)(2,1)S(1)} %pad_maximum_fusion.refs_2_.refs_0_), channel_id=1, source_target_pairs={{0,8},{8,16},{16,24},{24,0},{32,40},{40,48},{48,56},{56,32},{64,72... | collective-permute-start | bytes 2359304 | tf_op jit(solution)/shard_map/ppermute | solution.py:439
  28.3 25.1 %collective-permute-start.5 = (bf16[4,2,64,768]{3,2,1,0:T(8,128)(2,1)S(1)}, bf16[4,2,64,768]{3,2,1,0:T(8,128)(2,1)}, u32[]{:S(2)}, u32[]{:S(2)}) collective-permute-start(bf16[4,2,64,768]{3,2,1,0:T(8,128)(2,1)S(1)} %pad_maximum_fusion.refs_2_.refs_0_), channel_id=1, source_target_pairs={{0,24},{8,0},{16,8},{24,16},{32,56},{40,32},{48,40},{56,48},{64,88... | collective-permute-start | bytes 2359304 | tf_op jit(solution)/shard_map/ppermute | solution.py:439
  39.8 88.9 %all-gather.6.cloned.1.call-start = ((), (), s32[]{:S(2)}) async-start(), calls=%async_computation.13 | async-start | bytes 6684672 | tf_op jit(solution)/shard_map/all_gather | solution.py:494
  67.3 186.2 %all-gather.8.cloned.1.call-start = ((), (), s32[]{:S(2)}) async-start(), calls=%async_computation.14 | async-start | bytes 6684672 | tf_op jit(solution)/shard_map/all_gather | solution.py:494
  70.1 46.2 %all-to-all-start.3 = ((s32[8,1,128]{2,1,0:T(1,128)}), s32[8,1,128]{2,1,0:T(1,128)S(1)}, u32[]{:S(2)}, u32[]{:S(2)}) async-start(s32[8,1,128]{2,1,0:T(1,128)} %broadcast_in_dim.274), calls=%async_computation.3 | async-start | bytes 8192 | tf_op jit(solution)/shard_map/all_to_all | solution.py:427
  131.9 45.2 %collective-permute-start.14 = (bf16[6,64,768]{2,1,0:T(8,128)(2,1)S(1)}, bf16[6,64,768]{2,1,0:T(8,128)(2,1)S(1)}, u32[]{:S(2)}, u32[]{:S(2)}) collective-permute-start(bf16[6,64,768]{2,1,0:T(8,128)(2,1)S(1)} %get-tuple-element.215.refs_1_), channel_id=1, source_target_pairs={{0,2},{1,3},{2,4},{3,5},{4,6},{5,7},{6,0},{7,1},{8,10},{9,11},{10,... | collective-permute-start | bytes 1769480 | tf_op jit(solution)/shard_map/ppermute | solution.py:471
  133.3 43.8 %collective-permute-start.15 = (bf16[6,64,768]{2,1,0:T(8,128)(2,1)S(1)}, bf16[6,64,768]{2,1,0:T(8,128)(2,1)S(1)}, u32[]{:S(2)}, u32[]{:S(2)}) collective-permute-start(bf16[6,64,768]{2,1,0:T(8,128)(2,1)S(1)} %get-tuple-element.216.refs_2_), channel_id=1, source_target_pairs={{0,3},{1,2},{2,5},{3,4},{4,7},{5,6},{6,1},{7,0},{8,11},{9,10},{10,... | collective-permute-start | bytes 1769480 | tf_op jit(solution)/shard_map/ppermute | solution.py:471
  134.2 43.0 %collective-permute-start.16 = (bf16[6,64,768]{2,1,0:T(8,128)(2,1)S(1)}, bf16[6,64,768]{2,1,0:T(8,128)(2,1)S(1)}, u32[]{:S(2)}, u32[]{:S(2)}) collective-permute-start(bf16[6,64,768]{2,1,0:T(8,128)(2,1)S(1)} %get-tuple-element.217.refs_3_), channel_id=1, source_target_pairs={{0,6},{1,7},{2,0},{3,1},{4,2},{5,3},{6,4},{7,5},{8,14},{9,15},{10,... | collective-permute-start | bytes 1769480 | tf_op jit(solution)/shard_map/ppermute | solution.py:471
  135.8 41.3 %collective-permute-start.17 = (bf16[6,64,768]{2,1,0:T(8,128)(2,1)S(1)}, bf16[6,64,768]{2,1,0:T(8,128)(2,1)S(1)}, u32[]{:S(2)}, u32[]{:S(2)}) collective-permute-start(bf16[6,64,768]{2,1,0:T(8,128)(2,1)S(1)} %get-tuple-element.218.refs_4_), channel_id=1, source_target_pairs={{0,7},{1,6},{2,1},{3,0},{4,3},{5,2},{6,5},{7,4},{8,15},{9,14},{10,... | collective-permute-start | bytes 1769480 | tf_op jit(solution)/shard_map/ppermute | solution.py:471
  193.2 54.2 %collective-permute-start.18 = (bf16[6,64,768]{2,1,0:T(8,128)(2,1)S(1)}, bf16[6,64,768]{2,1,0:T(8,128)(2,1)S(1)}, u32[]{:S(2)}, u32[]{:S(2)}) collective-permute-start(bf16[6,64,768]{2,1,0:T(8,128)(2,1)S(1)} %get-tuple-element.219.refs_0_), channel_id=1, source_target_pairs={{0,1},{1,0},{2,3},{3,2},{4,5},{5,4},{6,7},{7,6},{8,9},{9,8},{10,11... | collective-permute-start | bytes 1769480 | tf_op jit(solution)/shard_map/ppermute | solution.py:471
  193.3 54.1 %collective-permute-start.19 = (bf16[6,64,768]{2,1,0:T(8,128)(2,1)S(1)}, bf16[6,64,768]{2,1,0:T(8,128)(2,1)S(1)}, u32[]{:S(2)}, u32[]{:S(2)}) collective-permute-start(bf16[6,64,768]{2,1,0:T(8,128)(2,1)S(1)} %get-tuple-element.220.refs_1_), channel_id=1, source_target_pairs={{0,4},{1,5},{2,6},{3,7},{4,0},{5,1},{6,2},{7,3},{8,12},{9,13},{10,... | collective-permute-start | bytes 1769480 | tf_op jit(solution)/shard_map/ppermute | solution.py:471
  194.2 53.2 %collective-permute-start.20 = (bf16[6,64,768]{2,1,0:T(8,128)(2,1)S(1)}, bf16[6,64,768]{2,1,0:T(8,128)(2,1)}, u32[]{:S(2)}, u32[]{:S(2)}) collective-permute-start(bf16[6,64,768]{2,1,0:T(8,128)(2,1)S(1)} %get-tuple-element.221.refs_2_), channel_id=1, source_target_pairs={{0,5},{1,4},{2,7},{3,6},{4,1},{5,0},{6,3},{7,2},{8,13},{9,12},{10,... | collective-permute-start | bytes 1769480 | tf_op jit(solution)/shard_map/ppermute | solution.py:471
  264.6 17.7 %collective-permute-start.22 = (bf16[6,64,768]{2,1,0:T(8,128)(2,1)}, bf16[6,64,768]{2,1,0:T(8,128)(2,1)}, u32[]{:S(2)}, u32[]{:S(2)}) collective-permute-start(bf16[6,64,768]{2,1,0:T(8,128)(2,1)} %get-tuple-element.224), channel_id=1, source_target_pairs={{0,2},{1,3},{2,4},{3,5},{4,6},{5,7},{6,0},{7,1},{8,10},{9,11},{10,... | collective-permute-start | bytes 1769480 | tf_op jit(solution)/shard_map/ppermute | solution.py:471
  265.3 54.0 %collective-permute-start.23 = (bf16[6,64,768]{2,1,0:T(8,128)(2,1)S(1)}, bf16[6,64,768]{2,1,0:T(8,128)(2,1)}, u32[]{:S(2)}, u32[]{:S(2)}) collective-permute-start(bf16[6,64,768]{2,1,0:T(8,128)(2,1)S(1)} %get-tuple-element.225), channel_id=1, source_target_pairs={{0,3},{1,2},{2,5},{3,4},{4,7},{5,6},{6,1},{7,0},{8,11},{9,10},{10,... | collective-permute-start | bytes 1769480 | tf_op jit(solution)/shard_map/ppermute | solution.py:471
  265.4 53.9 %collective-permute-start.24 = (bf16[6,64,768]{2,1,0:T(8,128)(2,1)S(1)}, bf16[6,64,768]{2,1,0:T(8,128)(2,1)}, u32[]{:S(2)}, u32[]{:S(2)}) collective-permute-start(bf16[6,64,768]{2,1,0:T(8,128)(2,1)S(1)} %get-tuple-element.226), channel_id=1, source_target_pairs={{0,4},{1,5},{2,6},{3,7},{4,0},{5,1},{6,2},{7,3},{8,12},{9,13},{10,... | collective-permute-start | bytes 1769480 | tf_op jit(solution)/shard_map/ppermute | solution.py:471
  269.2 50.1 %collective-permute-start.25 = (bf16[6,64,768]{2,1,0:T(8,128)(2,1)S(1)}, bf16[6,64,768]{2,1,0:T(8,128)(2,1)}, u32[]{:S(2)}, u32[]{:S(2)}) collective-permute-start(bf16[6,64,768]{2,1,0:T(8,128)(2,1)S(1)} %get-tuple-element.227), channel_id=1, source_target_pairs={{0,5},{1,4},{2,7},{3,6},{4,1},{5,0},{6,3},{7,2},{8,13},{9,12},{10,... | collective-permute-start | bytes 1769480 | tf_op jit(solution)/shard_map/ppermute | solution.py:471
  271.6 47.7 %collective-permute-start.26 = (bf16[6,64,768]{2,1,0:T(8,128)(2,1)S(1)}, bf16[6,64,768]{2,1,0:T(8,128)(2,1)}, u32[]{:S(2)}, u32[]{:S(2)}) collective-permute-start(bf16[6,64,768]{2,1,0:T(8,128)(2,1)S(1)} %get-tuple-element.228), channel_id=1, source_target_pairs={{0,6},{1,7},{2,0},{3,1},{4,2},{5,3},{6,4},{7,5},{8,14},{9,15},{10,... | collective-permute-start | bytes 1769480 | tf_op jit(solution)/shard_map/ppermute | solution.py:471
  282.3 37.9 %collective-permute-start.27 = (bf16[6,64,768]{2,1,0:T(8,128)(2,1)S(1)}, bf16[6,64,768]{2,1,0:T(8,128)(2,1)}, u32[]{:S(2)}, u32[]{:S(2)}) collective-permute-start(bf16[6,64,768]{2,1,0:T(8,128)(2,1)S(1)} %get-tuple-element.229), channel_id=1, source_target_pairs={{0,7},{1,6},{2,1},{3,0},{4,3},{5,2},{6,5},{7,4},{8,15},{9,14},{10,... | collective-permute-start | bytes 1769480 | tf_op jit(solution)/shard_map/ppermute | solution.py:471
  282.3 16.8 %all-to-all-start.11 = ((f32[16,1,1024]{2,1,0:T(1,128)}), f32[16,1,1024]{2,1,0:T(1,128)S(1)}, u32[]{:S(2)}, u32[]{:S(2)}) async-start(f32[16,1,1024]{2,1,0:T(1,128)} %copy.17), calls=%async_computation.11 | async-start | bytes 131072 | tf_op jit(solution)/shard_map/all_to_all | solution.py:427
  299.1 15.7 %all-to-all-start.10 = ((f32[16,4,1,1024]{3,2,1,0:T(1,128)}), f32[16,4,1,1024]{3,2,1,0:T(1,128)S(1)}, u32[]{:S(2)}, u32[]{:S(2)}) async-start(f32[16,4,1,1024]{3,2,1,0:T(1,128)} %column_sums.5), calls=%async_computation.10 | async-start | bytes 524288 | tf_op jit(solution)/shard_map/all_to_all | solution.py:427
  351.7 15.9 %all-to-all-start = ((f32[16,1,1024]{2,1,0:T(1,128)}), f32[16,1,1024]{2,1,0:T(1,128)S(1)}, u32[]{:S(2)}, u32[]{:S(2)}) async-start(f32[16,1,1024]{2,1,0:T(1,128)} %copy.36), calls=%async_computation | async-start | bytes 131072 | tf_op jit(solution)/shard_map/while/body/while/body/eval_jaxpr/all_to_all | solution.py:427
  367.6 33.9 %all-to-all-start.1 = ((f32[16,1,1024]{2,1,0:T(1,128)}), f32[16,1,1024]{2,1,0:T(1,128)S(1)}, u32[]{:S(2)}, u32[]{:S(2)}) async-start(f32[16,1,1024]{2,1,0:T(1,128)} %copy.38), calls=%async_computation.1 | async-start | bytes 131072 | tf_op jit(solution)/shard_map/while/body/while/body/eval_jaxpr/all_to_all | solution.py:427
  426.7 14.3 %all-to-all-start.2 = ((f32[16,1,1024]{2,1,0:T(1,128)}), f32[16,1,1024]{2,1,0:T(1,128)S(1)}, u32[]{:S(2)}, u32[]{:S(2)}) async-start(f32[16,1,1024]{2,1,0:T(1,128)} %copy.40), calls=%async_computation.2 | async-start | bytes 131072 | tf_op jit(solution)/shard_map/while/body/while/body/eval_jaxpr/all_to_all | solution.py:427
  613.7 15.4 %all-to-all-start = ((f32[16,1,1024]{2,1,0:T(1,128)}), f32[16,1,1024]{2,1,0:T(1,128)S(1)}, u32[]{:S(2)}, u32[]{:S(2)}) async-start(f32[16,1,1024]{2,1,0:T(1,128)} %copy.36), calls=%async_computation | async-start | bytes 131072 | tf_op jit(solution)/shard_map/while/body/while/body/eval_jaxpr/all_to_all | solution.py:427
  629.1 31.2 %all-to-all-start.1 = ((f32[16,1,1024]{2,1,0:T(1,128)}), f32[16,1,1024]{2,1,0:T(1,128)S(1)}, u32[]{:S(2)}, u32[]{:S(2)}) async-start(f32[16,1,1024]{2,1,0:T(1,128)} %copy.38), calls=%async_computation.1 | async-start | bytes 131072 | tf_op jit(solution)/shard_map/while/body/while/body/eval_jaxpr/all_to_all | solution.py:427
  685.4 14.6 %all-to-all-start.2 = ((f32[16,1,1024]{2,1,0:T(1,128)}), f32[16,1,1024]{2,1,0:T(1,128)S(1)}, u32[]{:S(2)}, u32[]{:S(2)}) async-start(f32[16,1,1024]{2,1,0:T(1,128)} %copy.40), calls=%async_computation.2 | async-start | bytes 131072 | tf_op jit(solution)/shard_map/while/body/while/body/eval_jaxpr/all_to_all | solution.py:427
  872.7 15.4 %all-to-all-start = ((f32[16,1,1024]{2,1,0:T(1,128)}), f32[16,1,1024]{2,1,0:T(1,128)S(1)}, u32[]{:S(2)}, u32[]{:S(2)}) async-start(f32[16,1,1024]{2,1,0:T(1,128)} %copy.36), calls=%async_computation | async-start | bytes 131072 | tf_op jit(solution)/shard_map/while/body/while/body/eval_jaxpr/all_to_all | solution.py:427
  888.2 31.2 %all-to-all-start.1 = ((f32[16,1,1024]{2,1,0:T(1,128)}), f32[16,1,1024]{2,1,0:T(1,128)S(1)}, u32[]{:S(2)}, u32[]{:S(2)}) async-start(f32[16,1,1024]{2,1,0:T(1,128)} %copy.38), calls=%async_computation.1 | async-start | bytes 131072 | tf_op jit(solution)/shard_map/while/body/while/body/eval_jaxpr/all_to_all | solution.py:427
  944.5 14.6 %all-to-all-start.2 = ((f32[16,1,1024]{2,1,0:T(1,128)}), f32[16,1,1024]{2,1,0:T(1,128)S(1)}, u32[]{:S(2)}, u32[]{:S(2)}) async-start(f32[16,1,1024]{2,1,0:T(1,128)} %copy.40), calls=%async_computation.2 | async-start | bytes 131072 | tf_op jit(solution)/shard_map/while/body/while/body/eval_jaxpr/all_to_all | solution.py:427
  (59 other events, 1082.7 us)
Sparse Core Ops, SparseCore 0:
  9.7 43.5 all-gather.3
  67.4 61.3 all-gather.5
  130.9 60.8 all-gather.7

commit v3 on v2

--- a/solution.py
+++ b/solution.py
@@ -13,7 +13,8 @@
 F32, BF16 = jnp.float32, jnp.bfloat16
 LIMIT = 20.0
 ROWS = 512
-PARTS = 2
+BLOCKS = 4
+PARTS = (64, 64)
 LIGHT = pl.CostEstimate(flops=0, bytes_accessed=1024, transcendentals=0)
 NT = (((1,), (1,)), ((), ()))
 
@@ -88,6 +89,10 @@
     o_ref[:, block, :, cols] = jnp.broadcast_to(out[None], (o_ref.shape[0],) + out.shape)
 
 
+def all_within(x, low, high):
+    return jnp.min(jnp.where((x >= low) & (x <= high), 1.0, 0.0)) > 0.0
+
+
 def start_all(copies):
     for copy in copies:
         copy.start()
@@ -98,20 +103,24 @@
         copy.wait()
 
 
-def scores_kernel(scale, side, named, where, x_hbm, *refs):
-    pieces, refs = refs[:8], refs[-11:]
+def scores_kernel(scale, side, named, where, extra, x_hbm, *refs):
+    pieces, refs = refs[:10], refs[-11:]
     k_hbm, sum_ref, targets_hbm, x, y, k_out, lowest, x_sem, y_sem, k_sem, leave = refs
     blocks, width, _ = y.shape
     rows = k_out.shape[1]
     half = blocks // 2
+    mid = side // 2
     small = width // (side * side)
 
     def target_copy(route, far, near):
         first = lax.rem(where[route] - near + side, side)
         second = lax.rem(where[1 - route] - far + side, side)
         at = (first * side + second if route == 0 else second * side + first) * small
+        stage, entry = far, near
+        if far >= mid:
+            stage, entry = (far, near) if far == mid and near < mid else (far + 1, near - mid if far == mid else near)
         return pltpu.make_async_copy(
-            pieces[route * side + far].at[near],
+            pieces[route * (side + 1) + stage].at[entry],
             y.at[pl.ds(route * half, half), pl.ds(pl.multiple_of(at, small), small), :],
             y_sem.at[route, far, near],
         )
@@ -131,6 +140,7 @@
     start_all(target_copies(1))
     start_all([source_copy(b) for b in range(1, blocks)])
     lowest[...] = jnp.ones_like(lowest)
+    put(sum_ref, blocks, slice(None), extra[...])
     wait_all(target_copies(0) + target_copies(1))
     whole_targets = pltpu.make_async_copy(y, targets_hbm, leave)
     whole_targets.start()
@@ -165,7 +175,7 @@
         lowest[...] = low
         out_copy(i, slot).start()
         total = lane_totals(lanes)
-        fine = (jnp.min(low.astype(F32)) > math.exp(-LIMIT)) & (jnp.max(total) < math.exp(LIMIT))
+        fine = (jnp.min(low.astype(F32)) > math.exp(-LIMIT)) & all_within(total, 0.0, math.exp(LIMIT))
         put(sum_ref, b, pl.ds(pl.multiple_of(part * rows, rows), rows), jnp.where(fine, total, jnp.nan))
         return carry
 
@@ -184,12 +194,12 @@
     return [pltpu.with_memory_space_constraint(x, pltpu.HBM) for x in arrays]
 
 
-def score_weights(x, pieces, where, named, copies, side, after):
+def score_weights(x, pieces, where, named, extra, copies, side, after):
     blocks, width, depth = x.shape
     n = blocks * width
     return pl.pallas_call(
         functools.partial(scores_kernel, 2.0 / math.sqrt(depth) * math.log2(math.e), side),
-        in_specs=[SCALARS, SCALARS] + [ANYWHERE] * (9 + len(after)),
+        in_specs=[SCALARS, SCALARS, WHOLE] + [ANYWHERE] * (1 + len(pieces) + len(after)),
         out_specs=[ANYWHERE, WHOLE, ANYWHERE],
         scratch_shapes=[
             pltpu.VMEM((blocks, width, depth), BF16),
@@ -203,23 +213,35 @@
         ],
         out_shape=[
             jax.ShapeDtypeStruct((n, n), BF16),
-            jax.ShapeDtypeStruct((copies, blocks, 1, width), F32),
+            jax.ShapeDtypeStruct((copies, blocks + 1, 1, width), F32),
             jax.ShapeDtypeStruct((blocks, width, depth), BF16),
         ],
         compiler_params=pltpu.CompilerParams(vmem_limit_bytes=44 << 20),
         cost_estimate=LIGHT,
         name="score_weights",
-    )(named, where, *far([x, *pieces, *after]))
+    )(named, where, extra, *far([x, *pieces, *after]))
 
 
 def inverse_parts(g_ref, low, high):
-    total = jnp.sum(g_ref[...], axis=0)
-    fine = (jnp.min(total) >= low) & (jnp.max(total) <= high)
+    total = jnp.sum(g_ref[:, :BLOCKS], axis=0)
+    fine = all_within(total, low, high)
     return [1.0 / total[b] for b in range(total.shape[0])], jnp.where(fine, 0.0, jnp.nan)
 
 
 def column_kernel(g_ref, k_hbm, *refs):
-    o_ref, k, sem = refs[-3:]
+    columns(g_ref, k_hbm, *refs[-3:])
+
+
+def last_column_kernel(g_ref, k_hbm, plan, *refs):
+    o_ref, k, sem, logs = refs[-4:]
+    total = jnp.sum(g_ref[:, :BLOCKS], axis=0)
+    logs[...] = -jnp.log(total)
+    for s in range(o_ref.shape[0]):
+        o_ref[s, total.shape[0]] = logs[jnp.maximum(plan[s], 0)]
+    columns(g_ref, k_hbm, o_ref, k, sem)
+
+
+def columns(g_ref, k_hbm, o_ref, k, sem):
     parts, n, cols = k.shape
     copies = [pltpu.make_async_copy(k_hbm.at[:, pl.ds(j * cols, cols)], k.at[j], sem.at[j]) for j in range(parts)]
     start_all(copies)
@@ -264,34 +286,38 @@
 
 def weighted_sums(kernel, gathered, k, copies, after=()):
     n = k.shape[0]
+    blocks, width = BLOCKS, gathered.shape[3]
     parts = n // ROWS
-    shape = (parts, n, ROWS) if kernel is column_kernel else (parts, ROWS, n)
+    last = kernel is last_column_kernel
+    shape = (parts, ROWS, n) if kernel is row_kernel else (parts, n, ROWS)
     return pl.pallas_call(
         kernel,
-        in_specs=[WHOLE, ANYWHERE] + [ANYWHERE] * len(after),
+        in_specs=[WHOLE, ANYWHERE] + [SCALARS] * last + [ANYWHERE] * (len(after) - last),
         out_specs=WHOLE,
-        out_shape=jax.ShapeDtypeStruct((copies,) + gathered.shape[1:], F32),
-        scratch_shapes=[pltpu.VMEM(shape, BF16), pltpu.SemaphoreType.DMA((parts,))],
+        out_shape=jax.ShapeDtypeStruct((copies, blocks + last, 1, width), F32),
+        scratch_shapes=[pltpu.VMEM(shape, BF16), pltpu.SemaphoreType.DMA((parts,))]
+        + ([pltpu.VMEM((blocks, 1, width), F32)] if last else []),
         compiler_params=pltpu.CompilerParams(vmem_limit_bytes=44 << 20),
         cost_estimate=LIGHT,
-        name="column_sums" if kernel is column_kernel else "row_sums",
-    )(gathered, *far([k, *after]))
+        name="row_sums" if kernel is row_kernel else "column_sums",
+    )(gathered, *far([k]), *after[:last], *far(after[last:]))
 
 
 def cut_kernel(x_ref, *refs):
-    outs = refs[-PARTS:]
-    rows = outs[0].shape[1]
-    for part, out in enumerate(outs):
-        out[...] = x_ref[:, part * rows : (part + 1) * rows, :]
+    start = 0
+    for out in refs[-len(PARTS) :]:
+        rows = out.shape[1]
+        out[...] = x_ref[:, start : start + rows, :]
+        start += rows
 
 
 def cut(x, after):
-    shape = (x.shape[0], x.shape[1] // PARTS, x.shape[2])
+    whole = x.shape[1] // sum(PARTS)
     return pl.pallas_call(
         cut_kernel,
         in_specs=[WHOLE] + [ANYWHERE] * len(after),
-        out_specs=[WHOLE] * PARTS,
-        out_shape=[jax.ShapeDtypeStruct(shape, x.dtype)] * PARTS,
+        out_specs=[WHOLE] * len(PARTS),
+        out_shape=[jax.ShapeDtypeStruct((x.shape[0], rows * whole, x.shape[2]), x.dtype) for rows in PARTS],
         compiler_params=pltpu.CompilerParams(vmem_limit_bytes=16 << 20),
         cost_estimate=LIGHT,
         name="cut_rows",
@@ -311,6 +337,28 @@
         cost_estimate=LIGHT,
         name="gate",
     )(x, *far(after))
+
+
+def potentials_kernel(homes, row_ref, col_ref, row_pot, column_pot, tile_row):
+    rows = jnp.sum(row_ref[:, :BLOCKS], axis=0)
+    columns = jnp.sum(col_ref[:, :BLOCKS], axis=0)
+    for b in range(BLOCKS):
+        row_pot[b : b + 1] = -jnp.log(rows[b])
+        column_pot[b : b + 1] = -jnp.log(columns[b])
+    for j in range(tile_row.shape[0]):
+        tile_row[j : j + 1] = col_ref[homes[j], BLOCKS]
+
+
+def potentials(row_gathered, gathered, homes):
+    width = gathered.shape[3]
+    return pl.pallas_call(
+        potentials_kernel,
+        in_specs=[SCALARS, WHOLE, WHOLE],
+        out_specs=[WHOLE] * 3,
+        out_shape=[jax.ShapeDtypeStruct((n, width), F32) for n in (BLOCKS, BLOCKS, homes.shape[0])],
+        cost_estimate=LIGHT,
+        name="potentials",
+    )(homes, row_gathered, gathered)
 
 
 def pick_kernel(ids, table, first, *refs):
@@ -353,21 +401,20 @@
     x_hbm, refs = refs[:count], refs[count:]
     y_hbm, r_ref, c_ref, o_hbm, x, y, o, x_sem, y_sem, o_sem = refs
     tiles, width, depth = x.shape
-    piece = x_hbm[0].shape[1]
-    groups = count // PARTS
+    groups = count // len(PARTS)
+    piece = width // groups
     cuts = o_sem.shape[1]
     rows = width // cuts
 
     def x_copies(j):
-        return [
-            pltpu.make_async_copy(
-                x_hbm[part * groups + p].at[j],
-                x.at[j, pl.ds(pl.multiple_of((places[p] * PARTS + part) * piece, piece), piece)],
-                x_sem.at[j, part, p],
-            )
-            for part in range(PARTS)
-            for p in range(groups)
-        ]
+        copies = []
+        for part in range(len(PARTS)):
+            for p in range(groups):
+                src = x_hbm[part * groups + p]
+                at = places[p] * piece + sum(x_hbm[earlier * groups].shape[1] for earlier in range(part))
+                rows = pl.ds(pl.multiple_of(at, 16), src.shape[1])
+                copies.append(pltpu.make_async_copy(src.at[j], x.at[j, rows], x_sem.at[j, part, p]))
+        return copies
 
     def y_copy(j):
         return pltpu.make_async_copy(y_hbm.at[tile_tgt[j]], y.at[j], y_sem.at[j])
@@ -376,17 +423,24 @@
         at = pl.ds(q * rows, rows)
         return pltpu.make_async_copy(o.at[j, at], o_hbm.at[0, 0, j, at], o_sem.at[j, q])
 
-    for j in range(tiles):
+    def fetch(j):
         y_copy(j).start()
         start_all(x_copies(j))
 
+    fetch(0)
+    fetch(1)
+
     def step(j, carry):
+        @pl.when(j + 2 < tiles)
+        def _():
+            fetch(j + 2)
+
         y_copy(j).wait()
         wait_all(x_copies(j))
-        col = c_ref[tile_tgt[j]]
+        col = c_ref[pl.ds(tile_tgt[j], 1), :]
         for q in range(cuts):
             at = slice(q * rows, (q + 1) * rows)
-            row = jnp.broadcast_to(r_ref[j, :, at], (128, rows)).T
+            row = jnp.broadcast_to(r_ref[pl.ds(j, 1), at], (128, rows)).T
             for start in range(0, width, 256):
                 s = lax.dot_general(x[j, at], y[j, start : start + 256], NT, preferred_element_type=F32) * scale
                 for g in range(0, 256, 128):
@@ -412,7 +466,7 @@
             pltpu.VMEM((tiles, width, depth), BF16),
             pltpu.VMEM((tiles, width, depth), BF16),
             pltpu.VMEM((tiles, width, width), F32),
-            pltpu.SemaphoreType.DMA((tiles, PARTS, len(pieces) // PARTS)),
+            pltpu.SemaphoreType.DMA((tiles, len(PARTS), len(pieces) // len(PARTS))),
             pltpu.SemaphoreType.DMA((tiles,)),
             pltpu.SemaphoreType.DMA((tiles, cuts)),
         ],
@@ -420,16 +474,14 @@
         compiler_params=pltpu.CompilerParams(vmem_limit_bytes=54 << 20),
         cost_estimate=LIGHT,
         name="posterior",
-    )(tile_tgt, places, *far([*pieces, targets]), tile_row[:, None], column_pot[:, None])
+    )(tile_tgt, places, *far([*pieces, targets]), tile_row, column_pot)
 
 
 def swap(x, axis):
     return lax.all_to_all(x, axis, split_axis=0, concat_axis=0, tiled=True)
 
 
-def torus_pieces(shard, side):
-    half = shard.shape[0] // 2
-
+def torus_pieces(parts, side):
     def shift(x, axis, by):
         def to(i):
             a, b = divmod(i, side)
@@ -440,14 +492,14 @@
 
     pieces = []
     lines = []
-    for route, part in enumerate((shard[:half], shard[half:])):
+    for route, part in enumerate(parts):
         lines.append(jnp.stack([part] + [shift(part, route, k) for k in range(1, side)]))
     back = [shift(line, 1 - route, 1) for route, line in enumerate(lines)]
     ahead = [shift(line, 1 - route, -1) for route, line in enumerate(lines)]
     mid = side // 2
     for route, line in enumerate(lines):
         far = [shift(back[route][:mid], 1 - route, 1), shift(ahead[route][mid:], 1 - route, -1)]
-        pieces += [line, back[route], jnp.concatenate(far), ahead[route]]
+        pieces += [line, back[route], *far, ahead[route]]
     return pieces
 
 
@@ -474,12 +526,11 @@
 
     whole_blocks = lax.all_gather(source_emb, "tgt", axis=1, tiled=True)
     side = math.isqrt(src_count)
-    target_pieces = torus_pieces(target_emb, side)
+    target_pieces = torus_pieces((target_emb[: tgt_blocks // 2], target_emb[tgt_blocks // 2 :]), side)
 
     slots = jnp.concatenate([slot_source[0, 0], slot_target[0, 0]])
     slots = jnp.pad(slots, (0, 128 - 2 * tiles))[None, None]
     column_slots = swap(jnp.broadcast_to(slots, (src_count, 1, 128)), "src")[:, 0]
-    row_slots = swap(jnp.broadcast_to(slots, (tgt_count, 1, 128)), "tgt")[:, 0, :tiles]
     named_src = column_slots[:, :tiles].reshape(-1) - own_row * src_blocks
     named_tgt = column_slots[:, tiles : 2 * tiles].reshape(-1) - own_col * tgt_blocks
     named = jnp.any(
@@ -489,33 +540,38 @@
     ).astype(jnp.int32)
     plan_column = home_plan(column_slots[:, :tiles], own_row, src_blocks)
 
-    aims = row_slots[jnp.stack([turned(own_col, far, other) for far, other in turns])]
+    aimed = jnp.stack([turned(own_col, far, other) for far, other in turns])
+    slot_row = jnp.pad(tile_src.astype(F32), (0, target_emb.shape[1] * src_count - tiles))[None]
     shards = cut(source_emb, [whole_blocks, named] + target_pieces)
     tables = [lax.all_gather(shard, "src", axis=0, tiled=True) for shard in shards]
     where = jnp.stack([own_row // side, own_row % side])
-    weights, sums, targets = score_weights(whole_blocks, target_pieces, where, named, tgt_count, side, shards)
-    pieces = [[None] * len(turns) for _ in range(PARTS)]
-    beside = [0] + [i for i, (far, _) in enumerate(turns) if far % 2]
-    across = [i for i in range(len(turns)) if i not in beside]
-    stages = [(0, beside), (0, across), (1, list(range(len(turns))))]
-    picked = []
-    for (part, chosen), iteration in zip(stages, range(ITERS)):
+    weights, sums, targets = score_weights(whole_blocks, target_pieces, where, named, slot_row, tgt_count, side, shards)
+    pieces = [[None] * len(turns) for _ in PARTS]
+    windows = [[(0, [0, 2, 6, 3, 7, 4])], [(0, [1, 5]), (1, [0, 2, 6, 4])], [(1, [1, 3, 7, 5])]]
+    for iteration, window in enumerate(windows):
         if iteration:
             sums = weighted_sums(row_kernel, gathered, weights, tgt_count, after=picked)
             sums = gate(sums, arrived)
         row_gathered = swap(sums, "tgt")
-        sums = weighted_sums(column_kernel, row_gathered, weights, src_count)
-        picked = list(pick(tables[part], aims[jnp.array(chosen)], row_gathered))
-        arrived = [turn(x, *turns[i]) if i else x for x, i in zip(picked, chosen)]
-        for x, i in zip(arrived, chosen):
-            pieces[part][i] = x
+        if not iteration:
+            aims = row_gathered[:, BLOCKS, 0, :tiles].astype(jnp.int32)[aimed]
+        picked, arrived = [], []
+        for number, (part, chosen) in enumerate(window):
+            if number:
+                sums = weighted_sums(column_kernel, row_gathered, weights, src_count)
+            taken = pick(tables[part], aims[jnp.array(chosen)], sums if number else row_gathered)
+            for x, i in zip(taken, chosen):
+                pieces[part][i] = turn(x, *turns[i]) if i else x
+                picked.append(x)
+                arrived.append(pieces[part][i])
+        if iteration == ITERS - 1:
+            sums = weighted_sums(last_column_kernel, row_gathered, weights, src_count, after=[plan_column, *picked])
+        elif len(window) == 1:
+            sums = weighted_sums(column_kernel, row_gathered, weights, src_count, after=picked)
         gathered = swap(sums, "src")
     pieces = pieces[0] + pieces[1]
 
-    row_total = jnp.sum(row_gathered, axis=0)[:, 0]
-    row_pot = -jnp.log(row_total)
-    column_pot = -jnp.log(jnp.sum(gathered, axis=0)[:, 0])
-    tile_row = jnp.take(swap(select_rows(row_pot, plan_column), "src"), tile_home, axis=0, mode="clip")
+    row_pot, column_pot, tile_row = potentials(row_gathered, gathered, tile_home)
 
     def unfinished(carry):
         return carry[0]
@@ -526,7 +582,7 @@
         potentials = log_domain(scores, tile_home, tile_tgt, plan_column, src_blocks, tgt_blocks)
         return (jnp.zeros((), jnp.bool_),) + potentials
 
-    out_of_range = jnp.logical_not(row_total[0, 0] > 0.0)
+    out_of_range = jnp.isnan(row_pot[0, 0])
     carry = (out_of_range, column_pot, row_pot, tile_row)
     _, column_pot, row_pot, tile_row = lax.while_loop(unfinished, redo, carry)
     log_post = posterior(pieces, places, targets, tile_row, column_pot, tile_tgt)

time: 1160 us -> 1130 us (0.974)
  starting transfers between devices: 142 us -> 116 us
    all_to_all x17 -> x14, starting transfers between devices: 91.1 us -> 73.9 us  [swap(): return lax.all_to_all(x, axis, split_axis=0, concat_axis=0, tiled=True)]
    ppermute x14, waiting for transfers between devices: 13 us -> 0.04 us  [turn(): lax.ppermute(x, 'tgt', [(t, turned(t, far, other)) for t in range(tgt_cou...]
    all_to_all x1 -> x2, blocking collectives: 14.1 us -> 26.5 us  [swap(): return lax.all_to_all(x, axis, split_axis=0, concat_axis=0, tiled=True)]
    all_to_all x17 -> x14, waiting for transfers between devices: 56.2 us -> 49.3 us  [swap(): return lax.all_to_all(x, axis, split_axis=0, concat_axis=0, tiled=True)]
    pallas_call x5 -> x6, Pallas kernels: 61 us -> 62.6 us  [the longest x5 60.8 us: weighted_sums(): pl.pallas_call(kernel, in_specs=[WHOLE, ANYWHERE] + [SCALARS] * last + [A...]
  transfers between devices with their start and end apart: 48 -> 45, of which waited for: 18 -> 14; matrix products, arithmetic and copies ran while one was open for 5% -> 5% of each run, Pallas kernels for 10% -> 10%
where the time goes in v3:
time: 1130 us; the launch traced here: 1120 us
  blocking collectives  591 us (52%)
  Pallas kernels  154 us (14%)
  other arithmetic  129 us (11%)
  starting transfers between devices  116 us (10%)
  waiting for transfers between devices  73.1 us (6%)
  local copies, waits for them, and re-layouts  35.6 us (3%)
  between operations  16.2 us (1%)
    pmax x3, blocking collectives, iterate(): largest = lax.pmax(local_max, 'src')  214 us
    psum x3, blocking collectives, iterate(): summed = lax.psum(local_sum * jnp.exp(local_max - largest), 'src')  209 us
    all_to_all x14, starting transfers between devices, swap(): return lax.all_to_all(x, axis, split_axis=0, concat_axis=0, tiled=True)  73.9 us
    pmax x3, blocking collectives, iterate(): largest = lax.pmax(local_max, 'tgt')  71.5 us
    psum x3, blocking collectives, iterate(): summed = lax.psum(local_sum * jnp.exp(local_max - largest), 'tgt')  70.7 us
    pallas_call x5, Pallas kernels, weighted_sums(): pl.pallas_call(kernel, in_specs=[WHOLE, ANYWHERE] + [SCALARS] * last + [A...  60.8 us
    all_to_all x14, waiting for transfers between devices, swap(): return lax.all_to_all(x, axis, split_axis=0, concat_axis=0, tiled=True)  49.3 us
    pallas_call x1, Pallas kernels, score_weights(): pl.pallas_call(functools.partial(scores_kernel, 2.0 / math.sqrt(depth) *...  39.9 us
  transfers between devices with their start and end apart: 45, of which 14 were waited for; matrix products, arithmetic and copies ran while one was open for 5% of the time, Pallas kernels for 10%

profile of v3, /device:TPU:0, one launch (start us, length us, event | category | flops | bytes accessed | tf_op | source)
XLA Modules:
  0.0 1115.5 jit_solution(17617240759545411203)
XLA Ops:
  69.8 39.9 %score_weights.1 = (bf16[4096,4096]{1,0:T(8,128)(2,1)}, f32[8,5,1,1024]{3,2,1,0:T(1,128)}, bf16[4,1024,768]{2,1,0:T(8,128)(2,1)}) custom-call(s32[4,4]{1,0:T(4,128)S(1)} %copy-done.24, s32[2]{0:T(128)S(1)} %pad_add_fusion.1.where, f32[1,1024]{1,0:T(1,128)S(1)} %bitcast.81, bf16[4,1024,768]{2,1,0:T(8,128)(2,1)} %all-gather.4.cloned.1.call-done.refs_0_.x_hbm, ...), custom_call_target="tpu_custom_call" | custom-call | bytes 1024 | tf_op jit(solution)/shard_map/score_weights/pallas_call | solution.py:200
  139.8 11.9 %column_sums.3 = f32[16,4,1,1024]{3,2,1,0:T(1,128)S(1)} custom-call(f32[8,5,1,1024]{3,2,1,0:T(1,128)S(1)} %copy-done.10, bf16[4096,4096]{1,0:T(8,128)(2,1)} %get-tuple-element.217.k_hbm, bf16[6,64,768]{2,1,0:T(8,128)(2,1)} %get-tuple-element.447.refs_0_, bf16[6,64,768]{2,1,0:T(8,128)(2,1)} %copy-done.6, bf16[6,64,768]{2,1,0:T(8,128)(2,1)} %copy-done.5, ...), custom_call_target="tpu_custom_call" | custom-call | bytes 1024 | tf_op jit(solution)/shard_map/column_sums/pallas_call | solution.py:293
  151.7 14.0 %all_to_all.71.g_ref = f32[16,4,1,1024]{3,2,1,0:T(1,128)S(1)} all-to-all(f32[16,4,1,1024]{3,2,1,0:T(1,128)S(1)} %column_sums.3), channel_id=1, replica_groups=mesh['src'=16,'tgt'=8] {'src'}, dimensions={0} | all-to-all | bytes 524288 | tf_op jit(solution)/shard_map/all_to_all | solution.py:481
  165.7 12.5 %row_sums.2.x_ref = f32[8,4,1,1024]{3,2,1,0:T(1,128)S(1)} custom-call(f32[16,4,1,1024]{3,2,1,0:T(1,128)S(1)} %all_to_all.71.g_ref, bf16[4096,4096]{1,0:T(8,128)(2,1)} %get-tuple-element.217.k_hbm, bf16[6,64,768]{2,1,0:T(8,128)(2,1)} %get-tuple-element.447.refs_0_, bf16[6,64,768]{2,1,0:T(8,128)(2,1)} %copy-done.6, bf16[6,64,768]{2,1,0:T(8,128)(2,1)} %copy-done.5, ...), custom_call_target="tpu_custom_call" | custom-call | bytes 1024 | tf_op jit(solution)/shard_map/row_sums/pallas_call | solution.py:293
  197.8 11.6 %column_sums.4.first = f32[16,4,1,1024]{3,2,1,0:T(1,128)S(1)} custom-call(f32[8,4,1,1024]{3,2,1,0:T(1,128)S(1)} %copy-done.12, bf16[4096,4096]{1,0:T(8,128)(2,1)} %get-tuple-element.217.k_hbm), custom_call_target="tpu_custom_call" | custom-call | bytes 1024 | tf_op jit(solution)/shard_map/column_sums/pallas_call | solution.py:293
  217.7 12.5 %all_to_all.72.g_ref = f32[16,4,1,1024]{3,2,1,0:T(1,128)S(1)} all-to-all(f32[16,4,1,1024]{3,2,1,0:T(1,128)} %copy-done.1), channel_id=1, replica_groups=mesh['src'=16,'tgt'=8] {'src'}, dimensions={0} | all-to-all | bytes 524288 | tf_op jit(solution)/shard_map/all_to_all | solution.py:481
  230.2 12.0 %row_sums.3.x_ref = f32[8,4,1,1024]{3,2,1,0:T(1,128)S(1)} custom-call(f32[16,4,1,1024]{3,2,1,0:T(1,128)S(1)} %all_to_all.72.g_ref, bf16[4096,4096]{1,0:T(8,128)(2,1)} %get-tuple-element.217.k_hbm, bf16[6,64,768]{2,1,0:T(8,128)(2,1)} %copy-done.18, bf16[6,64,768]{2,1,0:T(8,128)(2,1)} %copy-done.17, bf16[6,64,768]{2,1,0:T(8,128)(2,1)} %get-tuple-element.455.refs_2_.refs_8_, ...), custom_call_target="tpu_custom_call" | custom-call | bytes 1024 | tf_op jit(solution)/shard_map/row_sums/pallas_call | solution.py:293
  263.2 12.8 %column_sums.5 = f32[16,5,1,1024]{3,2,1,0:T(1,128)} custom-call(f32[8,4,1,1024]{3,2,1,0:T(1,128)S(1)} %copy-done.8, bf16[4096,4096]{1,0:T(8,128)(2,1)} %get-tuple-element.217.k_hbm, s32[16]{0:T(128)S(1)} %broadcast_select_fusion.3.plan, bf16[6,64,768]{2,1,0:T(8,128)(2,1)} %copy-done.16, bf16[6,64,768]{2,1,0:T(8,128)(2,1)} %copy-done.15, ...), custom_call_target="tpu_custom_call" | custom-call | bytes 1024 | tf_op jit(solution)/shard_map/column_sums/pallas_call | solution.py:293
  279.8 9.5 all-to-all-done.9.col_ref
  293.8 796.6 %while.28 = (pred[]{:T(512)}, f32[4,1024]{1,0:T(4,128)}, f32[4,1024]{1,0:T(4,128)}, f32[6,1024]{1,0:T(8,128)}, s32[6]{0:T(128)S(1)}, /*index=5*/s32[8]{0:T(128)S...) while((pred[]{:T(512)}, f32[4,1024]{1,0:T(4,128)}, ...), condition=%region_20.21_spmd, body=%region_3.20_spmd | while | flops 64245064 | bytes 104225968 | solution.py:587
  293.9 18.2 %posterior.2 = f32[1,1,6,1024,1024]{4,3,2,1,0:T(8,128)} custom-call(s32[6]{0:T(128)S(1)} %get-tuple-element.495.tile_tgt, s32[8]{0:T(128)S(1)} %get-tuple-element.496.places, bf16[6,64,768]{2,1,0:T(8,128)(2,1)} %get-tuple-element.497.refs_0_, bf16[6,64,768]{2,1,0:T(8,128)(2,1)} %get-tuple-element.498.refs_1_, ...), custom_call_target="tpu_custom_call" | custom-call | bytes 1024 | tf_op jit(solution)/shard_map/while/body/posterior/pallas_call | solution.py:461
  312.2 777.6 %while.30 = (s32[]{:T(128)}, f32[4,1024]{1,0:T(4,128)S(1)}, f32[4,1024]{1,0:T(4,128)}, f32[6,1024]{1,0:T(8,128)}, s32[6]{0:T(128)S(1)}, /*index=5*/s32[6]{0:T(12...) while((s32[]{:T(128)}, f32[4,1024]{1,0:T(4,128)S(1)}, ...), condition=%wide.region_19.19_spmd.clone, body=%wide.region_4.18_spmd.clone.sunk | while | flops 64245064 | bytes 103953936 | solution.py:71
  326.7 11.0 exponential_reduce_fusion.4
  346.1 23.9 %pmax.20 = f32[4,1024]{1,0:T(4,128)S(1)} all-reduce(f32[4,1024]{1,0:T(4,128)S(1)} %select_reduce_fusion.13), channel_id=1, replica_groups=mesh['src'=16,'tgt'=8] {'tgt'}, use_global_device_ids=true, to_apply=%region_8.7 | all-reduce | flops 4096 | bytes 32768 | tf_op jit(solution)/shard_map/while/body/while/body/eval_jaxpr/pmax | solution.py:54
  370.1 23.6 %psum.20 = f32[4,1024]{1,0:T(4,128)S(1)} all-reduce(f32[4,1024]{1,0:T(4,128)S(1)} %exponential_multiply_fusion.4), channel_id=1, replica_groups=mesh['src'=16,'tgt'=8] {'tgt'}, use_global_device_ids=true, to_apply=%region_12.11 | all-reduce | flops 4096 | bytes 32768 | tf_op jit(solution)/shard_map/while/body/while/body/eval_jaxpr/psum | solution.py:55
  410.3 9.4 add_reduce_fusion.5
  419.7 10.6 exponential_reduce_fusion.5
  430.5 71.2 %pmax.21 = f32[4,1024]{1,0:T(4,128)S(1)} all-reduce(f32[4,1024]{1,0:T(4,128)S(1)} %select_reduce_fusion.16), channel_id=1, replica_groups=mesh['src'=16,'tgt'=8] {'src'}, use_global_device_ids=true, to_apply=%region_15.14 | all-reduce | flops 4096 | bytes 32768 | tf_op jit(solution)/shard_map/while/body/while/body/eval_jaxpr/pmax | solution.py:62
  501.8 69.6 %psum.21 = f32[4,1024]{1,0:T(4,128)S(1)} all-reduce(f32[4,1024]{1,0:T(4,128)S(1)} %exponential_multiply_fusion.5), channel_id=1, replica_groups=mesh['src'=16,'tgt'=8] {'src'}, use_global_device_ids=true, to_apply=%region_18.17 | all-reduce | flops 4096 | bytes 32768 | tf_op jit(solution)/shard_map/while/body/while/body/eval_jaxpr/psum | solution.py:63
  585.9 11.0 exponential_reduce_fusion.4
  605.2 23.9 %pmax.20 = f32[4,1024]{1,0:T(4,128)S(1)} all-reduce(f32[4,1024]{1,0:T(4,128)S(1)} %select_reduce_fusion.13), channel_id=1, replica_groups=mesh['src'=16,'tgt'=8] {'tgt'}, use_global_device_ids=true, to_apply=%region_8.7 | all-reduce | flops 4096 | bytes 32768 | tf_op jit(solution)/shard_map/while/body/while/body/eval_jaxpr/pmax | solution.py:54
  629.3 23.6 %psum.20 = f32[4,1024]{1,0:T(4,128)S(1)} all-reduce(f32[4,1024]{1,0:T(4,128)S(1)} %exponential_multiply_fusion.4), channel_id=1, replica_groups=mesh['src'=16,'tgt'=8] {'tgt'}, use_global_device_ids=true, to_apply=%region_12.11 | all-reduce | flops 4096 | bytes 32768 | tf_op jit(solution)/shard_map/while/body/while/body/eval_jaxpr/psum | solution.py:55
  678.9 10.6 exponential_reduce_fusion.5
  689.7 71.2 %pmax.21 = f32[4,1024]{1,0:T(4,128)S(1)} all-reduce(f32[4,1024]{1,0:T(4,128)S(1)} %select_reduce_fusion.16), channel_id=1, replica_groups=mesh['src'=16,'tgt'=8] {'src'}, use_global_device_ids=true, to_apply=%region_15.14 | all-reduce | flops 4096 | bytes 32768 | tf_op jit(solution)/shard_map/while/body/while/body/eval_jaxpr/pmax | solution.py:62
  761.0 69.6 %psum.21 = f32[4,1024]{1,0:T(4,128)S(1)} all-reduce(f32[4,1024]{1,0:T(4,128)S(1)} %exponential_multiply_fusion.5), channel_id=1, replica_groups=mesh['src'=16,'tgt'=8] {'src'}, use_global_device_ids=true, to_apply=%region_18.17 | all-reduce | flops 4096 | bytes 32768 | tf_op jit(solution)/shard_map/while/body/while/body/eval_jaxpr/psum | solution.py:63
  845.1 11.0 exponential_reduce_fusion.4
  864.4 23.9 %pmax.20 = f32[4,1024]{1,0:T(4,128)S(1)} all-reduce(f32[4,1024]{1,0:T(4,128)S(1)} %select_reduce_fusion.13), channel_id=1, replica_groups=mesh['src'=16,'tgt'=8] {'tgt'}, use_global_device_ids=true, to_apply=%region_8.7 | all-reduce | flops 4096 | bytes 32768 | tf_op jit(solution)/shard_map/while/body/while/body/eval_jaxpr/pmax | solution.py:54
  888.5 23.6 %psum.20 = f32[4,1024]{1,0:T(4,128)S(1)} all-reduce(f32[4,1024]{1,0:T(4,128)S(1)} %exponential_multiply_fusion.4), channel_id=1, replica_groups=mesh['src'=16,'tgt'=8] {'tgt'}, use_global_device_ids=true, to_apply=%region_12.11 | all-reduce | flops 4096 | bytes 32768 | tf_op jit(solution)/shard_map/while/body/while/body/eval_jaxpr/psum | solution.py:55
  938.1 10.6 exponential_reduce_fusion.5
  948.8 71.2 %pmax.21 = f32[4,1024]{1,0:T(4,128)S(1)} all-reduce(f32[4,1024]{1,0:T(4,128)S(1)} %select_reduce_fusion.16), channel_id=1, replica_groups=mesh['src'=16,'tgt'=8] {'src'}, use_global_device_ids=true, to_apply=%region_15.14 | all-reduce | flops 4096 | bytes 32768 | tf_op jit(solution)/shard_map/while/body/while/body/eval_jaxpr/pmax | solution.py:62
  1020.2 69.6 %psum.21 = f32[4,1024]{1,0:T(4,128)S(1)} all-reduce(f32[4,1024]{1,0:T(4,128)S(1)} %exponential_multiply_fusion.5), channel_id=1, replica_groups=mesh['src'=16,'tgt'=8] {'src'}, use_global_device_ids=true, to_apply=%region_18.17 | all-reduce | flops 4096 | bytes 32768 | tf_op jit(solution)/shard_map/while/body/while/body/eval_jaxpr/psum | solution.py:63
  1090.4 18.4 %posterior.3 = f32[1,1,6,1024,1024]{4,3,2,1,0:T(8,128)} custom-call(s32[6]{0:T(128)S(1)} %get-tuple-element.600, s32[8]{0:T(128)S(1)} %get-tuple-element.598, bf16[6,64,768]{2,1,0:T(8,128)(2,1)} %get-tuple-element.542, bf16[6,64,768]{2,1,0:T(8,128)(2,1)} %get-tuple-element.555, bf16[6,64,768]{2,1,0:T(8,128)(2,1)} %get-tuple-element.545, ...), custom_call_target="tpu_custom_call" | custom-call | bytes 1024 | tf_op jit(solution)/shard_map/posterior/pallas_call | solution.py:461
  (371 shorter events, 286.6 us)
Async XLA Ops:
  7.2 58.1 %all-gather.4.cloned.1.call-start = ((), (), s32[]{:S(2)}) async-start(), calls=%async_computation.10 | async-start | bytes 7077888 | tf_op jit(solution)/shard_map/all_gather | solution.py:527
  13.6 13.8 %collective-permute-start.9 = (bf16[2,64,768]{2,1,0:T(8,128)(2,1)S(1)}, bf16[2,64,768]{2,1,0:T(8,128)(2,1)S(1)}, u32[]{:S(2)}, u32[]{:S(2)}) collective-permute-start(bf16[2,64,768]{2,1,0:T(8,128)(2,1)S(1)} %get-tuple-element.335), channel_id=1, source_target_pairs={{0,24},{8,0},{16,8},{24,16},{32,56},{40,32},{48,40},{56,48},{64,88... | collective-permute-start | bytes 589832 | tf_op jit(solution)/shard_map/ppermute | solution.py:491
  24.1 20.8 %collective-permute-start.3 = (bf16[4,2,64,768]{3,2,1,0:T(8,128)(2,1)S(1)}, bf16[4,2,64,768]{3,2,1,0:T(8,128)(2,1)S(1)}, u32[]{:S(2)}, u32[]{:S(2)}) collective-permute-start(bf16[4,2,64,768]{3,2,1,0:T(8,128)(2,1)S(1)} %pad_maximum_fusion.refs_2_.refs_0_), channel_id=1, source_target_pairs={{0,8},{8,16},{16,24},{24,0},{32,40},{40,48},{48,56},{56,32},{64,72... | collective-permute-start | bytes 2359304 | tf_op jit(solution)/shard_map/ppermute | solution.py:491
  25.7 20.3 %collective-permute-start.5 = (bf16[4,2,64,768]{3,2,1,0:T(8,128)(2,1)S(1)}, bf16[4,2,64,768]{3,2,1,0:T(8,128)(2,1)S(1)}, u32[]{:S(2)}, u32[]{:S(2)}) collective-permute-start(bf16[4,2,64,768]{3,2,1,0:T(8,128)(2,1)S(1)} %pad_maximum_fusion.refs_2_.refs_0_), channel_id=1, source_target_pairs={{0,24},{8,0},{16,8},{24,16},{32,56},{40,32},{48,40},{56,48},{64,88... | collective-permute-start | bytes 2359304 | tf_op jit(solution)/shard_map/ppermute | solution.py:491
  27.9 21.9 %collective-permute-start.10 = (bf16[4,2,64,768]{3,2,1,0:T(8,128)(2,1)S(1)}, bf16[4,2,64,768]{3,2,1,0:T(8,128)(2,1)}, u32[]{:S(2)}, u32[]{:S(2)}) collective-permute-start(bf16[4,2,64,768]{3,2,1,0:T(8,128)(2,1)S(1)} %pad_maximum_fusion.1.refs_7_.refs_5_), channel_id=1, source_target_pairs={{0,32},{8,40},{16,48},{24,56},{32,64},{40,72},{48,80},{56,88},{64,... | collective-permute-start | bytes 2359304 | tf_op jit(solution)/shard_map/ppermute | solution.py:491
  30.2 23.0 %collective-permute-start.12 = (bf16[4,2,64,768]{3,2,1,0:T(8,128)(2,1)S(1)}, bf16[4,2,64,768]{3,2,1,0:T(8,128)(2,1)}, u32[]{:S(2)}, u32[]{:S(2)}) collective-permute-start(bf16[4,2,64,768]{3,2,1,0:T(8,128)(2,1)S(1)} %pad_maximum_fusion.1.refs_7_.refs_5_), channel_id=1, source_target_pairs={{0,96},{8,104},{16,112},{24,120},{32,0},{40,8},{48,16},{56,24},{64... | collective-permute-start | bytes 2359304 | tf_op jit(solution)/shard_map/ppermute | solution.py:491
  34.7 22.0 %all-to-all-start.3 = ((s32[16,1,128]{2,1,0:T(1,128)}), s32[16,1,128]{2,1,0:T(1,128)S(1)}, u32[]{:S(2)}, u32[]{:S(2)}) async-start(s32[16,1,128]{2,1,0:T(1,128)} %broadcast_in_dim.253), calls=%async_computation.3 | async-start | bytes 16384 | tf_op jit(solution)/shard_map/all_to_all | solution.py:481
  39.4 88.9 %all-gather.6.cloned.1.call-start = ((), (), s32[]{:S(2)}) async-start(), calls=%async_computation.11 | async-start | bytes 6684672 | tf_op jit(solution)/shard_map/all_gather | solution.py:546
  67.4 142.7 %all-gather.8.cloned.1.call-start = ((), (), s32[]{:S(2)}) async-start(), calls=%async_computation.12 | async-start | bytes 6684672 | tf_op jit(solution)/shard_map/all_gather | solution.py:546
  131.8 47.2 %collective-permute-start.14 = (bf16[6,64,768]{2,1,0:T(8,128)(2,1)S(1)}, bf16[6,64,768]{2,1,0:T(8,128)(2,1)S(1)}, u32[]{:S(2)}, u32[]{:S(2)}) collective-permute-start(bf16[6,64,768]{2,1,0:T(8,128)(2,1)S(1)} %get-tuple-element.218.refs_1_), channel_id=1, source_target_pairs={{0,2},{1,3},{2,4},{3,5},{4,6},{5,7},{6,0},{7,1},{8,10},{9,11},{10,... | collective-permute-start | bytes 1769480 | tf_op jit(solution)/shard_map/ppermute | solution.py:523
  133.4 45.6 %collective-permute-start.15 = (bf16[6,64,768]{2,1,0:T(8,128)(2,1)S(1)}, bf16[6,64,768]{2,1,0:T(8,128)(2,1)S(1)}, u32[]{:S(2)}, u32[]{:S(2)}) collective-permute-start(bf16[6,64,768]{2,1,0:T(8,128)(2,1)S(1)} %get-tuple-element.219.refs_2_), channel_id=1, source_target_pairs={{0,6},{1,7},{2,0},{3,1},{4,2},{5,3},{6,4},{7,5},{8,14},{9,15},{10,... | collective-permute-start | bytes 1769480 | tf_op jit(solution)/shard_map/ppermute | solution.py:523
  135.1 43.9 %collective-permute-start.16 = (bf16[6,64,768]{2,1,0:T(8,128)(2,1)S(1)}, bf16[6,64,768]{2,1,0:T(8,128)(2,1)S(1)}, u32[]{:S(2)}, u32[]{:S(2)}) collective-permute-start(bf16[6,64,768]{2,1,0:T(8,128)(2,1)S(1)} %get-tuple-element.220.refs_3_), channel_id=1, source_target_pairs={{0,3},{1,2},{2,5},{3,4},{4,7},{5,6},{6,1},{7,0},{8,11},{9,10},{10,... | collective-permute-start | bytes 1769480 | tf_op jit(solution)/shard_map/ppermute | solution.py:523
  135.1 43.9 %collective-permute-start.17 = (bf16[6,64,768]{2,1,0:T(8,128)(2,1)S(1)}, bf16[6,64,768]{2,1,0:T(8,128)(2,1)S(1)}, u32[]{:S(2)}, u32[]{:S(2)}) collective-permute-start(bf16[6,64,768]{2,1,0:T(8,128)(2,1)S(1)} %get-tuple-element.221.refs_4_), channel_id=1, source_target_pairs={{0,7},{1,6},{2,1},{3,0},{4,3},{5,2},{6,5},{7,4},{8,15},{9,14},{10,... | collective-permute-start | bytes 1769480 | tf_op jit(solution)/shard_map/ppermute | solution.py:523
  138.0 41.0 %collective-permute-start.18 = (bf16[6,64,768]{2,1,0:T(8,128)(2,1)S(1)}, bf16[6,64,768]{2,1,0:T(8,128)(2,1)S(1)}, u32[]{:S(2)}, u32[]{:S(2)}) collective-permute-start(bf16[6,64,768]{2,1,0:T(8,128)(2,1)S(1)} %get-tuple-element.222.refs_5_), channel_id=1, source_target_pairs={{0,4},{1,5},{2,6},{3,7},{4,0},{5,1},{6,2},{7,3},{8,12},{9,13},{10,... | collective-permute-start | bytes 1769480 | tf_op jit(solution)/shard_map/ppermute | solution.py:523
  195.5 47.4 %collective-permute-start.19 = (bf16[6,64,768]{2,1,0:T(8,128)(2,1)S(1)}, bf16[6,64,768]{2,1,0:T(8,128)(2,1)S(1)}, u32[]{:S(2)}, u32[]{:S(2)}) collective-permute-start(bf16[6,64,768]{2,1,0:T(8,128)(2,1)S(1)} %get-tuple-element.223.refs_0_), channel_id=1, source_target_pairs={{0,1},{1,0},{2,3},{3,2},{4,5},{5,4},{6,7},{7,6},{8,9},{9,8},{10,11... | collective-permute-start | bytes 1769480 | tf_op jit(solution)/shard_map/ppermute | solution.py:523
  195.6 47.3 %collective-permute-start.20 = (bf16[6,64,768]{2,1,0:T(8,128)(2,1)S(1)}, bf16[6,64,768]{2,1,0:T(8,128)(2,1)S(1)}, u32[]{:S(2)}, u32[]{:S(2)}) collective-permute-start(bf16[6,64,768]{2,1,0:T(8,128)(2,1)S(1)} %get-tuple-element.224.refs_1_), channel_id=1, source_target_pairs={{0,5},{1,4},{2,7},{3,6},{4,1},{5,0},{6,3},{7,2},{8,13},{9,12},{10,... | collective-permute-start | bytes 1769480 | tf_op jit(solution)/shard_map/ppermute | solution.py:523
  212.9 30.0 %collective-permute-start.21 = (bf16[6,64,768]{2,1,0:T(8,128)(2,1)S(1)}, bf16[6,64,768]{2,1,0:T(8,128)(2,1)S(1)}, u32[]{:S(2)}, u32[]{:S(2)}) collective-permute-start(bf16[6,64,768]{2,1,0:T(8,128)(2,1)S(1)} %get-tuple-element.226.refs_3_), channel_id=1, source_target_pairs={{0,2},{1,3},{2,4},{3,5},{4,6},{5,7},{6,0},{7,1},{8,10},{9,11},{10,... | collective-permute-start | bytes 1769480 | tf_op jit(solution)/shard_map/ppermute | solution.py:523
  214.2 28.7 %collective-permute-start.22 = (bf16[6,64,768]{2,1,0:T(8,128)(2,1)S(1)}, bf16[6,64,768]{2,1,0:T(8,128)(2,1)S(1)}, u32[]{:S(2)}, u32[]{:S(2)}) collective-permute-start(bf16[6,64,768]{2,1,0:T(8,128)(2,1)S(1)} %get-tuple-element.227.refs_4_), channel_id=1, source_target_pairs={{0,6},{1,7},{2,0},{3,1},{4,2},{5,3},{6,4},{7,5},{8,14},{9,15},{10,... | collective-permute-start | bytes 1769480 | tf_op jit(solution)/shard_map/ppermute | solution.py:523
  216.2 27.5 %collective-permute-start.23 = (bf16[6,64,768]{2,1,0:T(8,128)(2,1)S(1)}, bf16[6,64,768]{2,1,0:T(8,128)(2,1)}, u32[]{:S(2)}, u32[]{:S(2)}) collective-permute-start(bf16[6,64,768]{2,1,0:T(8,128)(2,1)S(1)} %get-tuple-element.228.refs_5_), channel_id=1, source_target_pairs={{0,4},{1,5},{2,6},{3,7},{4,0},{5,1},{6,2},{7,3},{8,12},{9,13},{10,... | collective-permute-start | bytes 1769480 | tf_op jit(solution)/shard_map/ppermute | solution.py:523
  258.9 34.9 %collective-permute-start.24 = (bf16[6,64,768]{2,1,0:T(8,128)(2,1)S(1)}, bf16[6,64,768]{2,1,0:T(8,128)(2,1)}, u32[]{:S(2)}, u32[]{:S(2)}) collective-permute-start(bf16[6,64,768]{2,1,0:T(8,128)(2,1)S(1)} %get-tuple-element.229.refs_0_), channel_id=1, source_target_pairs={{0,1},{1,0},{2,3},{3,2},{4,5},{5,4},{6,7},{7,6},{8,9},{9,8},{10,11... | collective-permute-start | bytes 1769480 | tf_op jit(solution)/shard_map/ppermute | solution.py:523
  259.0 34.8 %collective-permute-start.25 = (bf16[6,64,768]{2,1,0:T(8,128)(2,1)S(1)}, bf16[6,64,768]{2,1,0:T(8,128)(2,1)}, u32[]{:S(2)}, u32[]{:S(2)}) collective-permute-start(bf16[6,64,768]{2,1,0:T(8,128)(2,1)S(1)} %get-tuple-element.230.refs_1_), channel_id=1, source_target_pairs={{0,3},{1,2},{2,5},{3,4},{4,7},{5,6},{6,1},{7,0},{8,11},{9,10},{10,... | collective-permute-start | bytes 1769480 | tf_op jit(solution)/shard_map/ppermute | solution.py:523
  259.7 34.1 %collective-permute-start.26 = (bf16[6,64,768]{2,1,0:T(8,128)(2,1)S(1)}, bf16[6,64,768]{2,1,0:T(8,128)(2,1)}, u32[]{:S(2)}, u32[]{:S(2)}) collective-permute-start(bf16[6,64,768]{2,1,0:T(8,128)(2,1)S(1)} %get-tuple-element.231.refs_3_), channel_id=1, source_target_pairs={{0,5},{1,4},{2,7},{3,6},{4,1},{5,0},{6,3},{7,2},{8,13},{9,12},{10,... | collective-permute-start | bytes 1769480 | tf_op jit(solution)/shard_map/ppermute | solution.py:523
  261.4 32.4 %collective-permute-start.27 = (bf16[6,64,768]{2,1,0:T(8,128)(2,1)S(1)}, bf16[6,64,768]{2,1,0:T(8,128)(2,1)}, u32[]{:S(2)}, u32[]{:S(2)}) collective-permute-start(bf16[6,64,768]{2,1,0:T(8,128)(2,1)S(1)} %get-tuple-element.232.refs_2_), channel_id=1, source_target_pairs={{0,7},{1,6},{2,1},{3,0},{4,3},{5,2},{6,5},{7,4},{8,15},{9,14},{10,... | collective-permute-start | bytes 1769480 | tf_op jit(solution)/shard_map/ppermute | solution.py:523
  323.1 15.5 %all-to-all-start = ((f32[16,1,1024]{2,1,0:T(1,128)}), f32[16,1,1024]{2,1,0:T(1,128)S(1)}, u32[]{:S(2)}, u32[]{:S(2)}) async-start(f32[16,1,1024]{2,1,0:T(1,128)} %copy.30), calls=%async_computation | async-start | bytes 131072 | tf_op jit(solution)/shard_map/while/body/while/body/eval_jaxpr/all_to_all | solution.py:481
  338.7 31.2 %all-to-all-start.1 = ((f32[16,1,1024]{2,1,0:T(1,128)}), f32[16,1,1024]{2,1,0:T(1,128)S(1)}, u32[]{:S(2)}, u32[]{:S(2)}) async-start(f32[16,1,1024]{2,1,0:T(1,128)} %copy.32), calls=%async_computation.1 | async-start | bytes 131072 | tf_op jit(solution)/shard_map/while/body/while/body/eval_jaxpr/all_to_all | solution.py:481
  395.1 14.6 %all-to-all-start.2 = ((f32[16,1,1024]{2,1,0:T(1,128)}), f32[16,1,1024]{2,1,0:T(1,128)S(1)}, u32[]{:S(2)}, u32[]{:S(2)}) async-start(f32[16,1,1024]{2,1,0:T(1,128)} %copy.34), calls=%async_computation.2 | async-start | bytes 131072 | tf_op jit(solution)/shard_map/while/body/while/body/eval_jaxpr/all_to_all | solution.py:481
  582.4 15.5 %all-to-all-start = ((f32[16,1,1024]{2,1,0:T(1,128)}), f32[16,1,1024]{2,1,0:T(1,128)S(1)}, u32[]{:S(2)}, u32[]{:S(2)}) async-start(f32[16,1,1024]{2,1,0:T(1,128)} %copy.30), calls=%async_computation | async-start | bytes 131072 | tf_op jit(solution)/shard_map/while/body/while/body/eval_jaxpr/all_to_all | solution.py:481
  597.9 31.2 %all-to-all-start.1 = ((f32[16,1,1024]{2,1,0:T(1,128)}), f32[16,1,1024]{2,1,0:T(1,128)S(1)}, u32[]{:S(2)}, u32[]{:S(2)}) async-start(f32[16,1,1024]{2,1,0:T(1,128)} %copy.32), calls=%async_computation.1 | async-start | bytes 131072 | tf_op jit(solution)/shard_map/while/body/while/body/eval_jaxpr/all_to_all | solution.py:481
  654.2 14.6 %all-to-all-start.2 = ((f32[16,1,1024]{2,1,0:T(1,128)}), f32[16,1,1024]{2,1,0:T(1,128)S(1)}, u32[]{:S(2)}, u32[]{:S(2)}) async-start(f32[16,1,1024]{2,1,0:T(1,128)} %copy.34), calls=%async_computation.2 | async-start | bytes 131072 | tf_op jit(solution)/shard_map/while/body/while/body/eval_jaxpr/all_to_all | solution.py:481
  841.6 15.5 %all-to-all-start = ((f32[16,1,1024]{2,1,0:T(1,128)}), f32[16,1,1024]{2,1,0:T(1,128)S(1)}, u32[]{:S(2)}, u32[]{:S(2)}) async-start(f32[16,1,1024]{2,1,0:T(1,128)} %copy.30), calls=%async_computation | async-start | bytes 131072 | tf_op jit(solution)/shard_map/while/body/while/body/eval_jaxpr/all_to_all | solution.py:481
  857.1 31.2 %all-to-all-start.1 = ((f32[16,1,1024]{2,1,0:T(1,128)}), f32[16,1,1024]{2,1,0:T(1,128)S(1)}, u32[]{:S(2)}, u32[]{:S(2)}) async-start(f32[16,1,1024]{2,1,0:T(1,128)} %copy.32), calls=%async_computation.1 | async-start | bytes 131072 | tf_op jit(solution)/shard_map/while/body/while/body/eval_jaxpr/all_to_all | solution.py:481
  913.4 14.6 %all-to-all-start.2 = ((f32[16,1,1024]{2,1,0:T(1,128)}), f32[16,1,1024]{2,1,0:T(1,128)S(1)}, u32[]{:S(2)}, u32[]{:S(2)}) async-start(f32[16,1,1024]{2,1,0:T(1,128)} %copy.34), calls=%async_computation.2 | async-start | bytes 131072 | tf_op jit(solution)/shard_map/while/body/while/body/eval_jaxpr/all_to_all | solution.py:481
  (73 other events, 1454.8 us)
Sparse Core Ops, SparseCore 0:
  9.7 43.5 all-gather.3
  67.5 60.6 all-gather.5
  130.4 61.0 all-gather.7

commit v4 on v3

--- a/solution.py
+++ b/solution.py
@@ -104,8 +104,8 @@
 
 
 def scores_kernel(scale, side, named, where, extra, x_hbm, *refs):
-    pieces, refs = refs[:10], refs[-11:]
-    k_hbm, sum_ref, targets_hbm, x, y, k_out, lowest, x_sem, y_sem, k_sem, leave = refs
+    pieces, refs = refs[:10], refs[-12:]
+    k_hbm, sum_ref, ratio_ref, targets_hbm, x, y, k_out, lowest, x_sem, y_sem, k_sem, leave = refs
     blocks, width, _ = y.shape
     rows = k_out.shape[1]
     half = blocks // 2
@@ -159,6 +159,7 @@
 
         low = lowest[...]
         lanes = jnp.zeros((rows, 128), F32)
+        rounded = jnp.zeros((rows, 128), F32)
         here = x[b, pl.ds(pl.multiple_of(part * rows, rows), rows), :]
         for c in range(blocks):
             s = lax.dot_general(here, y[c], NT, preferred_element_type=F32)
@@ -166,17 +167,22 @@
             k = e.astype(BF16)
             is_named = named[b, c] > 0
             k_out[slot, :, c * width : (c + 1) * width] = jnp.where(is_named, k, jnp.zeros_like(k))
-            acc, least = e[:, :128], k[:, :128]
+            acc, kept, least = e[:, :128], k[:, :128].astype(F32), k[:, :128]
             for g in range(128, width, 128):
                 acc = acc + e[:, g : g + 128]
+                kept = kept + k[:, g : g + 128].astype(F32)
                 least = jnp.minimum(least, k[:, g : g + 128])
             lanes = lanes + jnp.where(is_named, acc, 0.0)
+            rounded = rounded + jnp.where(is_named, kept, 0.0)
             low = jnp.minimum(low, jnp.min(least.reshape(rows // 16, 16, 128), axis=0))
         lowest[...] = low
         out_copy(i, slot).start()
         total = lane_totals(lanes)
         fine = (jnp.min(low.astype(F32)) > math.exp(-LIMIT)) & all_within(total, 0.0, math.exp(LIMIT))
-        put(sum_ref, b, pl.ds(pl.multiple_of(part * rows, rows), rows), jnp.where(fine, total, jnp.nan))
+        at = pl.ds(pl.multiple_of(part * rows, rows), rows)
+        put(sum_ref, b, at, jnp.where(fine, total, jnp.nan))
+        low_sum = lane_totals(rounded)
+        ratio_ref[b, :, at] = jnp.where(low_sum > 0.0, total / low_sum, 1.0)
         return carry
 
     lax.fori_loop(0, blocks * per, step, 0)
@@ -200,7 +206,7 @@
     return pl.pallas_call(
         functools.partial(scores_kernel, 2.0 / math.sqrt(depth) * math.log2(math.e), side),
         in_specs=[SCALARS, SCALARS, WHOLE] + [ANYWHERE] * (1 + len(pieces) + len(after)),
-        out_specs=[ANYWHERE, WHOLE, ANYWHERE],
+        out_specs=[ANYWHERE, WHOLE, WHOLE, ANYWHERE],
         scratch_shapes=[
             pltpu.VMEM((blocks, width, depth), BF16),
             pltpu.VMEM((blocks, width, depth), BF16),
@@ -214,6 +220,7 @@
         out_shape=[
             jax.ShapeDtypeStruct((n, n), BF16),
             jax.ShapeDtypeStruct((copies, blocks + 1, 1, width), F32),
+            jax.ShapeDtypeStruct((blocks, 1, width), F32),
             jax.ShapeDtypeStruct((blocks, width, depth), BF16),
         ],
         compiler_params=pltpu.CompilerParams(vmem_limit_bytes=44 << 20),
@@ -228,26 +235,26 @@
     return [1.0 / total[b] for b in range(total.shape[0])], jnp.where(fine, 0.0, jnp.nan)
 
 
-def column_kernel(g_ref, k_hbm, *refs):
-    columns(g_ref, k_hbm, *refs[-3:])
-
-
-def last_column_kernel(g_ref, k_hbm, plan, *refs):
+def column_kernel(g_ref, ratio, k_hbm, *refs):
+    columns(g_ref, ratio, k_hbm, *refs[-3:])
+
+
+def last_column_kernel(g_ref, ratio, k_hbm, plan, *refs):
     o_ref, k, sem, logs = refs[-4:]
     total = jnp.sum(g_ref[:, :BLOCKS], axis=0)
     logs[...] = -jnp.log(total)
     for s in range(o_ref.shape[0]):
         o_ref[s, total.shape[0]] = logs[jnp.maximum(plan[s], 0)]
-    columns(g_ref, k_hbm, o_ref, k, sem)
-
-
-def columns(g_ref, k_hbm, o_ref, k, sem):
+    columns(g_ref, ratio, k_hbm, o_ref, k, sem)
+
+
+def columns(g_ref, ratio, k_hbm, o_ref, k, sem):
     parts, n, cols = k.shape
     copies = [pltpu.make_async_copy(k_hbm.at[:, pl.ds(j * cols, cols)], k.at[j], sem.at[j]) for j in range(parts)]
     start_all(copies)
     inv, spoil = inverse_parts(g_ref, 1e-38, 1e38)
     blocks, width = len(inv), inv[0].shape[1]
-    lhs = [stack3(v) for v in inv]
+    lhs = [stack3(v * ratio[b]) for b, v in enumerate(inv)]
     per = width // cols
     for j in range(parts):
         copies[j].wait()
@@ -258,7 +265,7 @@
         put(o_ref, j // per, slice(start, start + cols), acc[0:1] + acc[1:2] + acc[2:3] + spoil)
 
 
-def row_kernel(g_ref, k_hbm, *refs):
+def row_kernel(g_ref, ratio, k_hbm, *refs):
     o_ref, k, sem = refs[-3:]
     parts, rows, n = k.shape
     copies = [pltpu.make_async_copy(k_hbm.at[pl.ds(j * rows, rows)], k.at[j], sem.at[j]) for j in range(parts)]
@@ -281,10 +288,12 @@
                 at = c * width + g
                 lanes = lanes + k[j, :, at : at + 128].astype(F32) * inv[c][:, g : g + 128]
         start = (j % per) * rows
-        put(o_ref, j // per, slice(start, start + rows), acc[0:1] + acc[1:2] + acc[2:3] + lane_totals(lanes) + spoil)
-
-
-def weighted_sums(kernel, gathered, k, copies, after=()):
+        at = slice(start, start + rows)
+        out = (acc[0:1] + acc[1:2] + acc[2:3] + lane_totals(lanes)) * ratio[j // per, :, at]
+        put(o_ref, j // per, at, out + spoil)
+
+
+def weighted_sums(kernel, gathered, ratio, k, copies, after=()):
     n = k.shape[0]
     blocks, width = BLOCKS, gathered.shape[3]
     parts = n // ROWS
@@ -292,7 +301,7 @@
     shape = (parts, ROWS, n) if kernel is row_kernel else (parts, n, ROWS)
     return pl.pallas_call(
         kernel,
-        in_specs=[WHOLE, ANYWHERE] + [SCALARS] * last + [ANYWHERE] * (len(after) - last),
+        in_specs=[WHOLE, WHOLE, ANYWHERE] + [SCALARS] * last + [ANYWHERE] * (len(after) - last),
         out_specs=WHOLE,
         out_shape=jax.ShapeDtypeStruct((copies, blocks + last, 1, width), F32),
         scratch_shapes=[pltpu.VMEM(shape, BF16), pltpu.SemaphoreType.DMA((parts,))]
@@ -300,7 +309,7 @@
         compiler_params=pltpu.CompilerParams(vmem_limit_bytes=44 << 20),
         cost_estimate=LIGHT,
         name="row_sums" if kernel is row_kernel else "column_sums",
-    )(gathered, *far([k]), *after[:last], *far(after[last:]))
+    )(gathered, ratio, *far([k]), *after[:last], *far(after[last:]))
 
 
 def cut_kernel(x_ref, *refs):
@@ -325,15 +334,15 @@
 
 
 def gate_kernel(x_ref, *refs):
-    refs[-1][...] = x_ref[...]
-
-
-def gate(x, after):
+    refs[-1][...] = jnp.broadcast_to(x_ref[...], refs[-1].shape)
+
+
+def gate(x, copies, after):
     return pl.pallas_call(
         gate_kernel,
         in_specs=[WHOLE] + [ANYWHERE] * len(after),
         out_specs=WHOLE,
-        out_shape=jax.ShapeDtypeStruct(x.shape, x.dtype),
+        out_shape=jax.ShapeDtypeStruct((copies,) + x.shape[1:], x.dtype),
         cost_estimate=LIGHT,
         name="gate",
     )(x, *far(after))
@@ -394,7 +403,7 @@
         compiler_params=pltpu.CompilerParams(vmem_limit_bytes=16 << 20),
         cost_estimate=LIGHT,
         name="pick_pieces",
-    )(ids, *far([table, after]))
+    )(ids, *far([table]), after)
 
 
 def posterior_kernel(scale, count, tile_tgt, places, *refs):
@@ -545,29 +554,29 @@
     shards = cut(source_emb, [whole_blocks, named] + target_pieces)
     tables = [lax.all_gather(shard, "src", axis=0, tiled=True) for shard in shards]
     where = jnp.stack([own_row // side, own_row % side])
-    weights, sums, targets = score_weights(whole_blocks, target_pieces, where, named, slot_row, tgt_count, side, shards)
+    weights, sums, ratio, targets = score_weights(whole_blocks, target_pieces, where, named, slot_row, tgt_count, side, shards)
     pieces = [[None] * len(turns) for _ in PARTS]
     windows = [[(0, [0, 2, 6, 3, 7, 4])], [(0, [1, 5]), (1, [0, 2, 6, 4])], [(1, [1, 3, 7, 5])]]
     for iteration, window in enumerate(windows):
         if iteration:
-            sums = weighted_sums(row_kernel, gathered, weights, tgt_count, after=picked)
-            sums = gate(sums, arrived)
+            sums = weighted_sums(row_kernel, gathered, ratio, weights, 1, after=picked)
+            sums = gate(sums, tgt_count, arrived)
         row_gathered = swap(sums, "tgt")
         if not iteration:
             aims = row_gathered[:, BLOCKS, 0, :tiles].astype(jnp.int32)[aimed]
         picked, arrived = [], []
         for number, (part, chosen) in enumerate(window):
             if number:
-                sums = weighted_sums(column_kernel, row_gathered, weights, src_count)
+                sums = weighted_sums(column_kernel, row_gathered, ratio, weights, src_count, after=picked)
             taken = pick(tables[part], aims[jnp.array(chosen)], sums if number else row_gathered)
             for x, i in zip(taken, chosen):
                 pieces[part][i] = turn(x, *turns[i]) if i else x
                 picked.append(x)
                 arrived.append(pieces[part][i])
         if iteration == ITERS - 1:
-            sums = weighted_sums(last_column_kernel, row_gathered, weights, src_count, after=[plan_column, *picked])
+            sums = weighted_sums(last_column_kernel, row_gathered, ratio, weights, src_count, after=[plan_column, *picked])
         elif len(window) == 1:
-            sums = weighted_sums(column_kernel, row_gathered, weights, src_count, after=picked)
+            sums = weighted_sums(column_kernel, row_gathered, ratio, weights, src_count, after=picked)
         gathered = swap(sums, "src")
     pieces = pieces[0] + pieces[1]
 

time: 1130 us -> 1120 us (level)
  no operation moved by 1% of the time
where the time goes in v4:
time: 1120 us; the launch traced here: 1110 us
  blocking collectives  591 us (53%)
  Pallas kernels  155 us (14%)
  other arithmetic  129 us (12%)
  starting transfers between devices  116 us (10%)
  waiting for transfers between devices  71.2 us (6%)
  local copies, waits for them, and re-layouts  29.5 us (3%)
  between operations  16.1 us (1%)
    pmax x3, blocking collectives, iterate(): largest = lax.pmax(local_max, 'src')  214 us
    psum x3, blocking collectives, iterate(): summed = lax.psum(local_sum * jnp.exp(local_max - largest), 'src')  209 us
    all_to_all x14, starting transfers between devices, swap(): return lax.all_to_all(x, axis, split_axis=0, concat_axis=0, tiled=True)  74.1 us
    pmax x3, blocking collectives, iterate(): largest = lax.pmax(local_max, 'tgt')  71.5 us
    psum x3, blocking collectives, iterate(): summed = lax.psum(local_sum * jnp.exp(local_max - largest), 'tgt')  70.7 us
    pallas_call x5, Pallas kernels, weighted_sums(): pl.pallas_call(kernel, in_specs=[WHOLE, WHOLE, ANYWHERE] + [SCALARS] * la...  60.8 us
    all_to_all x14, waiting for transfers between devices, swap(): return lax.all_to_all(x, axis, split_axis=0, concat_axis=0, tiled=True)  49.3 us
    pallas_call x1, Pallas kernels, score_weights(): pl.pallas_call(functools.partial(scores_kernel, 2.0 / math.sqrt(depth) *...  41.7 us
  transfers between devices with their start and end apart: 45, of which 14 were waited for; matrix products, arithmetic and copies ran while one was open for 5% of the time, Pallas kernels for 10%

profile of v4, /device:TPU:0, one launch (start us, length us, event | category | flops | bytes accessed | tf_op | source)
XLA Modules:
  0.0 1108.8 jit_solution(17956442887991777555)
XLA Ops:
  69.1 41.7 %score_weights.1 = (bf16[4096,4096]{1,0:T(8,128)(2,1)}, f32[8,5,1,1024]{3,2,1,0:T(1,128)}, f32[4,1,1024]{2,1,0:T(1,128)S(1)}, bf16[4,1024,768]{2,1,0:T(8,128)(2,1)}) custom-call(s32[4,4]{1,0:T(4,128)S(1)} %copy-done.18, s32[2]{0:T(128)S(1)} %pad_add_fusion.1.where, f32[1,1024]{1,0:T(1,128)S(1)} %bitcast.81, ...), custom_call_target="tpu_custom_call" | custom-call | bytes 1024 | tf_op jit(solution)/shard_map/score_weights/pallas_call | solution.py:206
  138.1 12.0 %column_sums.3 = f32[16,4,1,1024]{3,2,1,0:T(1,128)S(1)} custom-call(f32[8,5,1,1024]{3,2,1,0:T(1,128)S(1)} %all-to-all-done.4.first.g_ref, f32[4,1,1024]{2,1,0:T(1,128)S(1)} %get-tuple-element.218.ratio, bf16[4096,4096]{1,0:T(8,128)(2,1)} %get-tuple-element.219.k_hbm, bf16[6,64,768]{2,1,0:T(8,128)(2,1)} %get-tuple-element.449.refs_0_, ...), custom_call_target="tpu_custom_call" | custom-call | bytes 1024 | tf_op jit(solution)/shard_map/column_sums/pallas_call | solution.py:302
  150.2 13.7 %all_to_all.71.g_ref = f32[16,4,1,1024]{3,2,1,0:T(1,128)S(1)} all-to-all(f32[16,4,1,1024]{3,2,1,0:T(1,128)S(1)} %column_sums.3), channel_id=1, replica_groups=mesh['src'=16,'tgt'=8] {'src'}, dimensions={0} | all-to-all | bytes 524288 | tf_op jit(solution)/shard_map/all_to_all | solution.py:490
  163.9 12.4 %row_sums.2.x_ref = f32[1,4,1,1024]{3,2,1,0:T(1,128)S(1)} custom-call(f32[16,4,1,1024]{3,2,1,0:T(1,128)S(1)} %all_to_all.71.g_ref, f32[4,1,1024]{2,1,0:T(1,128)S(1)} %get-tuple-element.218.ratio, bf16[4096,4096]{1,0:T(8,128)(2,1)} %get-tuple-element.219.k_hbm, bf16[6,64,768]{2,1,0:T(8,128)(2,1)} %get-tuple-element.449.refs_0_, ...), custom_call_target="tpu_custom_call" | custom-call | bytes 1024 | tf_op jit(solution)/shard_map/row_sums/pallas_call | solution.py:302
  193.4 11.6 %column_sums.4.first = f32[16,4,1,1024]{3,2,1,0:T(1,128)S(1)} custom-call(f32[8,4,1,1024]{3,2,1,0:T(1,128)S(1)} %all-to-all-done.6.first.g_ref, f32[4,1,1024]{2,1,0:T(1,128)S(1)} %get-tuple-element.218.ratio, bf16[4096,4096]{1,0:T(8,128)(2,1)} %get-tuple-element.219.k_hbm, bf16[6,64,768]{2,1,0:T(8,128)(2,1)} %copy-done.4, bf16[6,64,768]{2,1,0:T(8,128)(2,1)} %copy-done.2), custom_call_target="tpu_custom_call" | custom-call | bytes 1024 | tf_op jit(solution)/shard_map/column_sums/pallas_call | solution.py:302
  212.6 12.5 %all_to_all.72.g_ref = f32[16,4,1,1024]{3,2,1,0:T(1,128)S(1)} all-to-all(f32[16,4,1,1024]{3,2,1,0:T(1,128)S(1)} %column_sums.4.first), channel_id=1, replica_groups=mesh['src'=16,'tgt'=8] {'src'}, dimensions={0} | all-to-all | bytes 524288 | tf_op jit(solution)/shard_map/all_to_all | solution.py:490
  225.1 12.0 %row_sums.3.x_ref = f32[1,4,1,1024]{3,2,1,0:T(1,128)S(1)} custom-call(f32[16,4,1,1024]{3,2,1,0:T(1,128)S(1)} %all_to_all.72.g_ref, f32[4,1,1024]{2,1,0:T(1,128)S(1)} %get-tuple-element.218.ratio, bf16[4096,4096]{1,0:T(8,128)(2,1)} %get-tuple-element.219.k_hbm, bf16[6,64,768]{2,1,0:T(8,128)(2,1)} %copy-done.4, bf16[6,64,768]{2,1,0:T(8,128)(2,1)} %copy-done.2, ...), custom_call_target="tpu_custom_call" | custom-call | bytes 1024 | tf_op jit(solution)/shard_map/row_sums/pallas_call | solution.py:302
  256.6 12.8 %column_sums.5 = f32[16,5,1,1024]{3,2,1,0:T(1,128)} custom-call(f32[8,4,1,1024]{3,2,1,0:T(1,128)S(1)} %all-to-all-done.8.first.g_ref.row_ref, f32[4,1,1024]{2,1,0:T(1,128)S(1)} %get-tuple-element.218.ratio, bf16[4096,4096]{1,0:T(8,128)(2,1)} %get-tuple-element.219.k_hbm, s32[16]{0:T(128)S(1)} %broadcast_select_fusion.3.plan, bf16[6,64,768]{2,1,0:T(8,128)(2,1)} %copy-done.12, ...), custom_call_target="tpu_custom_call" | custom-call | bytes 1024 | tf_op jit(solution)/shard_map/column_sums/pallas_call | solution.py:302
  273.2 9.5 all-to-all-done.9.col_ref
  287.2 796.6 %while.28 = (pred[]{:T(512)}, f32[4,1024]{1,0:T(4,128)}, f32[4,1024]{1,0:T(4,128)}, f32[6,1024]{1,0:T(8,128)}, s32[6]{0:T(128)S(1)}, /*index=5*/s32[8]{0:T(128)S...) while((pred[]{:T(512)}, f32[4,1024]{1,0:T(4,128)}, ...), condition=%region_20.21_spmd, body=%region_3.20_spmd | while | flops 64245064 | bytes 104225968 | solution.py:596
  287.2 18.1 %posterior.2 = f32[1,1,6,1024,1024]{4,3,2,1,0:T(8,128)} custom-call(s32[6]{0:T(128)S(1)} %get-tuple-element.497.tile_tgt, s32[8]{0:T(128)S(1)} %get-tuple-element.498.places, bf16[6,64,768]{2,1,0:T(8,128)(2,1)} %get-tuple-element.499.refs_0_, bf16[6,64,768]{2,1,0:T(8,128)(2,1)} %get-tuple-element.500.refs_1_, ...), custom_call_target="tpu_custom_call" | custom-call | bytes 1024 | tf_op jit(solution)/shard_map/while/body/posterior/pallas_call | solution.py:470
  305.4 777.7 %while.30 = (s32[]{:T(128)}, f32[4,1024]{1,0:T(4,128)S(1)}, f32[4,1024]{1,0:T(4,128)}, f32[6,1024]{1,0:T(8,128)}, s32[6]{0:T(128)S(1)}, /*index=5*/s32[6]{0:T(12...) while((s32[]{:T(128)}, f32[4,1024]{1,0:T(4,128)S(1)}, ...), condition=%wide.region_19.19_spmd.clone, body=%wide.region_4.18_spmd.clone.sunk | while | flops 64245064 | bytes 103953936 | solution.py:71
  320.1 11.0 exponential_reduce_fusion.4
  339.4 23.9 %pmax.20 = f32[4,1024]{1,0:T(4,128)S(1)} all-reduce(f32[4,1024]{1,0:T(4,128)S(1)} %select_reduce_fusion.13), channel_id=1, replica_groups=mesh['src'=16,'tgt'=8] {'tgt'}, use_global_device_ids=true, to_apply=%region_8.7 | all-reduce | flops 4096 | bytes 32768 | tf_op jit(solution)/shard_map/while/body/while/body/eval_jaxpr/pmax | solution.py:54
  363.5 23.6 %psum.20 = f32[4,1024]{1,0:T(4,128)S(1)} all-reduce(f32[4,1024]{1,0:T(4,128)S(1)} %exponential_multiply_fusion.4), channel_id=1, replica_groups=mesh['src'=16,'tgt'=8] {'tgt'}, use_global_device_ids=true, to_apply=%region_12.11 | all-reduce | flops 4096 | bytes 32768 | tf_op jit(solution)/shard_map/while/body/while/body/eval_jaxpr/psum | solution.py:55
  403.7 9.4 add_reduce_fusion.5
  413.1 10.6 exponential_reduce_fusion.5
  423.9 71.2 %pmax.21 = f32[4,1024]{1,0:T(4,128)S(1)} all-reduce(f32[4,1024]{1,0:T(4,128)S(1)} %select_reduce_fusion.16), channel_id=1, replica_groups=mesh['src'=16,'tgt'=8] {'src'}, use_global_device_ids=true, to_apply=%region_15.14 | all-reduce | flops 4096 | bytes 32768 | tf_op jit(solution)/shard_map/while/body/while/body/eval_jaxpr/pmax | solution.py:62
  495.2 69.6 %psum.21 = f32[4,1024]{1,0:T(4,128)S(1)} all-reduce(f32[4,1024]{1,0:T(4,128)S(1)} %exponential_multiply_fusion.5), channel_id=1, replica_groups=mesh['src'=16,'tgt'=8] {'src'}, use_global_device_ids=true, to_apply=%region_18.17 | all-reduce | flops 4096 | bytes 32768 | tf_op jit(solution)/shard_map/while/body/while/body/eval_jaxpr/psum | solution.py:63
  579.3 11.0 exponential_reduce_fusion.4
  598.6 23.9 %pmax.20 = f32[4,1024]{1,0:T(4,128)S(1)} all-reduce(f32[4,1024]{1,0:T(4,128)S(1)} %select_reduce_fusion.13), channel_id=1, replica_groups=mesh['src'=16,'tgt'=8] {'tgt'}, use_global_device_ids=true, to_apply=%region_8.7 | all-reduce | flops 4096 | bytes 32768 | tf_op jit(solution)/shard_map/while/body/while/body/eval_jaxpr/pmax | solution.py:54
  622.7 23.6 %psum.20 = f32[4,1024]{1,0:T(4,128)S(1)} all-reduce(f32[4,1024]{1,0:T(4,128)S(1)} %exponential_multiply_fusion.4), channel_id=1, replica_groups=mesh['src'=16,'tgt'=8] {'tgt'}, use_global_device_ids=true, to_apply=%region_12.11 | all-reduce | flops 4096 | bytes 32768 | tf_op jit(solution)/shard_map/while/body/while/body/eval_jaxpr/psum | solution.py:55
  672.3 10.6 exponential_reduce_fusion.5
  683.0 71.2 %pmax.21 = f32[4,1024]{1,0:T(4,128)S(1)} all-reduce(f32[4,1024]{1,0:T(4,128)S(1)} %select_reduce_fusion.16), channel_id=1, replica_groups=mesh['src'=16,'tgt'=8] {'src'}, use_global_device_ids=true, to_apply=%region_15.14 | all-reduce | flops 4096 | bytes 32768 | tf_op jit(solution)/shard_map/while/body/while/body/eval_jaxpr/pmax | solution.py:62
  754.4 69.6 %psum.21 = f32[4,1024]{1,0:T(4,128)S(1)} all-reduce(f32[4,1024]{1,0:T(4,128)S(1)} %exponential_multiply_fusion.5), channel_id=1, replica_groups=mesh['src'=16,'tgt'=8] {'src'}, use_global_device_ids=true, to_apply=%region_18.17 | all-reduce | flops 4096 | bytes 32768 | tf_op jit(solution)/shard_map/while/body/while/body/eval_jaxpr/psum | solution.py:63
  838.5 11.0 exponential_reduce_fusion.4
  857.8 23.9 %pmax.20 = f32[4,1024]{1,0:T(4,128)S(1)} all-reduce(f32[4,1024]{1,0:T(4,128)S(1)} %select_reduce_fusion.13), channel_id=1, replica_groups=mesh['src'=16,'tgt'=8] {'tgt'}, use_global_device_ids=true, to_apply=%region_8.7 | all-reduce | flops 4096 | bytes 32768 | tf_op jit(solution)/shard_map/while/body/while/body/eval_jaxpr/pmax | solution.py:54
  881.8 23.6 %psum.20 = f32[4,1024]{1,0:T(4,128)S(1)} all-reduce(f32[4,1024]{1,0:T(4,128)S(1)} %exponential_multiply_fusion.4), channel_id=1, replica_groups=mesh['src'=16,'tgt'=8] {'tgt'}, use_global_device_ids=true, to_apply=%region_12.11 | all-reduce | flops 4096 | bytes 32768 | tf_op jit(solution)/shard_map/while/body/while/body/eval_jaxpr/psum | solution.py:55
  931.5 10.6 exponential_reduce_fusion.5
  942.2 71.2 %pmax.21 = f32[4,1024]{1,0:T(4,128)S(1)} all-reduce(f32[4,1024]{1,0:T(4,128)S(1)} %select_reduce_fusion.16), channel_id=1, replica_groups=mesh['src'=16,'tgt'=8] {'src'}, use_global_device_ids=true, to_apply=%region_15.14 | all-reduce | flops 4096 | bytes 32768 | tf_op jit(solution)/shard_map/while/body/while/body/eval_jaxpr/pmax | solution.py:62
  1013.5 69.6 %psum.21 = f32[4,1024]{1,0:T(4,128)S(1)} all-reduce(f32[4,1024]{1,0:T(4,128)S(1)} %exponential_multiply_fusion.5), channel_id=1, replica_groups=mesh['src'=16,'tgt'=8] {'src'}, use_global_device_ids=true, to_apply=%region_18.17 | all-reduce | flops 4096 | bytes 32768 | tf_op jit(solution)/shard_map/while/body/while/body/eval_jaxpr/psum | solution.py:63
  1083.7 18.3 %posterior.3 = f32[1,1,6,1024,1024]{4,3,2,1,0:T(8,128)} custom-call(s32[6]{0:T(128)S(1)} %get-tuple-element.600, s32[8]{0:T(128)S(1)} %get-tuple-element.598, bf16[6,64,768]{2,1,0:T(8,128)(2,1)} %get-tuple-element.544, bf16[6,64,768]{2,1,0:T(8,128)(2,1)} %get-tuple-element.555, bf16[6,64,768]{2,1,0:T(8,128)(2,1)} %get-tuple-element.547, ...), custom_call_target="tpu_custom_call" | custom-call | bytes 1024 | tf_op jit(solution)/shard_map/posterior/pallas_call | solution.py:470
  (355 shorter events, 278.5 us)
Async XLA Ops:
  7.2 57.4 %all-gather.4.cloned.1.call-start = ((), (), s32[]{:S(2)}) async-start(), calls=%async_computation.10 | async-start | bytes 7077888 | tf_op jit(solution)/shard_map/all_gather | solution.py:536
  24.1 20.8 %collective-permute-start.3 = (bf16[4,2,64,768]{3,2,1,0:T(8,128)(2,1)S(1)}, bf16[4,2,64,768]{3,2,1,0:T(8,128)(2,1)S(1)}, u32[]{:S(2)}, u32[]{:S(2)}) collective-permute-start(bf16[4,2,64,768]{3,2,1,0:T(8,128)(2,1)S(1)} %pad_maximum_fusion.refs_2_.refs_0_), channel_id=1, source_target_pairs={{0,8},{8,16},{16,24},{24,0},{32,40},{40,48},{48,56},{56,32},{64,72... | collective-permute-start | bytes 2359304 | tf_op jit(solution)/shard_map/ppermute | solution.py:500
  25.7 19.6 %collective-permute-start.5 = (bf16[4,2,64,768]{3,2,1,0:T(8,128)(2,1)S(1)}, bf16[4,2,64,768]{3,2,1,0:T(8,128)(2,1)S(1)}, u32[]{:S(2)}, u32[]{:S(2)}) collective-permute-start(bf16[4,2,64,768]{3,2,1,0:T(8,128)(2,1)S(1)} %pad_maximum_fusion.refs_2_.refs_0_), channel_id=1, source_target_pairs={{0,24},{8,0},{16,8},{24,16},{32,56},{40,32},{48,40},{56,48},{64,88... | collective-permute-start | bytes 2359304 | tf_op jit(solution)/shard_map/ppermute | solution.py:500
  27.9 21.1 %collective-permute-start.10 = (bf16[4,2,64,768]{3,2,1,0:T(8,128)(2,1)S(1)}, bf16[4,2,64,768]{3,2,1,0:T(8,128)(2,1)}, u32[]{:S(2)}, u32[]{:S(2)}) collective-permute-start(bf16[4,2,64,768]{3,2,1,0:T(8,128)(2,1)S(1)} %pad_maximum_fusion.1.refs_7_.refs_5_), channel_id=1, source_target_pairs={{0,32},{8,40},{16,48},{24,56},{32,64},{40,72},{48,80},{56,88},{64,... | collective-permute-start | bytes 2359304 | tf_op jit(solution)/shard_map/ppermute | solution.py:500
  30.2 22.2 %collective-permute-start.12 = (bf16[4,2,64,768]{3,2,1,0:T(8,128)(2,1)S(1)}, bf16[4,2,64,768]{3,2,1,0:T(8,128)(2,1)}, u32[]{:S(2)}, u32[]{:S(2)}) collective-permute-start(bf16[4,2,64,768]{3,2,1,0:T(8,128)(2,1)S(1)} %pad_maximum_fusion.1.refs_7_.refs_5_), channel_id=1, source_target_pairs={{0,96},{8,104},{16,112},{24,120},{32,0},{40,8},{48,16},{56,24},{64... | collective-permute-start | bytes 2359304 | tf_op jit(solution)/shard_map/ppermute | solution.py:500
  34.7 21.2 %all-to-all-start.3 = ((s32[16,1,128]{2,1,0:T(1,128)}), s32[16,1,128]{2,1,0:T(1,128)S(1)}, u32[]{:S(2)}, u32[]{:S(2)}) async-start(s32[16,1,128]{2,1,0:T(1,128)} %broadcast_in_dim.253), calls=%async_computation.3 | async-start | bytes 16384 | tf_op jit(solution)/shard_map/all_to_all | solution.py:490
  39.4 88.1 %all-gather.6.cloned.1.call-start = ((), (), s32[]{:S(2)}) async-start(), calls=%async_computation.11 | async-start | bytes 6684672 | tf_op jit(solution)/shard_map/all_gather | solution.py:555
  44.9 13.9 %collective-permute-start.4 = (bf16[2,2,64,768]{3,2,1,0:T(8,128)(2,1)S(1)}, bf16[2,2,64,768]{3,2,1,0:T(8,128)(2,1)}, u32[]{:S(2)}, u32[]{:S(2)}) collective-permute-start(bf16[2,2,64,768]{3,2,1,0:T(8,128)(2,1)S(1)} %slice.59), channel_id=1, source_target_pairs={{0,8},{8,16},{16,24},{24,0},{32,40},{40,48},{48,56},{56,32},{64,72... | collective-permute-start | bytes 1179656 | tf_op jit(solution)/shard_map/ppermute | solution.py:500
  66.7 138.3 %all-gather.8.cloned.1.call-start = ((), (), s32[]{:S(2)}) async-start(), calls=%async_computation.12 | async-start | bytes 6684672 | tf_op jit(solution)/shard_map/all_gather | solution.py:555
  130.9 46.1 %collective-permute-start.14 = (bf16[6,64,768]{2,1,0:T(8,128)(2,1)S(1)}, bf16[6,64,768]{2,1,0:T(8,128)(2,1)S(1)}, u32[]{:S(2)}, u32[]{:S(2)}) collective-permute-start(bf16[6,64,768]{2,1,0:T(8,128)(2,1)S(1)} %get-tuple-element.220.refs_1_), channel_id=1, source_target_pairs={{0,2},{1,3},{2,4},{3,5},{4,6},{5,7},{6,0},{7,1},{8,10},{9,11},{10,... | collective-permute-start | bytes 1769480 | tf_op jit(solution)/shard_map/ppermute | solution.py:532
  132.6 44.4 %collective-permute-start.15 = (bf16[6,64,768]{2,1,0:T(8,128)(2,1)S(1)}, bf16[6,64,768]{2,1,0:T(8,128)(2,1)S(1)}, u32[]{:S(2)}, u32[]{:S(2)}) collective-permute-start(bf16[6,64,768]{2,1,0:T(8,128)(2,1)S(1)} %get-tuple-element.221.refs_2_), channel_id=1, source_target_pairs={{0,6},{1,7},{2,0},{3,1},{4,2},{5,3},{6,4},{7,5},{8,14},{9,15},{10,... | collective-permute-start | bytes 1769480 | tf_op jit(solution)/shard_map/ppermute | solution.py:532
  134.2 42.8 %collective-permute-start.16 = (bf16[6,64,768]{2,1,0:T(8,128)(2,1)S(1)}, bf16[6,64,768]{2,1,0:T(8,128)(2,1)S(1)}, u32[]{:S(2)}, u32[]{:S(2)}) collective-permute-start(bf16[6,64,768]{2,1,0:T(8,128)(2,1)S(1)} %get-tuple-element.222.refs_3_), channel_id=1, source_target_pairs={{0,3},{1,2},{2,5},{3,4},{4,7},{5,6},{6,1},{7,0},{8,11},{9,10},{10,... | collective-permute-start | bytes 1769480 | tf_op jit(solution)/shard_map/ppermute | solution.py:532
  134.4 42.6 %collective-permute-start.17 = (bf16[6,64,768]{2,1,0:T(8,128)(2,1)S(1)}, bf16[6,64,768]{2,1,0:T(8,128)(2,1)S(1)}, u32[]{:S(2)}, u32[]{:S(2)}) collective-permute-start(bf16[6,64,768]{2,1,0:T(8,128)(2,1)S(1)} %get-tuple-element.223.refs_4_), channel_id=1, source_target_pairs={{0,7},{1,6},{2,1},{3,0},{4,3},{5,2},{6,5},{7,4},{8,15},{9,14},{10,... | collective-permute-start | bytes 1769480 | tf_op jit(solution)/shard_map/ppermute | solution.py:532
  137.3 39.7 %collective-permute-start.18 = (bf16[6,64,768]{2,1,0:T(8,128)(2,1)S(1)}, bf16[6,64,768]{2,1,0:T(8,128)(2,1)}, u32[]{:S(2)}, u32[]{:S(2)}) collective-permute-start(bf16[6,64,768]{2,1,0:T(8,128)(2,1)S(1)} %get-tuple-element.224.refs_5_), channel_id=1, source_target_pairs={{0,4},{1,5},{2,6},{3,7},{4,0},{5,1},{6,2},{7,3},{8,12},{9,13},{10,... | collective-permute-start | bytes 1769480 | tf_op jit(solution)/shard_map/ppermute | solution.py:532
  191.9 45.8 %collective-permute-start.19 = (bf16[6,64,768]{2,1,0:T(8,128)(2,1)S(1)}, bf16[6,64,768]{2,1,0:T(8,128)(2,1)S(1)}, u32[]{:S(2)}, u32[]{:S(2)}) collective-permute-start(bf16[6,64,768]{2,1,0:T(8,128)(2,1)S(1)} %get-tuple-element.225.refs_0_), channel_id=1, source_target_pairs={{0,1},{1,0},{2,3},{3,2},{4,5},{5,4},{6,7},{7,6},{8,9},{9,8},{10,11... | collective-permute-start | bytes 1769480 | tf_op jit(solution)/shard_map/ppermute | solution.py:532
  192.0 45.7 %collective-permute-start.20 = (bf16[6,64,768]{2,1,0:T(8,128)(2,1)S(1)}, bf16[6,64,768]{2,1,0:T(8,128)(2,1)S(1)}, u32[]{:S(2)}, u32[]{:S(2)}) collective-permute-start(bf16[6,64,768]{2,1,0:T(8,128)(2,1)S(1)} %get-tuple-element.226.refs_1_), channel_id=1, source_target_pairs={{0,5},{1,4},{2,7},{3,6},{4,1},{5,0},{6,3},{7,2},{8,13},{9,12},{10,... | collective-permute-start | bytes 1769480 | tf_op jit(solution)/shard_map/ppermute | solution.py:532
  207.8 29.9 %collective-permute-start.21 = (bf16[6,64,768]{2,1,0:T(8,128)(2,1)S(1)}, bf16[6,64,768]{2,1,0:T(8,128)(2,1)S(1)}, u32[]{:S(2)}, u32[]{:S(2)}) collective-permute-start(bf16[6,64,768]{2,1,0:T(8,128)(2,1)S(1)} %get-tuple-element.228.refs_3_), channel_id=1, source_target_pairs={{0,2},{1,3},{2,4},{3,5},{4,6},{5,7},{6,0},{7,1},{8,10},{9,11},{10,... | collective-permute-start | bytes 1769480 | tf_op jit(solution)/shard_map/ppermute | solution.py:532
  209.1 28.7 %collective-permute-start.22 = (bf16[6,64,768]{2,1,0:T(8,128)(2,1)S(1)}, bf16[6,64,768]{2,1,0:T(8,128)(2,1)S(1)}, u32[]{:S(2)}, u32[]{:S(2)}) collective-permute-start(bf16[6,64,768]{2,1,0:T(8,128)(2,1)S(1)} %get-tuple-element.229.refs_4_), channel_id=1, source_target_pairs={{0,6},{1,7},{2,0},{3,1},{4,2},{5,3},{6,4},{7,5},{8,14},{9,15},{10,... | collective-permute-start | bytes 1769480 | tf_op jit(solution)/shard_map/ppermute | solution.py:532
  211.1 28.3 %collective-permute-start.23 = (bf16[6,64,768]{2,1,0:T(8,128)(2,1)S(1)}, bf16[6,64,768]{2,1,0:T(8,128)(2,1)}, u32[]{:S(2)}, u32[]{:S(2)}) collective-permute-start(bf16[6,64,768]{2,1,0:T(8,128)(2,1)S(1)} %get-tuple-element.230.refs_5_), channel_id=1, source_target_pairs={{0,4},{1,5},{2,6},{3,7},{4,0},{5,1},{6,2},{7,3},{8,12},{9,13},{10,... | collective-permute-start | bytes 1769480 | tf_op jit(solution)/shard_map/ppermute | solution.py:532
  253.2 34.0 %collective-permute-start.24 = (bf16[6,64,768]{2,1,0:T(8,128)(2,1)S(1)}, bf16[6,64,768]{2,1,0:T(8,128)(2,1)}, u32[]{:S(2)}, u32[]{:S(2)}) collective-permute-start(bf16[6,64,768]{2,1,0:T(8,128)(2,1)S(1)} %get-tuple-element.231.refs_0_), channel_id=1, source_target_pairs={{0,1},{1,0},{2,3},{3,2},{4,5},{5,4},{6,7},{7,6},{8,9},{9,8},{10,11... | collective-permute-start | bytes 1769480 | tf_op jit(solution)/shard_map/ppermute | solution.py:532
  253.3 33.9 %collective-permute-start.25 = (bf16[6,64,768]{2,1,0:T(8,128)(2,1)S(1)}, bf16[6,64,768]{2,1,0:T(8,128)(2,1)}, u32[]{:S(2)}, u32[]{:S(2)}) collective-permute-start(bf16[6,64,768]{2,1,0:T(8,128)(2,1)S(1)} %get-tuple-element.232.refs_1_), channel_id=1, source_target_pairs={{0,3},{1,2},{2,5},{3,4},{4,7},{5,6},{6,1},{7,0},{8,11},{9,10},{10,... | collective-permute-start | bytes 1769480 | tf_op jit(solution)/shard_map/ppermute | solution.py:532
  253.9 33.2 %collective-permute-start.26 = (bf16[6,64,768]{2,1,0:T(8,128)(2,1)S(1)}, bf16[6,64,768]{2,1,0:T(8,128)(2,1)}, u32[]{:S(2)}, u32[]{:S(2)}) collective-permute-start(bf16[6,64,768]{2,1,0:T(8,128)(2,1)S(1)} %get-tuple-element.233.refs_3_), channel_id=1, source_target_pairs={{0,5},{1,4},{2,7},{3,6},{4,1},{5,0},{6,3},{7,2},{8,13},{9,12},{10,... | collective-permute-start | bytes 1769480 | tf_op jit(solution)/shard_map/ppermute | solution.py:532
  255.7 31.5 %collective-permute-start.27 = (bf16[6,64,768]{2,1,0:T(8,128)(2,1)S(1)}, bf16[6,64,768]{2,1,0:T(8,128)(2,1)}, u32[]{:S(2)}, u32[]{:S(2)}) collective-permute-start(bf16[6,64,768]{2,1,0:T(8,128)(2,1)S(1)} %get-tuple-element.234.refs_2_), channel_id=1, source_target_pairs={{0,7},{1,6},{2,1},{3,0},{4,3},{5,2},{6,5},{7,4},{8,15},{9,14},{10,... | collective-permute-start | bytes 1769480 | tf_op jit(solution)/shard_map/ppermute | solution.py:532
  316.4 15.7 %all-to-all-start = ((f32[16,1,1024]{2,1,0:T(1,128)}), f32[16,1,1024]{2,1,0:T(1,128)S(1)}, u32[]{:S(2)}, u32[]{:S(2)}) async-start(f32[16,1,1024]{2,1,0:T(1,128)} %copy.30), calls=%async_computation | async-start | bytes 131072 | tf_op jit(solution)/shard_map/while/body/while/body/eval_jaxpr/all_to_all | solution.py:490
  332.1 31.2 %all-to-all-start.1 = ((f32[16,1,1024]{2,1,0:T(1,128)}), f32[16,1,1024]{2,1,0:T(1,128)S(1)}, u32[]{:S(2)}, u32[]{:S(2)}) async-start(f32[16,1,1024]{2,1,0:T(1,128)} %copy.32), calls=%async_computation.1 | async-start | bytes 131072 | tf_op jit(solution)/shard_map/while/body/while/body/eval_jaxpr/all_to_all | solution.py:490
  388.4 14.6 %all-to-all-start.2 = ((f32[16,1,1024]{2,1,0:T(1,128)}), f32[16,1,1024]{2,1,0:T(1,128)S(1)}, u32[]{:S(2)}, u32[]{:S(2)}) async-start(f32[16,1,1024]{2,1,0:T(1,128)} %copy.34), calls=%async_computation.2 | async-start | bytes 131072 | tf_op jit(solution)/shard_map/while/body/while/body/eval_jaxpr/all_to_all | solution.py:490
  575.8 15.5 %all-to-all-start = ((f32[16,1,1024]{2,1,0:T(1,128)}), f32[16,1,1024]{2,1,0:T(1,128)S(1)}, u32[]{:S(2)}, u32[]{:S(2)}) async-start(f32[16,1,1024]{2,1,0:T(1,128)} %copy.30), calls=%async_computation | async-start | bytes 131072 | tf_op jit(solution)/shard_map/while/body/while/body/eval_jaxpr/all_to_all | solution.py:490
  591.3 31.2 %all-to-all-start.1 = ((f32[16,1,1024]{2,1,0:T(1,128)}), f32[16,1,1024]{2,1,0:T(1,128)S(1)}, u32[]{:S(2)}, u32[]{:S(2)}) async-start(f32[16,1,1024]{2,1,0:T(1,128)} %copy.32), calls=%async_computation.1 | async-start | bytes 131072 | tf_op jit(solution)/shard_map/while/body/while/body/eval_jaxpr/all_to_all | solution.py:490
  647.6 14.6 %all-to-all-start.2 = ((f32[16,1,1024]{2,1,0:T(1,128)}), f32[16,1,1024]{2,1,0:T(1,128)S(1)}, u32[]{:S(2)}, u32[]{:S(2)}) async-start(f32[16,1,1024]{2,1,0:T(1,128)} %copy.34), calls=%async_computation.2 | async-start | bytes 131072 | tf_op jit(solution)/shard_map/while/body/while/body/eval_jaxpr/all_to_all | solution.py:490
  835.0 15.5 %all-to-all-start = ((f32[16,1,1024]{2,1,0:T(1,128)}), f32[16,1,1024]{2,1,0:T(1,128)S(1)}, u32[]{:S(2)}, u32[]{:S(2)}) async-start(f32[16,1,1024]{2,1,0:T(1,128)} %copy.30), calls=%async_computation | async-start | bytes 131072 | tf_op jit(solution)/shard_map/while/body/while/body/eval_jaxpr/all_to_all | solution.py:490
  850.5 31.2 %all-to-all-start.1 = ((f32[16,1,1024]{2,1,0:T(1,128)}), f32[16,1,1024]{2,1,0:T(1,128)S(1)}, u32[]{:S(2)}, u32[]{:S(2)}) async-start(f32[16,1,1024]{2,1,0:T(1,128)} %copy.32), calls=%async_computation.1 | async-start | bytes 131072 | tf_op jit(solution)/shard_map/while/body/while/body/eval_jaxpr/all_to_all | solution.py:490
  906.8 14.6 %all-to-all-start.2 = ((f32[16,1,1024]{2,1,0:T(1,128)}), f32[16,1,1024]{2,1,0:T(1,128)S(1)}, u32[]{:S(2)}, u32[]{:S(2)}) async-start(f32[16,1,1024]{2,1,0:T(1,128)} %copy.34), calls=%async_computation.2 | async-start | bytes 131072 | tf_op jit(solution)/shard_map/while/body/while/body/eval_jaxpr/all_to_all | solution.py:490
  (65 other events, 1396.8 us)
Sparse Core Ops, SparseCore 0:
  9.7 43.5 all-gather.3
  66.8 60.6 all-gather.5
  129.6 60.8 all-gather.7

commit v5 on v4

--- a/solution.py
+++ b/solution.py
@@ -345,7 +345,7 @@
         out_shape=jax.ShapeDtypeStruct((copies,) + x.shape[1:], x.dtype),
         cost_estimate=LIGHT,
         name="gate",
-    )(x, *far(after))
+    )(x, *after)
 
 
 def potentials_kernel(homes, row_ref, col_ref, row_pot, column_pot, tile_row):
@@ -591,7 +591,7 @@
         potentials = log_domain(scores, tile_home, tile_tgt, plan_column, src_blocks, tgt_blocks)
         return (jnp.zeros((), jnp.bool_),) + potentials
 
-    out_of_range = jnp.isnan(row_pot[0, 0])
+    out_of_range = jnp.isnan(jnp.sum(row_gathered[:, 0, 0, 0]))
     carry = (out_of_range, column_pot, row_pot, tile_row)
     _, column_pot, row_pot, tile_row = lax.while_loop(unfinished, redo, carry)
     log_post = posterior(pieces, places, targets, tile_row, column_pot, tile_tgt)

time: 1120 us -> 1120 us (level)
  no operation moved by 1% of the time
where the time goes in v5:
time: 1120 us; the launch traced here: 1110 us
  blocking collectives  591 us (53%)
  Pallas kernels  156 us (14%)
  other arithmetic  131 us (12%)
  starting transfers between devices  117 us (10%)
  waiting for transfers between devices  66.1 us (6%)
  local copies, waits for them, and re-layouts  29.9 us (3%)
  between operations  16.1 us (1%)
    pmax x3, blocking collectives, iterate(): largest = lax.pmax(local_max, 'src')  214 us
    psum x3, blocking collectives, iterate(): summed = lax.psum(local_sum * jnp.exp(local_max - largest), 'src')  209 us
    all_to_all x14, starting transfers between devices, swap(): return lax.all_to_all(x, axis, split_axis=0, concat_axis=0, tiled=True)  75.3 us
    pmax x3, blocking collectives, iterate(): largest = lax.pmax(local_max, 'tgt')  71.5 us
    psum x3, blocking collectives, iterate(): summed = lax.psum(local_sum * jnp.exp(local_max - largest), 'tgt')  70.7 us
    pallas_call x5, Pallas kernels, weighted_sums(): pl.pallas_call(kernel, in_specs=[WHOLE, WHOLE, ANYWHERE] + [SCALARS] * la...  60.8 us
    all_to_all x14, waiting for transfers between devices, swap(): return lax.all_to_all(x, axis, split_axis=0, concat_axis=0, tiled=True)  43.5 us
    pallas_call x1, Pallas kernels, score_weights(): pl.pallas_call(functools.partial(scores_kernel, 2.0 / math.sqrt(depth) *...  41.7 us
  transfers between devices with their start and end apart: 45, of which 14 were waited for; matrix products, arithmetic and copies ran while one was open for 5% of the time, Pallas kernels for 10%

profile of v5, /device:TPU:0, one launch (start us, length us, event | category | flops | bytes accessed | tf_op | source)
XLA Modules:
  0.0 1107.9 jit_solution(14148224842325176580)
XLA Ops:
  70.8 41.7 %score_weights.1 = (bf16[4096,4096]{1,0:T(8,128)(2,1)}, f32[8,5,1,1024]{3,2,1,0:T(1,128)}, f32[4,1,1024]{2,1,0:T(1,128)S(1)}, bf16[4,1024,768]{2,1,0:T(8,128)(2,1)}) custom-call(s32[4,4]{1,0:T(4,128)S(1)} %copy-done.18, s32[2]{0:T(128)S(1)} %pad_add_fusion.1.where, f32[1,1024]{1,0:T(1,128)S(1)} %bitcast.80, ...), custom_call_target="tpu_custom_call" | custom-call | bytes 1024 | tf_op jit(solution)/shard_map/score_weights/pallas_call | solution.py:206
  139.8 12.0 %column_sums.3 = f32[16,4,1,1024]{3,2,1,0:T(1,128)S(1)} custom-call(f32[8,5,1,1024]{3,2,1,0:T(1,128)S(1)} %all-to-all-done.4.first.g_ref, f32[4,1,1024]{2,1,0:T(1,128)S(1)} %get-tuple-element.218.ratio, bf16[4096,4096]{1,0:T(8,128)(2,1)} %get-tuple-element.219.k_hbm, bf16[6,64,768]{2,1,0:T(8,128)(2,1)} %get-tuple-element.449.refs_0_, ...), custom_call_target="tpu_custom_call" | custom-call | bytes 1024 | tf_op jit(solution)/shard_map/column_sums/pallas_call | solution.py:302
  151.8 13.9 %all_to_all.71.g_ref = f32[16,4,1,1024]{3,2,1,0:T(1,128)S(1)} all-to-all(f32[16,4,1,1024]{3,2,1,0:T(1,128)S(1)} %column_sums.3), channel_id=1, replica_groups=mesh['src'=16,'tgt'=8] {'src'}, dimensions={0} | all-to-all | bytes 524288 | tf_op jit(solution)/shard_map/all_to_all | solution.py:490
  165.7 12.4 %row_sums.2.x_ref = f32[1,4,1,1024]{3,2,1,0:T(1,128)S(1)} custom-call(f32[16,4,1,1024]{3,2,1,0:T(1,128)S(1)} %all_to_all.71.g_ref, f32[4,1,1024]{2,1,0:T(1,128)S(1)} %get-tuple-element.218.ratio, bf16[4096,4096]{1,0:T(8,128)(2,1)} %get-tuple-element.219.k_hbm, bf16[6,64,768]{2,1,0:T(8,128)(2,1)} %get-tuple-element.449.refs_0_, ...), custom_call_target="tpu_custom_call" | custom-call | bytes 1024 | tf_op jit(solution)/shard_map/row_sums/pallas_call | solution.py:302
  194.4 11.6 %column_sums.4.first = f32[16,4,1,1024]{3,2,1,0:T(1,128)S(1)} custom-call(f32[8,4,1,1024]{3,2,1,0:T(1,128)S(1)} %all-to-all-done.6.first.g_ref, f32[4,1,1024]{2,1,0:T(1,128)S(1)} %get-tuple-element.218.ratio, bf16[4096,4096]{1,0:T(8,128)(2,1)} %get-tuple-element.219.k_hbm, bf16[6,64,768]{2,1,0:T(8,128)(2,1)} %copy-done.4, bf16[6,64,768]{2,1,0:T(8,128)(2,1)} %copy-done.2), custom_call_target="tpu_custom_call" | custom-call | bytes 1024 | tf_op jit(solution)/shard_map/column_sums/pallas_call | solution.py:302
  213.3 12.5 %all_to_all.72.g_ref = f32[16,4,1,1024]{3,2,1,0:T(1,128)S(1)} all-to-all(f32[16,4,1,1024]{3,2,1,0:T(1,128)S(1)} %column_sums.4.first), channel_id=1, replica_groups=mesh['src'=16,'tgt'=8] {'src'}, dimensions={0} | all-to-all | bytes 524288 | tf_op jit(solution)/shard_map/all_to_all | solution.py:490
  225.8 12.0 %row_sums.3.x_ref = f32[1,4,1,1024]{3,2,1,0:T(1,128)S(1)} custom-call(f32[16,4,1,1024]{3,2,1,0:T(1,128)S(1)} %all_to_all.72.g_ref, f32[4,1,1024]{2,1,0:T(1,128)S(1)} %get-tuple-element.218.ratio, bf16[4096,4096]{1,0:T(8,128)(2,1)} %get-tuple-element.219.k_hbm, bf16[6,64,768]{2,1,0:T(8,128)(2,1)} %copy-done.4, bf16[6,64,768]{2,1,0:T(8,128)(2,1)} %copy-done.2, ...), custom_call_target="tpu_custom_call" | custom-call | bytes 1024 | tf_op jit(solution)/shard_map/row_sums/pallas_call | solution.py:302
  257.3 12.8 %column_sums.5 = f32[16,5,1,1024]{3,2,1,0:T(1,128)} custom-call(f32[8,4,1,1024]{3,2,1,0:T(1,128)S(1)} %all-to-all-done.8.first.g_ref.row_ref, f32[4,1,1024]{2,1,0:T(1,128)S(1)} %get-tuple-element.218.ratio, bf16[4096,4096]{1,0:T(8,128)(2,1)} %get-tuple-element.219.k_hbm, s32[16]{0:T(128)S(1)} %broadcast_select_fusion.3.plan, bf16[6,64,768]{2,1,0:T(8,128)(2,1)} %copy-done.12, ...), custom_call_target="tpu_custom_call" | custom-call | bytes 1024 | tf_op jit(solution)/shard_map/column_sums/pallas_call | solution.py:302
  286.6 796.3 %while.28 = (pred[]{:T(512)}, f32[4,1024]{1,0:T(4,128)}, f32[4,1024]{1,0:T(4,128)}, f32[6,1024]{1,0:T(8,128)}, s32[6]{0:T(128)S(1)}, /*index=5*/s32[8]{0:T(128)S...) while((pred[]{:T(512)}, f32[4,1024]{1,0:T(4,128)}, ...), condition=%region_21.22_spmd, body=%region_4.21_spmd | while | flops 64245064 | bytes 106585304 | solution.py:596
  286.6 18.1 %posterior.2 = f32[1,1,6,1024,1024]{4,3,2,1,0:T(8,128)} custom-call(s32[6]{0:T(128)S(1)} %get-tuple-element.497.tile_tgt, s32[8]{0:T(128)S(1)} %get-tuple-element.498.places, bf16[6,64,768]{2,1,0:T(8,128)(2,1)} %get-tuple-element.569, bf16[6,64,768]{2,1,0:T(8,128)(2,1)} %get-tuple-element.500.refs_1_, bf16[6,64,768]{2,1,0:T(8,128)(2,1)} %get-tuple-element.501.refs_2_, ...), custom_call_target="tpu_custom_call" | custom-call | bytes 1024 | tf_op jit(solution)/shard_map/while/body/posterior/pallas_call | solution.py:470
  304.8 777.4 %while.30 = (s32[]{:T(128)}, f32[4,1024]{1,0:T(4,128)S(1)}, f32[4,1024]{1,0:T(4,128)}, f32[6,1024]{1,0:T(8,128)}, s32[6]{0:T(128)S(1)}, /*index=5*/s32[6]{0:T(12...) while((s32[]{:T(128)}, f32[4,1024]{1,0:T(4,128)S(1)}, ...), condition=%wide.region_20.20_spmd.clone, body=%wide.region_5.19_spmd.clone.sunk | while | flops 64245064 | bytes 103953936 | solution.py:71
  319.4 10.9 exponential_reduce_fusion.4
  338.7 23.9 %pmax.20 = f32[4,1024]{1,0:T(4,128)S(1)} all-reduce(f32[4,1024]{1,0:T(4,128)S(1)} %select_reduce_fusion.13), channel_id=1, replica_groups=mesh['src'=16,'tgt'=8] {'tgt'}, use_global_device_ids=true, to_apply=%region_9.8 | all-reduce | flops 4096 | bytes 32768 | tf_op jit(solution)/shard_map/while/body/while/body/eval_jaxpr/pmax | solution.py:54
  362.8 23.6 %psum.20 = f32[4,1024]{1,0:T(4,128)S(1)} all-reduce(f32[4,1024]{1,0:T(4,128)S(1)} %exponential_multiply_fusion.4), channel_id=1, replica_groups=mesh['src'=16,'tgt'=8] {'tgt'}, use_global_device_ids=true, to_apply=%region_13.12 | all-reduce | flops 4096 | bytes 32768 | tf_op jit(solution)/shard_map/while/body/while/body/eval_jaxpr/psum | solution.py:55
  403.0 9.4 add_reduce_fusion.5
  412.4 10.6 exponential_reduce_fusion.5
  423.2 71.2 %pmax.21 = f32[4,1024]{1,0:T(4,128)S(1)} all-reduce(f32[4,1024]{1,0:T(4,128)S(1)} %select_reduce_fusion.16), channel_id=1, replica_groups=mesh['src'=16,'tgt'=8] {'src'}, use_global_device_ids=true, to_apply=%region_16.15 | all-reduce | flops 4096 | bytes 32768 | tf_op jit(solution)/shard_map/while/body/while/body/eval_jaxpr/pmax | solution.py:62
  494.5 69.6 %psum.21 = f32[4,1024]{1,0:T(4,128)S(1)} all-reduce(f32[4,1024]{1,0:T(4,128)S(1)} %exponential_multiply_fusion.5), channel_id=1, replica_groups=mesh['src'=16,'tgt'=8] {'src'}, use_global_device_ids=true, to_apply=%region_19.18 | all-reduce | flops 4096 | bytes 32768 | tf_op jit(solution)/shard_map/while/body/while/body/eval_jaxpr/psum | solution.py:63
  578.5 10.9 exponential_reduce_fusion.4
  597.8 23.9 %pmax.20 = f32[4,1024]{1,0:T(4,128)S(1)} all-reduce(f32[4,1024]{1,0:T(4,128)S(1)} %select_reduce_fusion.13), channel_id=1, replica_groups=mesh['src'=16,'tgt'=8] {'tgt'}, use_global_device_ids=true, to_apply=%region_9.8 | all-reduce | flops 4096 | bytes 32768 | tf_op jit(solution)/shard_map/while/body/while/body/eval_jaxpr/pmax | solution.py:54
  621.9 23.6 %psum.20 = f32[4,1024]{1,0:T(4,128)S(1)} all-reduce(f32[4,1024]{1,0:T(4,128)S(1)} %exponential_multiply_fusion.4), channel_id=1, replica_groups=mesh['src'=16,'tgt'=8] {'tgt'}, use_global_device_ids=true, to_apply=%region_13.12 | all-reduce | flops 4096 | bytes 32768 | tf_op jit(solution)/shard_map/while/body/while/body/eval_jaxpr/psum | solution.py:55
  662.1 9.4 add_reduce_fusion.5
  671.5 10.6 exponential_reduce_fusion.5
  682.2 71.2 %pmax.21 = f32[4,1024]{1,0:T(4,128)S(1)} all-reduce(f32[4,1024]{1,0:T(4,128)S(1)} %select_reduce_fusion.16), channel_id=1, replica_groups=mesh['src'=16,'tgt'=8] {'src'}, use_global_device_ids=true, to_apply=%region_16.15 | all-reduce | flops 4096 | bytes 32768 | tf_op jit(solution)/shard_map/while/body/while/body/eval_jaxpr/pmax | solution.py:62
  753.6 69.6 %psum.21 = f32[4,1024]{1,0:T(4,128)S(1)} all-reduce(f32[4,1024]{1,0:T(4,128)S(1)} %exponential_multiply_fusion.5), channel_id=1, replica_groups=mesh['src'=16,'tgt'=8] {'src'}, use_global_device_ids=true, to_apply=%region_19.18 | all-reduce | flops 4096 | bytes 32768 | tf_op jit(solution)/shard_map/while/body/while/body/eval_jaxpr/psum | solution.py:63
  837.6 10.9 exponential_reduce_fusion.4
  856.9 23.9 %pmax.20 = f32[4,1024]{1,0:T(4,128)S(1)} all-reduce(f32[4,1024]{1,0:T(4,128)S(1)} %select_reduce_fusion.13), channel_id=1, replica_groups=mesh['src'=16,'tgt'=8] {'tgt'}, use_global_device_ids=true, to_apply=%region_9.8 | all-reduce | flops 4096 | bytes 32768 | tf_op jit(solution)/shard_map/while/body/while/body/eval_jaxpr/pmax | solution.py:54
  881.0 23.6 %psum.20 = f32[4,1024]{1,0:T(4,128)S(1)} all-reduce(f32[4,1024]{1,0:T(4,128)S(1)} %exponential_multiply_fusion.4), channel_id=1, replica_groups=mesh['src'=16,'tgt'=8] {'tgt'}, use_global_device_ids=true, to_apply=%region_13.12 | all-reduce | flops 4096 | bytes 32768 | tf_op jit(solution)/shard_map/while/body/while/body/eval_jaxpr/psum | solution.py:55
  930.6 10.6 exponential_reduce_fusion.5
  941.3 71.2 %pmax.21 = f32[4,1024]{1,0:T(4,128)S(1)} all-reduce(f32[4,1024]{1,0:T(4,128)S(1)} %select_reduce_fusion.16), channel_id=1, replica_groups=mesh['src'=16,'tgt'=8] {'src'}, use_global_device_ids=true, to_apply=%region_16.15 | all-reduce | flops 4096 | bytes 32768 | tf_op jit(solution)/shard_map/while/body/while/body/eval_jaxpr/pmax | solution.py:62
  1012.6 69.6 %psum.21 = f32[4,1024]{1,0:T(4,128)S(1)} all-reduce(f32[4,1024]{1,0:T(4,128)S(1)} %exponential_multiply_fusion.5), channel_id=1, replica_groups=mesh['src'=16,'tgt'=8] {'src'}, use_global_device_ids=true, to_apply=%region_19.18 | all-reduce | flops 4096 | bytes 32768 | tf_op jit(solution)/shard_map/while/body/while/body/eval_jaxpr/psum | solution.py:63
  1082.8 18.3 %posterior.3 = f32[1,1,6,1024,1024]{4,3,2,1,0:T(8,128)} custom-call(s32[6]{0:T(128)S(1)} %get-tuple-element.548, s32[8]{0:T(128)S(1)} %get-tuple-element.549, bf16[6,64,768]{2,1,0:T(8,128)(2,1)} %get-tuple-element.449.refs_0_, bf16[6,64,768]{2,1,0:T(8,128)(2,1)} %collective-permute-done.19.refs_0_.refs_1_, bf16[6,64,768]{2,1,0:T(8,128)(2,1)} %get-tuple-element.552, ...), custom_call_target="tpu_custom_call" | custom-call | bytes 1024 | tf_op jit(solution)/shard_map/posterior/pallas_call | solution.py:470
  (355 shorter events, 277.7 us)
Async XLA Ops:
  7.2 59.1 %all-gather.4.cloned.1.call-start = ((), (), s32[]{:S(2)}) async-start(), calls=%async_computation.10 | async-start | bytes 7077888 | tf_op jit(solution)/shard_map/all_gather | solution.py:536
  24.1 20.8 %collective-permute-start.3 = (bf16[4,2,64,768]{3,2,1,0:T(8,128)(2,1)S(1)}, bf16[4,2,64,768]{3,2,1,0:T(8,128)(2,1)S(1)}, u32[]{:S(2)}, u32[]{:S(2)}) collective-permute-start(bf16[4,2,64,768]{3,2,1,0:T(8,128)(2,1)S(1)} %pad_maximum_fusion.refs_2_.refs_0_), channel_id=1, source_target_pairs={{0,8},{8,16},{16,24},{24,0},{32,40},{40,48},{48,56},{56,32},{64,72... | collective-permute-start | bytes 2359304 | tf_op jit(solution)/shard_map/ppermute | solution.py:500
  25.7 20.3 %collective-permute-start.5 = (bf16[4,2,64,768]{3,2,1,0:T(8,128)(2,1)S(1)}, bf16[4,2,64,768]{3,2,1,0:T(8,128)(2,1)}, u32[]{:S(2)}, u32[]{:S(2)}) collective-permute-start(bf16[4,2,64,768]{3,2,1,0:T(8,128)(2,1)S(1)} %pad_maximum_fusion.refs_2_.refs_0_), channel_id=1, source_target_pairs={{0,24},{8,0},{16,8},{24,16},{32,56},{40,32},{48,40},{56,48},{64,88... | collective-permute-start | bytes 2359304 | tf_op jit(solution)/shard_map/ppermute | solution.py:500
  28.0 22.8 %collective-permute-start.10 = (bf16[4,2,64,768]{3,2,1,0:T(8,128)(2,1)S(1)}, bf16[4,2,64,768]{3,2,1,0:T(8,128)(2,1)}, u32[]{:S(2)}, u32[]{:S(2)}) collective-permute-start(bf16[4,2,64,768]{3,2,1,0:T(8,128)(2,1)S(1)} %pad_maximum_fusion.1.refs_7_.refs_5_), channel_id=1, source_target_pairs={{0,32},{8,40},{16,48},{24,56},{32,64},{40,72},{48,80},{56,88},{64,... | collective-permute-start | bytes 2359304 | tf_op jit(solution)/shard_map/ppermute | solution.py:500
  30.2 23.9 %collective-permute-start.12 = (bf16[4,2,64,768]{3,2,1,0:T(8,128)(2,1)S(1)}, bf16[4,2,64,768]{3,2,1,0:T(8,128)(2,1)}, u32[]{:S(2)}, u32[]{:S(2)}) collective-permute-start(bf16[4,2,64,768]{3,2,1,0:T(8,128)(2,1)S(1)} %pad_maximum_fusion.1.refs_7_.refs_5_), channel_id=1, source_target_pairs={{0,96},{8,104},{16,112},{24,120},{32,0},{40,8},{48,16},{56,24},{64... | collective-permute-start | bytes 2359304 | tf_op jit(solution)/shard_map/ppermute | solution.py:500
  34.7 22.9 %all-to-all-start.3 = ((s32[16,1,128]{2,1,0:T(1,128)}), s32[16,1,128]{2,1,0:T(1,128)S(1)}, u32[]{:S(2)}, u32[]{:S(2)}) async-start(s32[16,1,128]{2,1,0:T(1,128)} %broadcast_in_dim.253), calls=%async_computation.3 | async-start | bytes 16384 | tf_op jit(solution)/shard_map/all_to_all | solution.py:490
  39.4 89.8 %all-gather.6.cloned.1.call-start = ((), (), s32[]{:S(2)}) async-start(), calls=%async_computation.11 | async-start | bytes 6684672 | tf_op jit(solution)/shard_map/all_gather | solution.py:555
  45.7 14.0 %collective-permute-start.4 = (bf16[2,2,64,768]{3,2,1,0:T(8,128)(2,1)}, bf16[2,2,64,768]{3,2,1,0:T(8,128)(2,1)S(1)}, u32[]{:S(2)}, u32[]{:S(2)}) collective-permute-start(bf16[2,2,64,768]{3,2,1,0:T(8,128)(2,1)} %slice.59), channel_id=1, source_target_pairs={{0,8},{8,16},{16,24},{24,0},{32,40},{40,48},{48,56},{56,32},{64,72... | collective-permute-start | bytes 1179656 | tf_op jit(solution)/shard_map/ppermute | solution.py:500
  68.4 137.6 %all-gather.8.cloned.1.call-start = ((), (), s32[]{:S(2)}) async-start(), calls=%async_computation.12 | async-start | bytes 6684672 | tf_op jit(solution)/shard_map/all_gather | solution.py:555
  132.5 46.2 %collective-permute-start.14 = (bf16[6,64,768]{2,1,0:T(8,128)(2,1)S(1)}, bf16[6,64,768]{2,1,0:T(8,128)(2,1)S(1)}, u32[]{:S(2)}, u32[]{:S(2)}) collective-permute-start(bf16[6,64,768]{2,1,0:T(8,128)(2,1)S(1)} %get-tuple-element.220.refs_1_), channel_id=1, source_target_pairs={{0,2},{1,3},{2,4},{3,5},{4,6},{5,7},{6,0},{7,1},{8,10},{9,11},{10,... | collective-permute-start | bytes 1769480 | tf_op jit(solution)/shard_map/ppermute | solution.py:532
  134.2 44.6 %collective-permute-start.15 = (bf16[6,64,768]{2,1,0:T(8,128)(2,1)S(1)}, bf16[6,64,768]{2,1,0:T(8,128)(2,1)S(1)}, u32[]{:S(2)}, u32[]{:S(2)}) collective-permute-start(bf16[6,64,768]{2,1,0:T(8,128)(2,1)S(1)} %get-tuple-element.221.refs_2_), channel_id=1, source_target_pairs={{0,6},{1,7},{2,0},{3,1},{4,2},{5,3},{6,4},{7,5},{8,14},{9,15},{10,... | collective-permute-start | bytes 1769480 | tf_op jit(solution)/shard_map/ppermute | solution.py:532
  135.8 42.9 %collective-permute-start.16 = (bf16[6,64,768]{2,1,0:T(8,128)(2,1)S(1)}, bf16[6,64,768]{2,1,0:T(8,128)(2,1)S(1)}, u32[]{:S(2)}, u32[]{:S(2)}) collective-permute-start(bf16[6,64,768]{2,1,0:T(8,128)(2,1)S(1)} %get-tuple-element.222.refs_3_), channel_id=1, source_target_pairs={{0,3},{1,2},{2,5},{3,4},{4,7},{5,6},{6,1},{7,0},{8,11},{9,10},{10,... | collective-permute-start | bytes 1769480 | tf_op jit(solution)/shard_map/ppermute | solution.py:532
  136.0 42.8 %collective-permute-start.17 = (bf16[6,64,768]{2,1,0:T(8,128)(2,1)S(1)}, bf16[6,64,768]{2,1,0:T(8,128)(2,1)S(1)}, u32[]{:S(2)}, u32[]{:S(2)}) collective-permute-start(bf16[6,64,768]{2,1,0:T(8,128)(2,1)S(1)} %get-tuple-element.223.refs_4_), channel_id=1, source_target_pairs={{0,7},{1,6},{2,1},{3,0},{4,3},{5,2},{6,5},{7,4},{8,15},{9,14},{10,... | collective-permute-start | bytes 1769480 | tf_op jit(solution)/shard_map/ppermute | solution.py:532
  138.9 39.8 %collective-permute-start.18 = (bf16[6,64,768]{2,1,0:T(8,128)(2,1)S(1)}, bf16[6,64,768]{2,1,0:T(8,128)(2,1)S(1)}, u32[]{:S(2)}, u32[]{:S(2)}) collective-permute-start(bf16[6,64,768]{2,1,0:T(8,128)(2,1)S(1)} %get-tuple-element.224.refs_5_), channel_id=1, source_target_pairs={{0,4},{1,5},{2,6},{3,7},{4,0},{5,1},{6,2},{7,3},{8,12},{9,13},{10,... | collective-permute-start | bytes 1769480 | tf_op jit(solution)/shard_map/ppermute | solution.py:532
  192.6 45.8 %collective-permute-start.19 = (bf16[6,64,768]{2,1,0:T(8,128)(2,1)S(1)}, bf16[6,64,768]{2,1,0:T(8,128)(2,1)}, u32[]{:S(2)}, u32[]{:S(2)}) collective-permute-start(bf16[6,64,768]{2,1,0:T(8,128)(2,1)S(1)} %get-tuple-element.225.refs_0_), channel_id=1, source_target_pairs={{0,1},{1,0},{2,3},{3,2},{4,5},{5,4},{6,7},{7,6},{8,9},{9,8},{10,11... | collective-permute-start | bytes 1769480 | tf_op jit(solution)/shard_map/ppermute | solution.py:532
  192.7 45.7 %collective-permute-start.20 = (bf16[6,64,768]{2,1,0:T(8,128)(2,1)S(1)}, bf16[6,64,768]{2,1,0:T(8,128)(2,1)}, u32[]{:S(2)}, u32[]{:S(2)}) collective-permute-start(bf16[6,64,768]{2,1,0:T(8,128)(2,1)S(1)} %get-tuple-element.226.refs_1_), channel_id=1, source_target_pairs={{0,5},{1,4},{2,7},{3,6},{4,1},{5,0},{6,3},{7,2},{8,13},{9,12},{10,... | collective-permute-start | bytes 1769480 | tf_op jit(solution)/shard_map/ppermute | solution.py:532
  208.9 29.5 %collective-permute-start.21 = (bf16[6,64,768]{2,1,0:T(8,128)(2,1)S(1)}, bf16[6,64,768]{2,1,0:T(8,128)(2,1)S(1)}, u32[]{:S(2)}, u32[]{:S(2)}) collective-permute-start(bf16[6,64,768]{2,1,0:T(8,128)(2,1)S(1)} %get-tuple-element.228.refs_3_), channel_id=1, source_target_pairs={{0,2},{1,3},{2,4},{3,5},{4,6},{5,7},{6,0},{7,1},{8,10},{9,11},{10,... | collective-permute-start | bytes 1769480 | tf_op jit(solution)/shard_map/ppermute | solution.py:532
  209.8 28.7 %collective-permute-start.22 = (bf16[6,64,768]{2,1,0:T(8,128)(2,1)S(1)}, bf16[6,64,768]{2,1,0:T(8,128)(2,1)S(1)}, u32[]{:S(2)}, u32[]{:S(2)}) collective-permute-start(bf16[6,64,768]{2,1,0:T(8,128)(2,1)S(1)} %get-tuple-element.229.refs_4_), channel_id=1, source_target_pairs={{0,6},{1,7},{2,0},{3,1},{4,2},{5,3},{6,4},{7,5},{8,14},{9,15},{10,... | collective-permute-start | bytes 1769480 | tf_op jit(solution)/shard_map/ppermute | solution.py:532
  212.2 27.1 %collective-permute-start.23 = (bf16[6,64,768]{2,1,0:T(8,128)(2,1)S(1)}, bf16[6,64,768]{2,1,0:T(8,128)(2,1)}, u32[]{:S(2)}, u32[]{:S(2)}) collective-permute-start(bf16[6,64,768]{2,1,0:T(8,128)(2,1)S(1)} %get-tuple-element.230.refs_5_), channel_id=1, source_target_pairs={{0,4},{1,5},{2,6},{3,7},{4,0},{5,1},{6,2},{7,3},{8,12},{9,13},{10,... | collective-permute-start | bytes 1769480 | tf_op jit(solution)/shard_map/ppermute | solution.py:532
  253.7 32.9 %collective-permute-start.24 = (bf16[6,64,768]{2,1,0:T(8,128)(2,1)S(1)}, bf16[6,64,768]{2,1,0:T(8,128)(2,1)}, u32[]{:S(2)}, u32[]{:S(2)}) collective-permute-start(bf16[6,64,768]{2,1,0:T(8,128)(2,1)S(1)} %get-tuple-element.231.refs_0_), channel_id=1, source_target_pairs={{0,1},{1,0},{2,3},{3,2},{4,5},{5,4},{6,7},{7,6},{8,9},{9,8},{10,11... | collective-permute-start | bytes 1769480 | tf_op jit(solution)/shard_map/ppermute | solution.py:532
  253.8 32.8 %collective-permute-start.25 = (bf16[6,64,768]{2,1,0:T(8,128)(2,1)S(1)}, bf16[6,64,768]{2,1,0:T(8,128)(2,1)}, u32[]{:S(2)}, u32[]{:S(2)}) collective-permute-start(bf16[6,64,768]{2,1,0:T(8,128)(2,1)S(1)} %get-tuple-element.232.refs_1_), channel_id=1, source_target_pairs={{0,3},{1,2},{2,5},{3,4},{4,7},{5,6},{6,1},{7,0},{8,11},{9,10},{10,... | collective-permute-start | bytes 1769480 | tf_op jit(solution)/shard_map/ppermute | solution.py:532
  254.5 32.1 %collective-permute-start.26 = (bf16[6,64,768]{2,1,0:T(8,128)(2,1)S(1)}, bf16[6,64,768]{2,1,0:T(8,128)(2,1)}, u32[]{:S(2)}, u32[]{:S(2)}) collective-permute-start(bf16[6,64,768]{2,1,0:T(8,128)(2,1)S(1)} %get-tuple-element.233.refs_3_), channel_id=1, source_target_pairs={{0,5},{1,4},{2,7},{3,6},{4,1},{5,0},{6,3},{7,2},{8,13},{9,12},{10,... | collective-permute-start | bytes 1769480 | tf_op jit(solution)/shard_map/ppermute | solution.py:532
  256.2 30.4 %collective-permute-start.27 = (bf16[6,64,768]{2,1,0:T(8,128)(2,1)S(1)}, bf16[6,64,768]{2,1,0:T(8,128)(2,1)}, u32[]{:S(2)}, u32[]{:S(2)}) collective-permute-start(bf16[6,64,768]{2,1,0:T(8,128)(2,1)S(1)} %get-tuple-element.234.refs_2_), channel_id=1, source_target_pairs={{0,7},{1,6},{2,1},{3,0},{4,3},{5,2},{6,5},{7,4},{8,15},{9,14},{10,... | collective-permute-start | bytes 1769480 | tf_op jit(solution)/shard_map/ppermute | solution.py:532
  315.7 15.6 %all-to-all-start = ((f32[16,1,1024]{2,1,0:T(1,128)}), f32[16,1,1024]{2,1,0:T(1,128)S(1)}, u32[]{:S(2)}, u32[]{:S(2)}) async-start(f32[16,1,1024]{2,1,0:T(1,128)} %copy.30), calls=%async_computation | async-start | bytes 131072 | tf_op jit(solution)/shard_map/while/body/while/body/eval_jaxpr/all_to_all | solution.py:490
  331.4 31.2 %all-to-all-start.1 = ((f32[16,1,1024]{2,1,0:T(1,128)}), f32[16,1,1024]{2,1,0:T(1,128)S(1)}, u32[]{:S(2)}, u32[]{:S(2)}) async-start(f32[16,1,1024]{2,1,0:T(1,128)} %copy.32), calls=%async_computation.1 | async-start | bytes 131072 | tf_op jit(solution)/shard_map/while/body/while/body/eval_jaxpr/all_to_all | solution.py:490
  387.8 14.6 %all-to-all-start.2 = ((f32[16,1,1024]{2,1,0:T(1,128)}), f32[16,1,1024]{2,1,0:T(1,128)S(1)}, u32[]{:S(2)}, u32[]{:S(2)}) async-start(f32[16,1,1024]{2,1,0:T(1,128)} %copy.34), calls=%async_computation.2 | async-start | bytes 131072 | tf_op jit(solution)/shard_map/while/body/while/body/eval_jaxpr/all_to_all | solution.py:490
  575.0 15.5 %all-to-all-start = ((f32[16,1,1024]{2,1,0:T(1,128)}), f32[16,1,1024]{2,1,0:T(1,128)S(1)}, u32[]{:S(2)}, u32[]{:S(2)}) async-start(f32[16,1,1024]{2,1,0:T(1,128)} %copy.30), calls=%async_computation | async-start | bytes 131072 | tf_op jit(solution)/shard_map/while/body/while/body/eval_jaxpr/all_to_all | solution.py:490
  590.5 31.2 %all-to-all-start.1 = ((f32[16,1,1024]{2,1,0:T(1,128)}), f32[16,1,1024]{2,1,0:T(1,128)S(1)}, u32[]{:S(2)}, u32[]{:S(2)}) async-start(f32[16,1,1024]{2,1,0:T(1,128)} %copy.32), calls=%async_computation.1 | async-start | bytes 131072 | tf_op jit(solution)/shard_map/while/body/while/body/eval_jaxpr/all_to_all | solution.py:490
  646.8 14.6 %all-to-all-start.2 = ((f32[16,1,1024]{2,1,0:T(1,128)}), f32[16,1,1024]{2,1,0:T(1,128)S(1)}, u32[]{:S(2)}, u32[]{:S(2)}) async-start(f32[16,1,1024]{2,1,0:T(1,128)} %copy.34), calls=%async_computation.2 | async-start | bytes 131072 | tf_op jit(solution)/shard_map/while/body/while/body/eval_jaxpr/all_to_all | solution.py:490
  834.1 15.5 %all-to-all-start = ((f32[16,1,1024]{2,1,0:T(1,128)}), f32[16,1,1024]{2,1,0:T(1,128)S(1)}, u32[]{:S(2)}, u32[]{:S(2)}) async-start(f32[16,1,1024]{2,1,0:T(1,128)} %copy.30), calls=%async_computation | async-start | bytes 131072 | tf_op jit(solution)/shard_map/while/body/while/body/eval_jaxpr/all_to_all | solution.py:490
  849.6 31.2 %all-to-all-start.1 = ((f32[16,1,1024]{2,1,0:T(1,128)}), f32[16,1,1024]{2,1,0:T(1,128)S(1)}, u32[]{:S(2)}, u32[]{:S(2)}) async-start(f32[16,1,1024]{2,1,0:T(1,128)} %copy.32), calls=%async_computation.1 | async-start | bytes 131072 | tf_op jit(solution)/shard_map/while/body/while/body/eval_jaxpr/all_to_all | solution.py:490
  905.9 14.6 %all-to-all-start.2 = ((f32[16,1,1024]{2,1,0:T(1,128)}), f32[16,1,1024]{2,1,0:T(1,128)S(1)}, u32[]{:S(2)}, u32[]{:S(2)}) async-start(f32[16,1,1024]{2,1,0:T(1,128)} %copy.34), calls=%async_computation.2 | async-start | bytes 131072 | tf_op jit(solution)/shard_map/while/body/while/body/eval_jaxpr/all_to_all | solution.py:490
  (65 other events, 1852.8 us)
Sparse Core Ops, SparseCore 0:
  9.7 43.5 all-gather.3
  68.5 60.6 all-gather.5
  131.3 60.8 all-gather.7
